TPU v7x, 128 devices: a whole 4x4x4 slice. The times are simulated.
128 devices in a mesh: dom: 2 (over core), cls: 64 (over z, y, x).
Axes of the slice: x: 4, y: 4, z: 4, core: 2. Of those that a mesh axis runs over, the one named last changes fastest.
Arguments:
- images: bfloat16 [12288, 4096], P(('cls', 'dom')), may hold values from -12 to 12, as said below
- precision: bfloat16 [12288], P(('cls', 'dom')), may hold values from 0.00048828125 to 0.048828125
- rotation_offset: int32 [12288], P(('cls', 'dom')), may hold values from 0 to 35
- classes: bfloat16 [200, 4096], P('dom'), may hold values from -4 to 4
- prior_blocks: int32 [128, 40], P('cls', 'dom'), may hold values from 0 to 1, as said below
Outputs:
- new_classes: float32 [200, 4096], P('dom')
- log_evidence: float32 [12288], P(('cls', 'dom'))
Inputs may be any that keep to these rules, and one draw needn't show every extreme that they name: `images`: each image is a rotated class average scaled by a positive factor plus noise. `prior_blocks`: every particle block admits at least one class block.
All inputs are finite; a program needn't handle non-finite values.
Results may differ from a plain program's by a relative error of at most 0.0019.
Values may be sent and summed in bfloat16 or wider, within the bound.
No kernel may reach another device: no remote copies, remote signals or barrier semaphores. Data moves between devices by JAX's collectives and lax.ppermute only.
A program may use at most 64 MiB of HBM per device.

v0:
```python
import math

import jax
import jax.numpy as jnp
from jax import lax
from jax.sharding import PartitionSpec as P

FREQUENCIES = 64
ROTATIONS = 36
CLASS_BLOCK = 5


EXCLUDED = -1e30
PRIOR_WIDTH = 12.0
CLASS_PRIOR = 16.0


def trig_tables():
    angle_steps = (
        jnp.arange(ROTATIONS, dtype=jnp.int32)[:, None]
        * jnp.arange(FREQUENCIES, dtype=jnp.int32)[None, :]
        % ROTATIONS
    )
    angle = angle_steps.astype(jnp.float32) * (2.0 * math.pi / ROTATIONS)
    return (jnp.cos(angle), jnp.sin(angle))


def rotate_bank(class_bank, cos_table, sin_table):
    bank_size, image_width = class_bank.shape
    split_parts = class_bank.astype(jnp.float32).reshape(
        bank_size, 1, 2, FREQUENCIES, image_width // (2 * FREQUENCIES)
    )
    real_part = split_parts[:, :, 0]
    imag_part = split_parts[:, :, 1]
    cosine = cos_table[None, :, :, None]
    sine_term = sin_table[None, :, :, None]
    turned = jnp.stack(
        [real_part * cosine + imag_part * sine_term, imag_part * cosine - real_part * sine_term],
        axis=2,
    )
    return turned.reshape(bank_size * ROTATIONS, image_width).astype(jnp.bfloat16)


def back_rotate(aligned, cos_table, sin_table):
    bank_size = aligned.shape[0]
    image_width = aligned.shape[2]
    split_parts = aligned.reshape(
        bank_size, ROTATIONS, 2, FREQUENCIES, image_width // (2 * FREQUENCIES)
    )
    real_part = split_parts[:, :, 0]
    imag_part = split_parts[:, :, 1]

    def turn_sum(values, trig_table):
        return jnp.einsum("brfg,rf->bfg", values, trig_table, precision=lax.Precision.HIGHEST)

    back_real = turn_sum(real_part, cos_table) - turn_sum(imag_part, sin_table)
    back_imag = turn_sum(imag_part, cos_table) + turn_sum(real_part, sin_table)
    return jnp.stack([back_real, back_imag], axis=1).reshape(bank_size, image_width)


def rotation_prior(offsets):
    offset_steps = (jnp.arange(ROTATIONS, dtype=jnp.int32)[None, :] - offsets[:, None]) % ROTATIONS
    distance = jnp.minimum(offset_steps, ROTATIONS - offset_steps).astype(jnp.float32)
    return -0.5 * (distance / PRIOR_WIDTH) * (distance / PRIOR_WIDTH)


def expand_mask(mask_rows, rows_each):
    widened = jnp.repeat(jnp.repeat(mask_rows, rows_each, axis=0), CLASS_BLOCK, axis=1)
    return widened == 1


def class_scores(particles, precision, offsets, class_bank, allowed, cos_table, sin_table):
    row_count = particles.shape[0]
    blocks = class_bank.shape[0] // CLASS_BLOCK
    turn_prior = rotation_prior(offsets)
    noise_precision = precision.astype(jnp.float32)

    def one_block(block_index):
        members = lax.dynamic_slice_in_dim(class_bank, block_index * CLASS_BLOCK, CLASS_BLOCK, 0)
        turned = rotate_bank(members, cos_table, sin_table)
        correlation = lax.dot_general(
            particles, turned, (((1,), (1,)), ((), ())), preferred_element_type=jnp.float32
        )
        correlation = correlation.reshape(row_count, CLASS_BLOCK, ROTATIONS)
        class_norms = jnp.sum(jnp.square(members.astype(jnp.float32)), axis=1)
        admitted = lax.dynamic_slice_in_dim(allowed, block_index * CLASS_BLOCK, CLASS_BLOCK, 1)
        score = (
            noise_precision[:, None, None] * (correlation - 0.5 * class_norms[None, :, None])
            + turn_prior[:, None, :]
        )
        return jnp.where(admitted[:, :, None], score, EXCLUDED)

    return lax.map(one_block, jnp.arange(blocks, dtype=jnp.int32))


def class_sums(weights, particles, cos_table, sin_table):
    blocks = weights.shape[0]
    row_count = weights.shape[1]

    def one_block(block_weights):
        flat_weights = block_weights.reshape(row_count, CLASS_BLOCK * ROTATIONS)
        aligned = lax.dot_general(
            flat_weights, particles, (((0,), (0,)), ((), ())), preferred_element_type=jnp.float32
        )
        class_total = back_rotate(aligned.reshape(CLASS_BLOCK, ROTATIONS, -1), cos_table, sin_table)
        mass_total = (
            jnp.sum(flat_weights.astype(jnp.float32), axis=0)
            .reshape(CLASS_BLOCK, ROTATIONS)
            .sum(axis=1)
        )
        return (class_total, mass_total)

    class_total, mass_total = lax.map(one_block, weights)
    return (class_total.reshape(blocks * CLASS_BLOCK, -1), mass_total.reshape(-1))


def shards(images, precision, rotation_offset, classes, prior_blocks):
    cos_table, sin_table = trig_tables()
    own_rows = images.shape[0]
    group_images, group_precision = (
        lax.all_gather(images, "dom", axis=0, tiled=True),
        lax.all_gather(precision, "dom", axis=0, tiled=True),
    )
    group_offsets = lax.all_gather(rotation_offset, "dom", axis=0, tiled=True)
    allowed = expand_mask(prior_blocks, own_rows)
    scores = class_scores(
        group_images, group_precision, group_offsets, classes, allowed, cos_table, sin_table
    )
    local_peak = jnp.max(scores, axis=(0, 2, 3))
    peak_score = lax.pmax(local_peak, "dom")
    shifted = jnp.exp(scores - peak_score[None, :, None, None])
    total_mass = lax.psum(jnp.sum(shifted, axis=(0, 2, 3)), "dom")
    weights = (shifted / total_mass[None, :, None, None]).astype(jnp.bfloat16)
    evidence_all = peak_score + jnp.log(total_mass)
    log_evidence = lax.dynamic_slice_in_dim(
        evidence_all, lax.axis_index("dom") * own_rows, own_rows, 0
    )
    class_total, mass_total = class_sums(weights, group_images, cos_table, sin_table)
    class_total, mass_total = lax.psum((class_total, mass_total), "cls")
    new_classes = (class_total + CLASS_PRIOR * classes.astype(jnp.float32)) / (
        mass_total + CLASS_PRIOR
    )[:, None]
    return (new_classes, log_evidence)


def solution(mesh):
    in_specs = (
        P(("cls", "dom"), None),
        P(("cls", "dom")),
        P(("cls", "dom")),
        P("dom", None),
        P("cls", "dom"),
    )
    out_specs = (P("dom", None), P(("cls", "dom")))
    return jax.shard_map(shards, mesh=mesh, in_specs=in_specs, out_specs=out_specs, check_vma=False)
```

profile of v0, /device:TPU:0, one launch (start us, length us, event | category | flops | bytes accessed | tf_op | source)
XLA Modules:
  0.0 789.1 jit_solution(1248809711380433326)
XLA Ops:
  17.1 7.6 all-gather.2.cloned.1.call-done
  24.6 380.9 %while.26 = (s32[]{:T(128)}, f32[20,192,5,36]{1,3,2,0:T(8,128)}, s32[20]{0:T(128)S(1)}, pred[192,100]{0,1:T(8,128)(4,1)S(1)}, f32[192]{0:T(256)S(1)}, /*index=5*...) while((s32[]{:T(128)}, f32[20,192,5,36]{1,3,2,0:T(8,128)}, ...), condition=%wide.region_2.3_spmd.clone.clone, body=%wide.region_0.2_spmd.clone.clone.sunk | while | flops 287132672 | bytes 18140264 | solution.py:93
  33.0 8.0 %convert_element_type.110 = bf16[180,4096]{1,0:T(8,128)(2,1)S(1)} reshape(bf16[5,36,2,64,32]{4,3,2,1,0:T(8,128)(2,1)} %pad_maximum_fusion.4) | data formatting | bytes 2949120 | tf_op jit(solution)/shard_map/while/body/eval_jaxpr/convert_element_type | solution.py:41
  52.1 8.0 %convert_element_type.110 = bf16[180,4096]{1,0:T(8,128)(2,1)S(1)} reshape(bf16[5,36,2,64,32]{4,3,2,1,0:T(8,128)(2,1)} %pad_maximum_fusion.4) | data formatting | bytes 2949120 | tf_op jit(solution)/shard_map/while/body/eval_jaxpr/convert_element_type | solution.py:41
  71.1 8.0 %convert_element_type.110 = bf16[180,4096]{1,0:T(8,128)(2,1)S(1)} reshape(bf16[5,36,2,64,32]{4,3,2,1,0:T(8,128)(2,1)} %pad_maximum_fusion.4) | data formatting | bytes 2949120 | tf_op jit(solution)/shard_map/while/body/eval_jaxpr/convert_element_type | solution.py:41
  90.1 8.0 %convert_element_type.110 = bf16[180,4096]{1,0:T(8,128)(2,1)S(1)} reshape(bf16[5,36,2,64,32]{4,3,2,1,0:T(8,128)(2,1)} %pad_maximum_fusion.4) | data formatting | bytes 2949120 | tf_op jit(solution)/shard_map/while/body/eval_jaxpr/convert_element_type | solution.py:41
  109.2 8.0 %convert_element_type.110 = bf16[180,4096]{1,0:T(8,128)(2,1)S(1)} reshape(bf16[5,36,2,64,32]{4,3,2,1,0:T(8,128)(2,1)} %pad_maximum_fusion.4) | data formatting | bytes 2949120 | tf_op jit(solution)/shard_map/while/body/eval_jaxpr/convert_element_type | solution.py:41
  128.2 8.0 %convert_element_type.110 = bf16[180,4096]{1,0:T(8,128)(2,1)S(1)} reshape(bf16[5,36,2,64,32]{4,3,2,1,0:T(8,128)(2,1)} %pad_maximum_fusion.4) | data formatting | bytes 2949120 | tf_op jit(solution)/shard_map/while/body/eval_jaxpr/convert_element_type | solution.py:41
  147.3 8.0 %convert_element_type.110 = bf16[180,4096]{1,0:T(8,128)(2,1)S(1)} reshape(bf16[5,36,2,64,32]{4,3,2,1,0:T(8,128)(2,1)} %pad_maximum_fusion.4) | data formatting | bytes 2949120 | tf_op jit(solution)/shard_map/while/body/eval_jaxpr/convert_element_type | solution.py:41
  166.3 8.0 %convert_element_type.110 = bf16[180,4096]{1,0:T(8,128)(2,1)S(1)} reshape(bf16[5,36,2,64,32]{4,3,2,1,0:T(8,128)(2,1)} %pad_maximum_fusion.4) | data formatting | bytes 2949120 | tf_op jit(solution)/shard_map/while/body/eval_jaxpr/convert_element_type | solution.py:41
  185.4 8.0 %convert_element_type.110 = bf16[180,4096]{1,0:T(8,128)(2,1)S(1)} reshape(bf16[5,36,2,64,32]{4,3,2,1,0:T(8,128)(2,1)} %pad_maximum_fusion.4) | data formatting | bytes 2949120 | tf_op jit(solution)/shard_map/while/body/eval_jaxpr/convert_element_type | solution.py:41
  204.4 8.0 %convert_element_type.110 = bf16[180,4096]{1,0:T(8,128)(2,1)S(1)} reshape(bf16[5,36,2,64,32]{4,3,2,1,0:T(8,128)(2,1)} %pad_maximum_fusion.4) | data formatting | bytes 2949120 | tf_op jit(solution)/shard_map/while/body/eval_jaxpr/convert_element_type | solution.py:41
  223.5 8.0 %convert_element_type.110 = bf16[180,4096]{1,0:T(8,128)(2,1)S(1)} reshape(bf16[5,36,2,64,32]{4,3,2,1,0:T(8,128)(2,1)} %pad_maximum_fusion.4) | data formatting | bytes 2949120 | tf_op jit(solution)/shard_map/while/body/eval_jaxpr/convert_element_type | solution.py:41
  242.5 8.0 %convert_element_type.110 = bf16[180,4096]{1,0:T(8,128)(2,1)S(1)} reshape(bf16[5,36,2,64,32]{4,3,2,1,0:T(8,128)(2,1)} %pad_maximum_fusion.4) | data formatting | bytes 2949120 | tf_op jit(solution)/shard_map/while/body/eval_jaxpr/convert_element_type | solution.py:41
  261.5 8.0 %convert_element_type.110 = bf16[180,4096]{1,0:T(8,128)(2,1)S(1)} reshape(bf16[5,36,2,64,32]{4,3,2,1,0:T(8,128)(2,1)} %pad_maximum_fusion.4) | data formatting | bytes 2949120 | tf_op jit(solution)/shard_map/while/body/eval_jaxpr/convert_element_type | solution.py:41
  280.6 8.0 %convert_element_type.110 = bf16[180,4096]{1,0:T(8,128)(2,1)S(1)} reshape(bf16[5,36,2,64,32]{4,3,2,1,0:T(8,128)(2,1)} %pad_maximum_fusion.4) | data formatting | bytes 2949120 | tf_op jit(solution)/shard_map/while/body/eval_jaxpr/convert_element_type | solution.py:41
  299.6 8.0 %convert_element_type.110 = bf16[180,4096]{1,0:T(8,128)(2,1)S(1)} reshape(bf16[5,36,2,64,32]{4,3,2,1,0:T(8,128)(2,1)} %pad_maximum_fusion.4) | data formatting | bytes 2949120 | tf_op jit(solution)/shard_map/while/body/eval_jaxpr/convert_element_type | solution.py:41
  318.7 8.0 %convert_element_type.110 = bf16[180,4096]{1,0:T(8,128)(2,1)S(1)} reshape(bf16[5,36,2,64,32]{4,3,2,1,0:T(8,128)(2,1)} %pad_maximum_fusion.4) | data formatting | bytes 2949120 | tf_op jit(solution)/shard_map/while/body/eval_jaxpr/convert_element_type | solution.py:41
  337.7 8.0 %convert_element_type.110 = bf16[180,4096]{1,0:T(8,128)(2,1)S(1)} reshape(bf16[5,36,2,64,32]{4,3,2,1,0:T(8,128)(2,1)} %pad_maximum_fusion.4) | data formatting | bytes 2949120 | tf_op jit(solution)/shard_map/while/body/eval_jaxpr/convert_element_type | solution.py:41
  356.8 8.0 %convert_element_type.110 = bf16[180,4096]{1,0:T(8,128)(2,1)S(1)} reshape(bf16[5,36,2,64,32]{4,3,2,1,0:T(8,128)(2,1)} %pad_maximum_fusion.4) | data formatting | bytes 2949120 | tf_op jit(solution)/shard_map/while/body/eval_jaxpr/convert_element_type | solution.py:41
  375.8 8.0 %convert_element_type.110 = bf16[180,4096]{1,0:T(8,128)(2,1)S(1)} reshape(bf16[5,36,2,64,32]{4,3,2,1,0:T(8,128)(2,1)} %pad_maximum_fusion.4) | data formatting | bytes 2949120 | tf_op jit(solution)/shard_map/while/body/eval_jaxpr/convert_element_type | solution.py:41
  394.9 8.0 %convert_element_type.110 = bf16[180,4096]{1,0:T(8,128)(2,1)S(1)} reshape(bf16[5,36,2,64,32]{4,3,2,1,0:T(8,128)(2,1)} %pad_maximum_fusion.4) | data formatting | bytes 2949120 | tf_op jit(solution)/shard_map/while/body/eval_jaxpr/convert_element_type | solution.py:41
  423.4 172.6 %while.27 = (s32[]{:T(128)}, f32[20,5,4096]{2,1,0:T(8,128)}, f32[20,5]{1,0:T(8,128)S(1)}, bf16[20,192,5,36]{1,3,2,0:T(8,128)(2,1)}, bf16[192,4096]{0,1:T(8,128)(2,1)S(1)}, /*index=5*/s32[]{:T(128)}, s32[]{:T(128)}) while((s32[]{:T(128)}, f32[20,5,4096]{2,1,0:T(8,128)}, f32[20,5]{1,0:T(8,128)S(1)}, ...), condition=%wide.region_9.10_spmd.clone.clone, body=%wide.region_7.9_spmd.clone.clone.sunk | while | flops 286154496 | bytes 9270417 | solution.py:113
  599.8 179.5 %psum.23 = f32[100]{0:T(128)S(1)} all-reduce(f32[100]{0:T(128)S(1)} %reshape.91), channel_id=1, replica_groups=mesh['dom'=2,'cls'=64] {'cls'}, use_global_device_ids=true, to_apply=%region_11.12 | all-reduce | flops 100 | bytes 800 | tf_op jit(solution)/shard_map/psum | solution.py:139
  (677 shorter events, 409.8 us)
Async XLA Ops:
  7.2 17.5 %all-gather.2.cloned.1.call-start = ((), (), s32[]{:S(2)}) async-start(), calls=%async_computation | async-start | bytes 2359296 | tf_op jit(solution)/shard_map/all_gather | solution.py:121
  7.9 771.5 %all-reduce.4.cloned.1.call-start = ((), (), s32[]{:S(2)}) async-start(), calls=%async_computation.1 | async-start | bytes 3407872 | tf_op jit(solution)/shard_map/psum | solution.py:139
  33.0 8.1 %copy-start = (bf16[192,4096]{1,0:T(8,128)(2,1)S(1)}, bf16[192,4096]{1,0:T(8,128)(2,1)}, u32[]{:S(2)}) copy-start(bf16[192,4096]{1,0:T(8,128)(2,1)} %get-tuple-element.382) | copy-start | bytes 4718596 | tf_op jit(solution)/shard_map/while
  52.1 8.1 %copy-start = (bf16[192,4096]{1,0:T(8,128)(2,1)S(1)}, bf16[192,4096]{1,0:T(8,128)(2,1)}, u32[]{:S(2)}) copy-start(bf16[192,4096]{1,0:T(8,128)(2,1)} %get-tuple-element.382) | copy-start | bytes 4718596 | tf_op jit(solution)/shard_map/while
  71.1 8.1 %copy-start = (bf16[192,4096]{1,0:T(8,128)(2,1)S(1)}, bf16[192,4096]{1,0:T(8,128)(2,1)}, u32[]{:S(2)}) copy-start(bf16[192,4096]{1,0:T(8,128)(2,1)} %get-tuple-element.382) | copy-start | bytes 4718596 | tf_op jit(solution)/shard_map/while
  90.1 8.1 %copy-start = (bf16[192,4096]{1,0:T(8,128)(2,1)S(1)}, bf16[192,4096]{1,0:T(8,128)(2,1)}, u32[]{:S(2)}) copy-start(bf16[192,4096]{1,0:T(8,128)(2,1)} %get-tuple-element.382) | copy-start | bytes 4718596 | tf_op jit(solution)/shard_map/while
  109.2 8.1 %copy-start = (bf16[192,4096]{1,0:T(8,128)(2,1)S(1)}, bf16[192,4096]{1,0:T(8,128)(2,1)}, u32[]{:S(2)}) copy-start(bf16[192,4096]{1,0:T(8,128)(2,1)} %get-tuple-element.382) | copy-start | bytes 4718596 | tf_op jit(solution)/shard_map/while
  128.2 8.1 %copy-start = (bf16[192,4096]{1,0:T(8,128)(2,1)S(1)}, bf16[192,4096]{1,0:T(8,128)(2,1)}, u32[]{:S(2)}) copy-start(bf16[192,4096]{1,0:T(8,128)(2,1)} %get-tuple-element.382) | copy-start | bytes 4718596 | tf_op jit(solution)/shard_map/while
  147.3 8.1 %copy-start = (bf16[192,4096]{1,0:T(8,128)(2,1)S(1)}, bf16[192,4096]{1,0:T(8,128)(2,1)}, u32[]{:S(2)}) copy-start(bf16[192,4096]{1,0:T(8,128)(2,1)} %get-tuple-element.382) | copy-start | bytes 4718596 | tf_op jit(solution)/shard_map/while
  166.3 8.1 %copy-start = (bf16[192,4096]{1,0:T(8,128)(2,1)S(1)}, bf16[192,4096]{1,0:T(8,128)(2,1)}, u32[]{:S(2)}) copy-start(bf16[192,4096]{1,0:T(8,128)(2,1)} %get-tuple-element.382) | copy-start | bytes 4718596 | tf_op jit(solution)/shard_map/while
  185.4 8.1 %copy-start = (bf16[192,4096]{1,0:T(8,128)(2,1)S(1)}, bf16[192,4096]{1,0:T(8,128)(2,1)}, u32[]{:S(2)}) copy-start(bf16[192,4096]{1,0:T(8,128)(2,1)} %get-tuple-element.382) | copy-start | bytes 4718596 | tf_op jit(solution)/shard_map/while
  204.4 8.1 %copy-start = (bf16[192,4096]{1,0:T(8,128)(2,1)S(1)}, bf16[192,4096]{1,0:T(8,128)(2,1)}, u32[]{:S(2)}) copy-start(bf16[192,4096]{1,0:T(8,128)(2,1)} %get-tuple-element.382) | copy-start | bytes 4718596 | tf_op jit(solution)/shard_map/while
  223.5 8.1 %copy-start = (bf16[192,4096]{1,0:T(8,128)(2,1)S(1)}, bf16[192,4096]{1,0:T(8,128)(2,1)}, u32[]{:S(2)}) copy-start(bf16[192,4096]{1,0:T(8,128)(2,1)} %get-tuple-element.382) | copy-start | bytes 4718596 | tf_op jit(solution)/shard_map/while
  242.5 8.1 %copy-start = (bf16[192,4096]{1,0:T(8,128)(2,1)S(1)}, bf16[192,4096]{1,0:T(8,128)(2,1)}, u32[]{:S(2)}) copy-start(bf16[192,4096]{1,0:T(8,128)(2,1)} %get-tuple-element.382) | copy-start | bytes 4718596 | tf_op jit(solution)/shard_map/while
  261.5 8.1 %copy-start = (bf16[192,4096]{1,0:T(8,128)(2,1)S(1)}, bf16[192,4096]{1,0:T(8,128)(2,1)}, u32[]{:S(2)}) copy-start(bf16[192,4096]{1,0:T(8,128)(2,1)} %get-tuple-element.382) | copy-start | bytes 4718596 | tf_op jit(solution)/shard_map/while
  280.6 8.1 %copy-start = (bf16[192,4096]{1,0:T(8,128)(2,1)S(1)}, bf16[192,4096]{1,0:T(8,128)(2,1)}, u32[]{:S(2)}) copy-start(bf16[192,4096]{1,0:T(8,128)(2,1)} %get-tuple-element.382) | copy-start | bytes 4718596 | tf_op jit(solution)/shard_map/while
  299.6 8.1 %copy-start = (bf16[192,4096]{1,0:T(8,128)(2,1)S(1)}, bf16[192,4096]{1,0:T(8,128)(2,1)}, u32[]{:S(2)}) copy-start(bf16[192,4096]{1,0:T(8,128)(2,1)} %get-tuple-element.382) | copy-start | bytes 4718596 | tf_op jit(solution)/shard_map/while
  318.7 8.1 %copy-start = (bf16[192,4096]{1,0:T(8,128)(2,1)S(1)}, bf16[192,4096]{1,0:T(8,128)(2,1)}, u32[]{:S(2)}) copy-start(bf16[192,4096]{1,0:T(8,128)(2,1)} %get-tuple-element.382) | copy-start | bytes 4718596 | tf_op jit(solution)/shard_map/while
  337.7 8.1 %copy-start = (bf16[192,4096]{1,0:T(8,128)(2,1)S(1)}, bf16[192,4096]{1,0:T(8,128)(2,1)}, u32[]{:S(2)}) copy-start(bf16[192,4096]{1,0:T(8,128)(2,1)} %get-tuple-element.382) | copy-start | bytes 4718596 | tf_op jit(solution)/shard_map/while
  356.8 8.1 %copy-start = (bf16[192,4096]{1,0:T(8,128)(2,1)S(1)}, bf16[192,4096]{1,0:T(8,128)(2,1)}, u32[]{:S(2)}) copy-start(bf16[192,4096]{1,0:T(8,128)(2,1)} %get-tuple-element.382) | copy-start | bytes 4718596 | tf_op jit(solution)/shard_map/while
  375.8 8.1 %copy-start = (bf16[192,4096]{1,0:T(8,128)(2,1)S(1)}, bf16[192,4096]{1,0:T(8,128)(2,1)}, u32[]{:S(2)}) copy-start(bf16[192,4096]{1,0:T(8,128)(2,1)} %get-tuple-element.382) | copy-start | bytes 4718596 | tf_op jit(solution)/shard_map/while
  394.9 8.1 %copy-start = (bf16[192,4096]{1,0:T(8,128)(2,1)S(1)}, bf16[192,4096]{1,0:T(8,128)(2,1)}, u32[]{:S(2)}) copy-start(bf16[192,4096]{1,0:T(8,128)(2,1)} %get-tuple-element.382) | copy-start | bytes 4718596 | tf_op jit(solution)/shard_map/while
  596.0 183.4 %copy-start.1 = (bf16[100,4096]{1,0:T(8,128)(2,1)S(1)}, bf16[100,4096]{1,0:T(8,128)(2,1)}, u32[]{:S(2)}) copy-start(bf16[100,4096]{1,0:T(8,128)(2,1)} %get-tuple-element.415) | copy-start | bytes 2457604
Sparse Core Ops, SparseCore 0:
  9.6 14.9 all-gather.1
  599.2 132.4 all-reduce.3
where the time goes:
time: 793 us; the launch traced here: 789 us
  other arithmetic  275 us (35%)
  local copies, waits for them, and re-layouts  216 us (27%)
  blocking collectives  189 us (24%)
  matrix products  69.9 us (9%)
  loops' own time  16.6 us (2%)
  between operations  14.8 us (2%)
  waiting for transfers between devices  8.26 us (1%)
    psum x1, blocking collectives, shards(): class_total, mass_total = lax.psum((class_total, mass_total), 'cls')  180 us
    convert_element_type x20, local copies, waits for them, and re-layouts, rotate_bank(): turned.reshape(bank_size * ROTATIONS, image_width).astype(jnp.bfloat16)  161 us
    another operation x20, other arithmetic, rotate_bank(): jnp.stack([real_part * cosine + imag_part * sine_term, imag_part * cosine...  73.1 us
    while x40, other arithmetic  64.6 us
    dot_general x20, matrix products, one_block(): lax.dot_general(flat_weights, particles, (((0,), (0,)), ((), ())), prefer...  57.5 us
    another operation x20, other arithmetic  43.3 us
    reduce_sum x20, other arithmetic, one_block(): class_norms = jnp.sum(jnp.square(members.astype(jnp.float32)), axis=1)  21.3 us
    reduce_sum x20, other arithmetic, one_block(): mass_total = jnp.sum(flat_weights.astype(jnp.float32), axis=0).reshape(CL...  20.6 us
  transfers between devices with their start and end apart: 2, of which 1 were waited for; matrix products, arithmetic and copies ran while one was open for 1% of the time, Pallas kernels for 0%

commit v1 on v0

v1 whole, which is shorter than its diff:
```python
import math

import jax
import jax.numpy as jnp
import numpy as np
from jax import lax
from jax.experimental import pallas as pl
from jax.experimental.pallas import tpu as pltpu
from jax.sharding import PartitionSpec as P

FREQUENCIES = 64
CYCLES = 32
PART = FREQUENCIES * CYCLES
ROTATIONS = 36
CLASS_BLOCK = 5
EXCLUDED = -1e30
PRIOR_WIDTH = 12.0
CLASS_PRIOR = 16.0

RESIDUES = 19
GROUP = 4
LANES = 128
OWN = 96
HALF_CLASSES = 50
HALF_ROWS = 56
ROWS = 2 * HALF_ROWS
COLS = 2 * LANES
CHUNKS = 64
BLOCKS = 32
SUM_SCALE = 0.25

MEMBERS = []
for _j in range(RESIDUES):
    _same = [(m, 1) for m in range(FREQUENCIES) if m % ROTATIONS == _j]
    _back = [(m, -1) for m in range(FREQUENCIES) if m % ROTATIONS == (ROTATIONS - _j) % ROTATIONS and _j not in (0, 18)]
    MEMBERS.append(_same + _back)


def cosv(k):
    return float(np.cos(2.0 * np.pi * (k % 36) / 36.0))


def sinv(k):
    return float(np.sin(2.0 * np.pi * (k % 36) / 36.0))


def lin(values, coefs):
    total = None
    for v, c in zip(values, coefs):
        if abs(c) < 1e-12:
            continue
        if abs(c - 1.0) < 1e-12:
            term = v
        elif abs(c + 1.0) < 1e-12:
            term = -v
        else:
            term = v * c
        total = term if total is None else total + term
    return total


def dft_cos18(x):
    even = [lin([x[j] for j in range(0, 10, 2)], [cosv(2 * j * r) for j in range(0, 10, 2)]) for r in range(5)]
    odd = [lin([x[j] for j in range(1, 10, 2)], [cosv(2 * j * r) for j in range(1, 10, 2)]) for r in range(5)]
    return [even[r] + odd[r] for r in range(5)] + [even[9 - r] - odd[9 - r] for r in range(5, 10)]


def dft_sin18(x):
    even = [lin([x[j] for j in range(2, 9, 2)], [sinv(2 * j * r) for j in range(2, 9, 2)]) for r in range(1, 5)]
    odd = [lin([x[j] for j in range(1, 9, 2)], [sinv(2 * j * r) for j in range(1, 9, 2)]) for r in range(1, 5)]
    return [None] + [odd[r] + even[r] for r in range(4)] + [odd[8 - r] - even[8 - r] for r in range(5, 9)]


def cos_sum(a):
    even = dft_cos18([a[2 * j] for j in range(10)])
    odds = [a[j] for j in range(1, 18, 2)]
    odd = [lin(odds, [cosv(j * r) for j in range(1, 18, 2)]) for r in range(9)]
    return [even[r] + odd[r] for r in range(9)] + [even[9]] + [even[18 - r] - odd[18 - r] for r in range(10, 19)]


def sin_sum(b):
    even = dft_sin18([None] + [b[2 * j] for j in range(1, 9)])
    odds = [b[j] for j in range(1, 18, 2)]
    odd = [None] + [lin(odds, [sinv(j * r) for j in range(1, 18, 2)]) for r in range(1, 10)]
    return [None] + [odd[r] + even[r] for r in range(1, 9)] + [odd[9]] + [odd[18 - r] - even[18 - r] for r in range(10, 18)]


def gather_lanes(ref, part, j):
    rows = ref.shape[0]
    pieces = [ref[:, part * PART + m * CYCLES : part * PART + (m + 1) * CYCLES] for m, _ in MEMBERS[j]]
    if len(pieces) < GROUP:
        pieces.append(jnp.zeros((rows, (GROUP - len(pieces)) * CYCLES), ref.dtype))
    return jnp.concatenate(pieces, axis=1)


def sign_lanes(j, rows, dtype):
    lane = lax.broadcasted_iota(jnp.int32, (rows, LANES), 1)
    same = sum(1 for _, s in MEMBERS[j] if s > 0) * CYCLES
    return jnp.where(lane < same, 1.0, -1.0).astype(dtype)


def score_kernel(own_ref, other_ref, cls_ref, prec_ref, offset_ref, admit_ref, w_ref, xp_ref, stat_ref, ab_ref, sc_ref, base_ref, prior_ref):
    zeros = jnp.zeros((LANES - OWN, RESIDUES * COLS), jnp.bfloat16)
    xp_ref[OWN:LANES] = zeros
    xp_ref[LANES + OWN :] = zeros
    for j in range(RESIDUES):
        for part in range(2):
            at = j * COLS + part * LANES
            xp_ref[0:OWN, at : at + LANES] = gather_lanes(own_ref, part, j)
            xp_ref[LANES : LANES + OWN, at : at + LANES] = gather_lanes(other_ref, part, j)
    for j in range(RESIDUES):
        c_re = gather_lanes(cls_ref, 0, j)
        c_im = gather_lanes(cls_ref, 1, j)
        lhs = jnp.concatenate([c_re, c_im], axis=1)
        if 0 < j < 18:
            sign = sign_lanes(j, ROWS, jnp.bfloat16)
            lhs = jnp.concatenate([lhs, jnp.concatenate([c_im * sign, -(c_re * sign)], axis=1)], axis=0)
        got = lax.dot_general(
            lhs, xp_ref[:, j * COLS : (j + 1) * COLS], (((1,), (1,)), ((), ())), preferred_element_type=jnp.float32
        )
        ab_ref[j] = got[:ROWS]
        if 0 < j < 18:
            ab_ref[18 + j] = got[ROWS:]
    members = cls_ref[...].astype(jnp.float32)
    norm = jnp.sum(members * members, axis=1, keepdims=True)
    base_ref[...] = jnp.where(admit_ref[...] > 0.0, -0.5 * norm * prec_ref[...], EXCLUDED)
    steps = lax.rem(lax.broadcasted_iota(jnp.int32, (40, COLS), 0) - offset_ref[...] + ROTATIONS, ROTATIONS)
    distance = jnp.minimum(steps, ROTATIONS - steps).astype(jnp.float32) * (1.0 / PRIOR_WIDTH)
    prior_ref[...] = -0.5 * distance * distance

    for half in range(2):
        lanes = slice(half * LANES, (half + 1) * LANES)
        prec = jnp.broadcast_to(prec_ref[:, lanes], (8, LANES))

        def scores(i, peak):
            rows = pl.ds(pl.multiple_of(i * 8, 8), 8)
            a = [ab_ref[j, rows, lanes] for j in range(19)]
            b = [None] + [ab_ref[18 + j, rows, lanes] for j in range(1, 18)]
            base = base_ref[rows, lanes]
            c = cos_sum(a)
            s = sin_sum(b)
            for r in range(19):
                turned = [(r, c[r])] if r in (0, 18) else [(r, c[r] + s[r]), (36 - r, c[r] - s[r])]
                for turn, correlation in turned:
                    score = correlation * prec + (base + prior_ref[turn : turn + 1, lanes])
                    sc_ref[turn, rows, lanes] = score
                    peak = jnp.maximum(peak, score)
            return peak

        peak = lax.fori_loop(0, ROWS // 8, scores, jnp.full((8, LANES), EXCLUDED, jnp.float32))
        peak = jnp.broadcast_to(jnp.max(peak, axis=0, keepdims=True), (8, LANES))

        def weights(i, mass):
            rows = pl.ds(pl.multiple_of(i * 8, 8), 8)
            e = [jnp.exp(sc_ref[r, rows, lanes] - peak) for r in range(ROTATIONS)]
            both = [e[0]] + [e[r] + e[36 - r] for r in range(1, 18)] + [e[18]]
            diff = [None] + [e[r] - e[36 - r] for r in range(1, 18)]
            c = cos_sum(both)
            s = sin_sum(diff)
            for j in range(19):
                w_ref[j, rows, lanes] = c[j]
            for j in range(1, 18):
                w_ref[18 + j, rows, lanes] = s[j]
            return mass + c[0]

        mass = lax.fori_loop(0, ROWS // 8, weights, jnp.zeros((8, LANES), jnp.float32))
        stat_ref[0:8, lanes] = peak
        stat_ref[8:16, lanes] = jnp.broadcast_to(jnp.sum(mass, axis=0, keepdims=True), (8, LANES))


def sums_kernel(w_ref, xp_ref, mine_ref, theirs_ref, out_ref, evidence_ref, pc_ref):
    peak_a = mine_ref[0:1, :]
    mass_a = mine_ref[8:9, :]
    peak_b = jnp.concatenate([theirs_ref[0:1, LANES:], theirs_ref[0:1, :LANES]], axis=1)
    mass_b = jnp.concatenate([theirs_ref[8:9, LANES:], theirs_ref[8:9, :LANES]], axis=1)
    peak = jnp.maximum(peak_a, peak_b)
    lift = jnp.exp(peak_a - peak)
    mass = mass_a * lift + mass_b * jnp.exp(peak_b - peak)
    lane = lax.broadcasted_iota(jnp.int32, (1, COLS), 1)
    held = lax.rem(lane, LANES) < OWN
    mass = jnp.where(held, mass, 1.0)
    evidence_ref[...] = jnp.broadcast_to(peak + jnp.log(mass), (8, COLS))
    scale = jnp.where(held, lift / mass, 0.0)

    def split(value):
        scaled = value * scale
        high = scaled.astype(jnp.bfloat16)
        return high, (scaled - high.astype(jnp.float32)).astype(jnp.bfloat16)

    high, low = split(w_ref[0])
    ones = jnp.ones((8, COLS), jnp.bfloat16)
    dims = (((1,), (1,)), ((), ()))
    total = lax.dot_general(ones, high, dims, preferred_element_type=jnp.float32)
    total = total + lax.dot_general(ones, low, dims, preferred_element_type=jnp.float32)
    total = jnp.concatenate([total, jnp.zeros((8, LANES - ROWS), jnp.float32)], axis=1)[0:1]

    for j in range(RESIDUES):
        high, low = split(w_ref[j])
        if 0 < j < 18:
            high_s, low_s = split(w_ref[18 + j])
            high = jnp.concatenate([high, high_s], axis=0)
            low = jnp.concatenate([low, low_s], axis=0)
        images = xp_ref[:, j * COLS : (j + 1) * COLS]
        dims = (((1,), (0,)), ((), ()))
        got = lax.dot_general(high, images, dims, preferred_element_type=jnp.float32)
        got = got + lax.dot_general(low, images, dims, preferred_element_type=jnp.float32)
        re, im = got[:ROWS, :LANES], got[:ROWS, LANES:]
        if 0 < j < 18:
            sign = sign_lanes(j, ROWS, jnp.float32)
            re, im = re - sign * got[ROWS:, LANES:], im + sign * got[ROWS:, :LANES]
        pc_ref[:, j * COLS : j * COLS + LANES] = re * SUM_SCALE
        pc_ref[:, j * COLS + LANES : (j + 1) * COLS] = im * SUM_SCALE

    place = {}
    for j in range(RESIDUES):
        for at, (m, _) in enumerate(MEMBERS[j]):
            place[m] = j * COLS + at * CYCLES
    row = lax.broadcasted_iota(jnp.int32, (HALF_ROWS, LANES), 0)
    for block in range(BLOCKS):
        part, first = divmod(block, BLOCKS // 2)
        starts = [place[first * GROUP + q] + part * LANES for q in range(GROUP)]
        whole = jnp.concatenate([pc_ref[:, at : at + CYCLES] for at in starts], axis=1)
        for half in range(2):
            rows = whole[half * HALF_ROWS : (half + 1) * HALF_ROWS]
            out_ref[half * BLOCKS + block] = jnp.where(row == HALF_CLASSES, total * SUM_SCALE, rows)


def finish_kernel(half_ref, sum_ref, cls_ref, out_ref):
    total = sum_ref[HALF_CLASSES : HALF_CLASSES + 1, :]
    row = lax.broadcasted_iota(jnp.int32, (HALF_ROWS, LANES), 0)
    lane = lax.broadcasted_iota(jnp.int32, (HALF_ROWS, LANES), 1)
    weight = jnp.sum(jnp.where(lane == row + half_ref[0] * HALF_ROWS, total, 0.0), axis=1, keepdims=True)
    whole = sum_ref[...] * (1.0 / SUM_SCALE) + CLASS_PRIOR * cls_ref[...]
    out_ref[...] = whole / (weight * (1.0 / SUM_SCALE) + CLASS_PRIOR)


VMEM = pl.BlockSpec(memory_space=pltpu.VMEM)
SMEM = pl.BlockSpec(memory_space=pltpu.SMEM)


def pad_lanes(own, other):
    pad = jnp.zeros((LANES - OWN,), own.dtype)
    return jnp.concatenate([own, pad, other, pad])[None, :]


def shards(images, precision, rotation_offset, classes, prior_blocks):
    swap = [(0, 1), (1, 0)]
    other_images = lax.ppermute(images, "dom", swap)
    small = jnp.stack([precision, rotation_offset.astype(jnp.bfloat16)])
    other_small = lax.ppermute(small, "dom", swap)
    prec = pad_lanes(precision.astype(jnp.float32), other_small[0].astype(jnp.float32))
    offsets = pad_lanes(rotation_offset, other_small[1].astype(jnp.int32))

    dom = lax.axis_index("dom")
    mask_rows = jnp.stack([prior_blocks[dom], prior_blocks[1 - dom]])
    by_class = jnp.repeat(mask_rows, CLASS_BLOCK, axis=1).reshape(2, 2, HALF_CLASSES)
    by_class = jnp.pad(by_class, ((0, 0), (0, 0), (0, HALF_ROWS - HALF_CLASSES))).reshape(2, ROWS)
    admit = jnp.repeat((by_class == 1).astype(jnp.float32).T, LANES, axis=1)
    halves = jnp.pad(classes.reshape(2, HALF_CLASSES, -1), ((0, 0), (0, HALF_ROWS - HALF_CLASSES), (0, 0)))
    padded = halves.reshape(ROWS, -1)

    weights, by_residue, mine = pl.pallas_call(
        score_kernel,
        out_shape=(
            jax.ShapeDtypeStruct((36, ROWS, COLS), jnp.float32),
            jax.ShapeDtypeStruct((COLS, RESIDUES * COLS), jnp.bfloat16),
            jax.ShapeDtypeStruct((16, COLS), jnp.float32),
        ),
        in_specs=[VMEM] * 6,
        out_specs=(VMEM, VMEM, VMEM),
        scratch_shapes=[
            pltpu.VMEM((36, ROWS, COLS), jnp.float32),
            pltpu.VMEM((36, ROWS, COLS), jnp.float32),
            pltpu.VMEM((ROWS, COLS), jnp.float32),
            pltpu.VMEM((40, COLS), jnp.float32),
        ],
        compiler_params=pltpu.CompilerParams(vmem_limit_bytes=48 * 1024 * 1024),
        name="score",
    )(images, other_images, padded, prec, offsets, admit)

    theirs = lax.ppermute(mine, "dom", swap)

    parts, evidence = pl.pallas_call(
        sums_kernel,
        out_shape=(
            jax.ShapeDtypeStruct((CHUNKS, HALF_ROWS, LANES), jnp.float32),
            jax.ShapeDtypeStruct((8, COLS), jnp.float32),
        ),
        in_specs=[VMEM] * 4,
        out_specs=(VMEM, VMEM),
        scratch_shapes=[pltpu.VMEM((ROWS, RESIDUES * COLS), jnp.float32)],
        compiler_params=pltpu.CompilerParams(vmem_limit_bytes=48 * 1024 * 1024),
        name="sums",
    )(weights, by_residue, mine, theirs)

    got = lax.all_to_all(parts.astype(jnp.float16), "cls", 0, 0, tiled=True)
    total = jnp.sum(got.astype(jnp.float32), axis=0)
    cls = lax.axis_index("cls")
    half, block = cls // BLOCKS, cls % BLOCKS
    chunk = lax.dynamic_slice(halves, (half, 0, block * LANES), (1, HALF_ROWS, LANES))[0].astype(jnp.float32)
    new_chunk = pl.pallas_call(
        finish_kernel,
        out_shape=jax.ShapeDtypeStruct((HALF_ROWS, LANES), jnp.float32),
        in_specs=[SMEM, VMEM, VMEM],
        out_specs=VMEM,
        name="finish",
    )(half.astype(jnp.int32).reshape(1), total, chunk)
    repeated = jnp.broadcast_to(new_chunk.astype(jnp.float16)[None], (CHUNKS, HALF_ROWS, LANES))
    whole = lax.all_to_all(repeated, "cls", 0, 0, tiled=True)
    whole = whole.astype(jnp.float32).reshape(2, BLOCKS, HALF_ROWS, LANES)[:, :, :HALF_CLASSES]
    new_classes = whole.transpose(0, 2, 1, 3).reshape(2 * HALF_CLASSES, -1)
    return new_classes, evidence[0, :OWN]


def solution(mesh):
    in_specs = (
        P(("cls", "dom"), None),
        P(("cls", "dom")),
        P(("cls", "dom")),
        P("dom", None),
        P("cls", "dom"),
    )
    out_specs = (P("dom", None), P(("cls", "dom")))
    return jax.shard_map(shards, mesh=mesh, in_specs=in_specs, out_specs=out_specs, check_vma=False)
```

time: 793 us -> 80.6 us (0.10)
  other arithmetic: 275 us -> 5.47 us
  local copies, waits for them, and re-layouts: 216 us -> 7.23 us
  blocking collectives: 189 us -> 0 us
  matrix products: 69.9 us -> 0 us
  waiting for transfers between devices: 8.26 us -> 34.5 us
  starting transfers between devices: 0.08 us -> 16.8 us
  loops' own time: 16.6 us -> 0 us
  Pallas kernels: 0 us -> 15.3 us
  between operations: 14.8 us -> 0.8 us
    psum x2 -> x0, blocking collectives: 182 us -> none  [the longest x1 180 us: shards(): class_total, mass_total = lax.psum((class_total, mass_total), 'cls')]
    convert_element_type x20 -> x0, local copies, waits for them, and re-layouts: 161 us -> none  [rotate_bank(): turned.reshape(bank_size * ROTATIONS, image_width).astype(jnp.bfloat16)]
    another operation x100 -> x3, other arithmetic: 118 us -> 1.34 us  [the longest x2 1.32 us: shards(): small = jnp.stack([precision, rotation_offset.astype(jnp.bfloat16)])]
    dot_general x40 -> x0, matrix products: 69.9 us -> none  [the longest x20 57.5 us: one_block(): lax.dot_general(flat_weights, particles, (((0,), (0,)), ((), ())), prefer...]
    while x40 -> x0, other arithmetic: 64.6 us -> none
    reduce_sum x41 -> x1, other arithmetic: 44.7 us -> 0.77 us  [shards(): total = jnp.sum(got.astype(jnp.float32), axis=0)]
    all_to_all x0 -> x2, waiting for transfers between devices: none -> 33.3 us  [the longest x1 17.2 us: shards(): got = lax.all_to_all(parts.astype(jnp.float16), 'cls', 0, 0, tiled=True)]
    convert_element_type x22 -> x5, other arithmetic: 22.7 us -> 3.08 us  [the longest x1 1.04 us: shards(): got = lax.all_to_all(parts.astype(jnp.float16), 'cls', 0, 0, tiled=True)]
  transfers between devices with their start and end apart: 2 -> 5, of which waited for: 1 -> 3; matrix products, arithmetic and copies ran while one was open for 1% -> 8% of each run, Pallas kernels for 0% -> 0%
where the time goes in v1:
time: 80.6 us; the launch traced here: 80 us
  waiting for transfers between devices  34.5 us (43%)
  starting transfers between devices  16.8 us (21%)
  Pallas kernels  15.3 us (19%)
  local copies, waits for them, and re-layouts  7.23 us (9%)
  other arithmetic  5.47 us (7%)
    all_to_all x1, waiting for transfers between devices, shards(): got = lax.all_to_all(parts.astype(jnp.float16), 'cls', 0, 0, tiled=True)  17.2 us
    all_to_all x1, waiting for transfers between devices, shards(): whole = lax.all_to_all(repeated, 'cls', 0, 0, tiled=True)  16.2 us
    all_to_all x1, starting transfers between devices, shards(): got = lax.all_to_all(parts.astype(jnp.float16), 'cls', 0, 0, tiled=True)  11.5 us
    pallas_call x1, Pallas kernels, shards(): pl.pallas_call(score_kernel, out_shape=(jax.ShapeDtypeStruct((36, ROWS, C...  9.67 us
    all_to_all x1, starting transfers between devices, shards(): whole = lax.all_to_all(repeated, 'cls', 0, 0, tiled=True)  4.68 us
    pallas_call x1, Pallas kernels, shards(): pl.pallas_call(sums_kernel, out_shape=(jax.ShapeDtypeStruct((CHUNKS, HALF...  4.12 us
    unnamed x7, local copies, waits for them, and re-layouts  2.57 us
  transfers between devices with their start and end apart: 5, of which 3 were waited for; matrix products, arithmetic and copies ran while one was open for 8% of the time, Pallas kernels for 0%

profile of v1, /device:TPU:0, one launch (start us, length us, event | category | flops | bytes accessed | tf_op | source)
XLA Modules:
  0.0 80.0 jit_solution(14525789148926496498)
XLA Ops:
  0.7 0.7 convert_bitcast_fusion.1
  1.4 0.7 pad_maximum_fusion.1
  2.0 0.5 collective-permute-start.1
  2.5 0.7 convert_element_type.39
  3.2 0.8 constant_dynamic-slice_fusion.1
  4.3 0.2 broadcast_in_dim.29
  4.6 1.4 %reshape.39 = bf16[2,50,4096]{2,1,0:T(8,128)(2,1)S(1)} reshape(bf16[100,4096]{1,0:T(8,128)(2,1)} %param.8) | data formatting | bytes 1638400 | tf_op jit(solution)/shard_map/reshape | solution.py:259
  6.3 9.7 %score.1 = (f32[36,112,256]{2,1,0:T(8,128)}, bf16[256,4864]{1,0:T(8,128)(2,1)S(1)}, f32[16,256]{1,0:T(8,128)S(1)}) custom-call(bf16[96,4096]{1,0:T(8,128)(2,1)S(1)} %copy-done, bf16[96,4096]{1,0:T(8,128)(2,1)S(1)} %collective-permute-done.other_ref, bf16[112,4096]{1,0:T(8,128)(2,1)S(1)} %bitcast.30, f32[1,256]{1,0:T(1,128)S(1)} %bitcast.33, ...), custom_call_target="tpu_custom_call" | custom-call | tf_op jit(solution)/shard_map/score/pallas_call | solution.py:262
  16.0 1.2 %collective-permute-done.2.theirs_ref = f32[16,256]{1,0:T(8,128)S(1)} collective-permute-done((f32[16,256]{1,0:T(8,128)S(1)}, f32[16,256]{1,0:T(8,128)S(1)}, u32[]{:S(2)}, u32[]{:S(2)}) %collective-permute-start.2) | collective-permute-done | bytes 16416 | tf_op jit(solution)/shard_map/ppermute | solution.py:281
  17.1 4.1 %sums.1 = (f32[64,56,128]{2,1,0:T(8,128)S(1)}, f32[8,256]{1,0:T(8,128)S(1)}) custom-call(f32[36,112,256]{2,1,0:T(8,128)} %get-tuple-element.7.w_ref, bf16[256,4864]{1,0:T(8,128)(2,1)S(1)} %get-tuple-element.8.xp_ref, f32[16,256]{1,0:T(8,128)S(1)} %get-tuple-element.9.mine_ref, f32[16,256]{1,0:T(8,128)S(1)} %collective-permute-done.2.theirs_ref), custom_call_target="tpu_custom_call" | custom-call | tf_op jit(solution)/shard_map/sums/pallas_call | solution.py:283
  21.2 1.0 %convert_element_type.46 = f16[64,56,128]{2,1,0:T(8,128)(2,1)} convert(f32[64,56,128]{2,1,0:T(8,128)S(1)} %get-tuple-element.10) | non-fusion elementwise | flops 458752 | bytes 2752512 | tf_op jit(solution)/shard_map/convert_element_type | solution.py:296
  22.3 11.5 %all-to-all-start = ((f16[64,56,128]{2,1,0:T(8,128)(2,1)}), f16[64,56,128]{2,1,0:T(8,128)(2,1)S(1)}, u32[]{:S(2)}, u32[]{:S(2)}) async-start(f16[64,56,128]{2,1,0:T(8,128)(2,1)} %convert_element_type.46), calls=%async_computation | async-start | bytes 1835008 | tf_op jit(solution)/shard_map/all_to_all | solution.py:296
  33.8 0.6 bitcast_convert_fusion.cls_ref
  34.5 17.2 %all-to-all-done = f16[64,56,128]{2,1,0:T(8,128)(2,1)S(1)} async-done(((f16[64,56,128]{2,1,0:T(8,128)(2,1)}), f16[64,56,128]{2,1,0:T(8,128)(2,1)S(1)}, u32[]{:S(2)}, u32[]{:S(2)}) %all-to-all-start) | async-done | bytes 917536 | tf_op jit(solution)/shard_map/all_to_all | solution.py:296
  51.6 0.8 convert_reduce_fusion.sum_ref
  52.4 1.5 %finish.1 = f32[56,128]{1,0:T(8,128)} custom-call(s32[1]{0:T(128)} %bitcast.half_ref, f32[56,128]{1,0:T(8,128)} %convert_reduce_fusion.sum_ref, f32[56,128]{1,0:T(8,128)} %bitcast_convert_fusion.cls_ref), custom_call_target="tpu_custom_call" | custom-call | tf_op jit(solution)/shard_map/finish/pallas_call | solution.py:301
  53.9 0.8 convert_element_type.50
  54.6 1.0 %broadcast_in_dim.30 = f16[64,56,128]{2,1,0:T(8,128)(2,1)} broadcast(f16[56,128]{1,0:T(8,128)(2,1)S(1)} %convert_element_type.50), dimensions={1,2} | broadcast | bytes 931840 | tf_op jit(solution)/shard_map/broadcast_in_dim | solution.py:308
  55.7 4.7 %all-to-all-start.1 = ((f16[64,56,128]{2,1,0:T(8,128)(2,1)}), f16[64,56,128]{2,1,0:T(8,128)(2,1)S(1)}, u32[]{:S(2)}, u32[]{:S(2)}) async-start(f16[64,56,128]{2,1,0:T(8,128)(2,1)} %broadcast_in_dim.30), calls=%async_computation.1 | async-start | bytes 1835008 | tf_op jit(solution)/shard_map/all_to_all | solution.py:309
  60.4 0.5 slice_bitcast_fusion
  60.9 16.2 %all-to-all-done.1 = f16[64,56,128]{2,1,0:T(8,128)(2,1)S(1)} async-done(((f16[64,56,128]{2,1,0:T(8,128)(2,1)}), f16[64,56,128]{2,1,0:T(8,128)(2,1)S(1)}, u32[]{:S(2)}, u32[]{:S(2)}) %all-to-all-start.1) | async-done | bytes 917536 | tf_op jit(solution)/shard_map/all_to_all | solution.py:309
  77.2 0.3 copy.10
  77.5 0.1 pad.22
  77.6 2.4 %copy.12 = f32[13,8,32,128]{3,1,2,0:T(8,128)} copy(f32[13,8,32,128]{3,2,1,0:T(8,128)S(1)} %bitcast.34) | data formatting | bytes 3407872
  (22 shorter events, 0.9 us)
Async XLA Ops:
  0.6 5.6 %collective-permute-start = (bf16[96,4096]{1,0:T(8,128)(2,1)}, bf16[96,4096]{1,0:T(8,128)(2,1)S(1)}, u32[]{:S(2)}, u32[]{:S(2)}) collective-permute-start(bf16[96,4096]{1,0:T(8,128)(2,1)} %own_ref.1), channel_id=1, source_target_pairs={{0,64},{64,0},{1,65},{65,1},{2,66},{66,2},{3,67},{67,3},{4,68},{68... | collective-permute-start | bytes 2359304 | tf_op jit(solution)/shard_map/ppermute | solution.py:248
  2.0 4.0 %collective-permute-start.1 = (bf16[2,96]{1,0:T(2,128)(2,1)S(1)}, bf16[2,96]{1,0:T(2,128)(2,1)S(1)}, u32[]{:S(2)}, u32[]{:S(2)}) collective-permute-start(bf16[2,96]{1,0:T(2,128)(2,1)S(1)} %pad_maximum_fusion.1), channel_id=1, source_target_pairs={{0,64},{64,0},{1,65},{65,1},{2,66},{66,2},{3,67},{67,3},{4,68},{68... | collective-permute-start | bytes 1160 | tf_op jit(solution)/shard_map/ppermute | solution.py:250
  4.5 1.6 %copy-start.1 = (s32[96]{0:T(128)S(1)}, s32[96]{0:T(128)}, u32[]{:S(2)}) copy-start(s32[96]{0:T(128)} %param.7) | copy-start | bytes 1156
  4.5 1.7 %copy-start = (bf16[96,4096]{1,0:T(8,128)(2,1)S(1)}, bf16[96,4096]{1,0:T(8,128)(2,1)}, u32[]{:S(2)}) copy-start(bf16[96,4096]{1,0:T(8,128)(2,1)} %own_ref.1) | copy-start | bytes 2359300
  15.9 1.2 %collective-permute-start.2 = (f32[16,256]{1,0:T(8,128)S(1)}, f32[16,256]{1,0:T(8,128)S(1)}, u32[]{:S(2)}, u32[]{:S(2)}) collective-permute-start(f32[16,256]{1,0:T(8,128)S(1)} %get-tuple-element.9.mine_ref), channel_id=1, source_target_pairs={{0,64},{64,0},{1,65},{65,1},{2,66},{66,2},{3,67},{67,3},{4,68},{68... | collective-permute-start | bytes 49160 | tf_op jit(solution)/shard_map/ppermute | solution.py:281
  22.3 29.3 %all-to-all-start = ((f16[64,56,128]{2,1,0:T(8,128)(2,1)}), f16[64,56,128]{2,1,0:T(8,128)(2,1)S(1)}, u32[]{:S(2)}, u32[]{:S(2)}) async-start(f16[64,56,128]{2,1,0:T(8,128)(2,1)} %convert_element_type.46), calls=%async_computation | async-start | bytes 1835008 | tf_op jit(solution)/shard_map/all_to_all | solution.py:296
  55.7 21.4 %all-to-all-start.1 = ((f16[64,56,128]{2,1,0:T(8,128)(2,1)}), f16[64,56,128]{2,1,0:T(8,128)(2,1)S(1)}, u32[]{:S(2)}, u32[]{:S(2)}) async-start(f16[64,56,128]{2,1,0:T(8,128)(2,1)} %broadcast_in_dim.30), calls=%async_computation.1 | async-start | bytes 1835008 | tf_op jit(solution)/shard_map/all_to_all | solution.py:309

commit v2 on v1

v2 whole, which is shorter than its diff:
```python
import math

import jax
import jax.numpy as jnp
import numpy as np
from jax import lax
from jax.experimental import pallas as pl
from jax.experimental.pallas import tpu as pltpu
from jax.sharding import PartitionSpec as P

FREQUENCIES = 64
CYCLES = 32
PART = FREQUENCIES * CYCLES
ROTATIONS = 36
CLASS_BLOCK = 5
EXCLUDED = -1e30
PRIOR_WIDTH = 12.0
CLASS_PRIOR = 16.0

RESIDUES = 19
GROUP = 4
LANES = 128
OWN = 96
CLASSES = 100
ROWS = 104
SPLIT = 48
HALF_ROWS = 56
TOTAL_ROW = 52
COLS = 2 * LANES
CHUNKS = 64
BLOCKS = 32
SUM_SCALE = 0.25

MEMBERS = []
for _j in range(RESIDUES):
    _same = [(m, 1) for m in range(FREQUENCIES) if m % ROTATIONS == _j]
    _back = [(m, -1) for m in range(FREQUENCIES) if m % ROTATIONS == (ROTATIONS - _j) % ROTATIONS and _j not in (0, 18)]
    MEMBERS.append(_same + _back)


def cosv(k):
    return float(np.cos(2.0 * np.pi * (k % 36) / 36.0))


def sinv(k):
    return float(np.sin(2.0 * np.pi * (k % 36) / 36.0))


def lin(values, coefs):
    total = None
    for v, c in zip(values, coefs):
        if abs(c) < 1e-12:
            continue
        if abs(c - 1.0) < 1e-12:
            term = v
        elif abs(c + 1.0) < 1e-12:
            term = -v
        else:
            term = v * c
        total = term if total is None else total + term
    return total


def dft_cos18(x):
    even = [lin([x[j] for j in range(0, 10, 2)], [cosv(2 * j * r) for j in range(0, 10, 2)]) for r in range(5)]
    odd = [lin([x[j] for j in range(1, 10, 2)], [cosv(2 * j * r) for j in range(1, 10, 2)]) for r in range(5)]
    return [even[r] + odd[r] for r in range(5)] + [even[9 - r] - odd[9 - r] for r in range(5, 10)]


def dft_sin18(x):
    even = [lin([x[j] for j in range(2, 9, 2)], [sinv(2 * j * r) for j in range(2, 9, 2)]) for r in range(1, 5)]
    odd = [lin([x[j] for j in range(1, 9, 2)], [sinv(2 * j * r) for j in range(1, 9, 2)]) for r in range(1, 5)]
    return [None] + [odd[r] + even[r] for r in range(4)] + [odd[8 - r] - even[8 - r] for r in range(5, 9)]


def cos_sum(a):
    even = dft_cos18([a[2 * j] for j in range(10)])
    odds = [a[j] for j in range(1, 18, 2)]
    odd = [lin(odds, [cosv(j * r) for j in range(1, 18, 2)]) for r in range(9)]
    return [even[r] + odd[r] for r in range(9)] + [even[9]] + [even[18 - r] - odd[18 - r] for r in range(10, 19)]


def sin_sum(b):
    even = dft_sin18([None] + [b[2 * j] for j in range(1, 9)])
    odds = [b[j] for j in range(1, 18, 2)]
    odd = [None] + [lin(odds, [sinv(j * r) for j in range(1, 18, 2)]) for r in range(1, 10)]
    return [None] + [odd[r] + even[r] for r in range(1, 9)] + [odd[9]] + [odd[18 - r] - even[18 - r] for r in range(10, 18)]


def gather_lanes(ref, part, j):
    rows = ref.shape[0]
    pieces = [ref[:, part * PART + m * CYCLES : part * PART + (m + 1) * CYCLES] for m, _ in MEMBERS[j]]
    if len(pieces) < GROUP:
        pieces.append(jnp.zeros((rows, (GROUP - len(pieces)) * CYCLES), ref.dtype))
    return jnp.concatenate(pieces, axis=1)


def sign_lanes(j, rows):
    lane = lax.broadcasted_iota(jnp.int32, (rows, LANES), 1)
    same = sum(1 for _, s in MEMBERS[j] if s > 0) * CYCLES
    return jnp.where(lane < same, 1.0, -1.0)


def particle_row(values):
    return jnp.concatenate([values, jnp.zeros((1, LANES - OWN), values.dtype)], axis=1)


def arrange_classes(cls_ref, cp_ref, norm_ref):
    zeros = jnp.zeros((ROWS - CLASSES, COLS), jnp.float32)
    norm = jnp.zeros((CLASSES, LANES), jnp.float32)
    for j in range(RESIDUES):
        c_re = gather_lanes(cls_ref, 0, j).astype(jnp.float32)
        c_im = gather_lanes(cls_ref, 1, j).astype(jnp.float32)
        norm = norm + c_re * c_re + c_im * c_im
        cosine = jnp.concatenate([jnp.concatenate([c_re, c_im], axis=1), zeros], axis=0)
        if 0 < j < 18:
            sign = sign_lanes(j, CLASSES)
            sine = jnp.concatenate([jnp.concatenate([c_im * sign, -(c_re * sign)], axis=1), zeros], axis=0)
        else:
            sine = jnp.zeros((ROWS, COLS), jnp.float32)
        cp_ref[j] = jnp.concatenate([cosine, sine], axis=0).astype(jnp.bfloat16)
    norm = jnp.broadcast_to(jnp.sum(norm, axis=1, keepdims=True), (CLASSES, LANES))
    norm_ref[...] = jnp.concatenate([norm, jnp.zeros((ROWS - CLASSES, LANES), jnp.float32)], axis=0)


def score_block(blocks_ref, block_row, image_ref, precision, offset, cp_ref, norm_ref, w_ref, xp_ref, stat_ref, ab_ref, sc_ref, base_ref, prior_ref):
    row = lax.broadcasted_iota(jnp.int32, (ROWS, LANES), 0)
    admit = jnp.zeros((ROWS, LANES), jnp.int32)
    for block in range(CLASSES // CLASS_BLOCK):
        inside = (row >= block * CLASS_BLOCK) & (row < (block + 1) * CLASS_BLOCK)
        admit = jnp.where(inside, blocks_ref[block_row, block], admit)
    base_ref[...] = jnp.where(admit == 1, -0.5 * norm_ref[...] * precision, EXCLUDED)
    steps = lax.rem(lax.broadcasted_iota(jnp.int32, (40, LANES), 0) - offset + ROTATIONS, ROTATIONS)
    distance = jnp.minimum(steps, ROTATIONS - steps).astype(jnp.float32) * (1.0 / PRIOR_WIDTH)
    prior_ref[...] = -0.5 * distance * distance
    xp_ref[OWN:LANES] = jnp.zeros((LANES - OWN, RESIDUES * COLS), jnp.bfloat16)
    for j in range(RESIDUES):
        for part in range(2):
            at = j * COLS + part * LANES
            xp_ref[0:OWN, at : at + LANES] = gather_lanes(image_ref, part, j)
        got = lax.dot_general(
            cp_ref[j], xp_ref[:, j * COLS : (j + 1) * COLS], (((1,), (1,)), ((), ())), preferred_element_type=jnp.float32
        )
        ab_ref[j] = got[:ROWS]
        if 0 < j < 18:
            ab_ref[18 + j] = got[ROWS:]

    prec = jnp.broadcast_to(precision, (8, LANES))

    def scores(i, peak):
        rows = pl.ds(pl.multiple_of(i * 8, 8), 8)
        a = [ab_ref[j, rows] for j in range(19)]
        b = [None] + [ab_ref[18 + j, rows] for j in range(1, 18)]
        base = base_ref[rows]
        c = cos_sum(a)
        s = sin_sum(b)
        for r in range(19):
            turned = [(r, c[r])] if r in (0, 18) else [(r, c[r] + s[r]), (36 - r, c[r] - s[r])]
            for turn, correlation in turned:
                score = correlation * prec + (base + prior_ref[turn : turn + 1])
                sc_ref[turn, rows] = score
                peak = jnp.maximum(peak, score)
        return peak

    peak = lax.fori_loop(0, ROWS // 8, scores, jnp.full((8, LANES), EXCLUDED, jnp.float32), unroll=True)
    peak = jnp.broadcast_to(jnp.max(peak, axis=0, keepdims=True), (8, LANES))

    def weights(i, mass):
        rows = pl.ds(pl.multiple_of(i * 8, 8), 8)
        e = [jnp.exp(sc_ref[r, rows] - peak) for r in range(ROTATIONS)]
        both = [e[0]] + [e[r] + e[36 - r] for r in range(1, 18)] + [e[18]]
        diff = [None] + [e[r] - e[36 - r] for r in range(1, 18)]
        c = cos_sum(both)
        s = sin_sum(diff)
        for j in range(19):
            w_ref[j, rows] = c[j]
        for j in range(1, 18):
            w_ref[18 + j, rows] = s[j]
        return mass + c[0]

    mass = lax.fori_loop(0, ROWS // 8, weights, jnp.zeros((8, LANES), jnp.float32), unroll=True)
    stat_ref[0:8] = peak
    stat_ref[8:16] = jnp.broadcast_to(jnp.sum(mass, axis=0, keepdims=True), (8, LANES))


def class_kernel(cls_ref, cp_ref, norm_ref):
    arrange_classes(cls_ref, cp_ref, norm_ref)


def own_kernel(blocks_ref, image_ref, prec_ref, offset_ref, cp_ref, norm_ref, w_ref, xp_ref, stat_ref, *scratch):
    precision = particle_row(prec_ref[...].astype(jnp.float32))
    offset = particle_row(offset_ref[...])
    score_block(blocks_ref, lax.axis_index("dom"), image_ref, precision, offset, cp_ref, norm_ref, w_ref, xp_ref, stat_ref, *scratch)


def other_kernel(blocks_ref, image_ref, prec_ref, offset_ref, cp_ref, norm_ref, stat_a, w_ref, xp_ref, stats_ref, *scratch):
    precision = particle_row(prec_ref[...].astype(jnp.float32))
    offset = particle_row(offset_ref[...])
    score_block(blocks_ref, 1 - lax.axis_index("dom"), image_ref, precision, offset, cp_ref, norm_ref, w_ref, xp_ref, stats_ref.at[1], *scratch)
    stats_ref[0] = stat_a[...]


def sums_kernel(w_a, w_b, xp_a, xp_b, mine, theirs, out_ref, evidence_ref, pc_ref):
    held = lax.broadcasted_iota(jnp.int32, (1, LANES), 1) < OWN

    def settle(mine, theirs):
        peak = jnp.maximum(mine[0:1], theirs[0:1])
        lift = jnp.exp(mine[0:1] - peak)
        mass = mine[8:9] * lift + theirs[8:9] * jnp.exp(theirs[0:1] - peak)
        mass = jnp.where(held, mass, 1.0)
        return jnp.where(held, lift / mass, 0.0), peak + jnp.log(mass)

    scale_a, evidence = settle(mine[0], theirs[1])
    scale_b, _ = settle(mine[1], theirs[0])
    evidence_ref[...] = jnp.broadcast_to(evidence, (8, LANES))

    def weights_of(i):
        return jnp.concatenate([w_a[i] * scale_a, w_b[i] * scale_b], axis=1)

    totals = weights_of(0)
    totals = jnp.concatenate([totals, jnp.zeros((LANES - ROWS, COLS), jnp.float32)], axis=0)
    high = totals.astype(jnp.bfloat16)
    low = (totals - high.astype(jnp.float32)).astype(jnp.bfloat16)
    ones = jnp.ones((16, COLS), jnp.bfloat16)
    dims = (((1,), (1,)), ((), ()))
    total = lax.dot_general(ones, high, dims, preferred_element_type=jnp.float32)
    total = total + lax.dot_general(ones, low, dims, preferred_element_type=jnp.float32)
    total = total[0:1]

    for j in range(RESIDUES):
        pair = 0 < j < 18
        weight = weights_of(j)
        if pair:
            weight = jnp.concatenate([weight, weights_of(18 + j)], axis=0)
        else:
            weight = jnp.concatenate([weight, jnp.zeros((8, COLS), jnp.float32)], axis=0)
        high = weight.astype(jnp.bfloat16)
        low = (weight - high.astype(jnp.float32)).astype(jnp.bfloat16)
        lanes = slice(j * COLS, (j + 1) * COLS)
        images = jnp.concatenate([xp_a[:, lanes], xp_b[:, lanes]], axis=0)
        dims = (((1,), (0,)), ((), ()))
        got = lax.dot_general(high, images, dims, preferred_element_type=jnp.float32)
        got = got + lax.dot_general(low, images, dims, preferred_element_type=jnp.float32)
        re, im = got[:ROWS, :LANES], got[:ROWS, LANES:]
        if pair:
            sign = sign_lanes(j, ROWS)
            re, im = re - sign * got[ROWS:, LANES:], im + sign * got[ROWS:, :LANES]
        pc_ref[:, j * COLS : j * COLS + LANES] = re * SUM_SCALE
        pc_ref[:, j * COLS + LANES : (j + 1) * COLS] = im * SUM_SCALE

    place = {}
    for j in range(RESIDUES):
        for at, (m, _) in enumerate(MEMBERS[j]):
            place[m] = j * COLS + at * CYCLES
    row = lax.broadcasted_iota(jnp.int32, (HALF_ROWS, LANES), 0)
    for block in range(BLOCKS):
        part, first = divmod(block, BLOCKS // 2)
        starts = [place[first * GROUP + q] + part * LANES for q in range(GROUP)]
        whole = jnp.concatenate([pc_ref[:, at : at + CYCLES] for at in starts], axis=1)
        for half in range(2):
            rows = whole[half * SPLIT : half * SPLIT + HALF_ROWS]
            out_ref[half * BLOCKS + block] = jnp.where(row == TOTAL_ROW, total * SUM_SCALE, rows)


FINISH_STEPS = 4
STEP_BLOCKS = BLOCKS // FINISH_STEPS


def finish_kernel(sum_ref, cls_hbm, out_hbm, cls_ref, out_ref, cls_sem, out_sems):
    fetch = pltpu.make_async_copy(cls_hbm, cls_ref, cls_sem)
    fetch.start()
    row = lax.broadcasted_iota(jnp.int32, (HALF_ROWS, LANES), 0)
    lane = lax.broadcasted_iota(jnp.int32, (HALF_ROWS, LANES), 1)
    share = []
    for half in range(2):
        total = sum_ref[half, 0, TOTAL_ROW : TOTAL_ROW + 1, :]
        weight = jnp.sum(jnp.where(lane == row + half * SPLIT, total, 0.0), axis=1, keepdims=True)
        share.append(1.0 / (weight * (1.0 / SUM_SCALE) + CLASS_PRIOR))
    fetch.wait()
    copies = []
    for step in range(FINISH_STEPS):
        for block in range(step * STEP_BLOCKS, (step + 1) * STEP_BLOCKS):
            lanes = slice(block * LANES, (block + 1) * LANES)
            old = cls_ref[:, lanes].astype(jnp.float32)
            for half in range(2):
                count = SPLIT if half == 0 else CLASSES - SPLIT
                rows = slice(half * SPLIT, half * SPLIT + count)
                new = sum_ref[half, block, 0:count] * (1.0 / SUM_SCALE) + CLASS_PRIOR * old[rows]
                out_ref[rows, lanes] = new * share[half][:count]
        lanes = slice(step * STEP_BLOCKS * LANES, (step + 1) * STEP_BLOCKS * LANES)
        copy = pltpu.make_async_copy(out_ref.at[:, lanes], out_hbm.at[:, lanes], out_sems.at[step])
        copy.start()
        copies.append(copy)
    for copy in copies:
        copy.wait()


VMEM = pl.BlockSpec(memory_space=pltpu.VMEM)
SMEM = pl.BlockSpec(memory_space=pltpu.SMEM)


ANY = pl.BlockSpec(memory_space=pl.ANY)
MIB = 1024 * 1024


def shards(images, precision, rotation_offset, classes, prior_blocks):
    swap = [(0, 1), (1, 0)]
    other_images = lax.ppermute(images, "dom", swap)
    other_precision = lax.ppermute(precision, "dom", swap)
    other_offset = lax.ppermute(rotation_offset, "dom", swap)

    block_out = (
        jax.ShapeDtypeStruct((36, ROWS, LANES), jnp.float32),
        jax.ShapeDtypeStruct((LANES, RESIDUES * COLS), jnp.bfloat16),
    )
    class_out = (
        jax.ShapeDtypeStruct((RESIDUES, 2 * ROWS, COLS), jnp.bfloat16),
        jax.ShapeDtypeStruct((ROWS, LANES), jnp.float32),
    )
    block_scratch = [
        pltpu.VMEM((36, ROWS, LANES), jnp.float32),
        pltpu.VMEM((36, ROWS, LANES), jnp.float32),
        pltpu.VMEM((ROWS, LANES), jnp.float32),
        pltpu.VMEM((40, LANES), jnp.float32),
    ]
    cost = pl.CostEstimate(flops=4 * 10**9, bytes_accessed=8 * MIB, transcendentals=36 * 104 * 128)

    cp, norm = pl.pallas_call(
        class_kernel,
        out_shape=class_out,
        in_specs=[VMEM],
        out_specs=(VMEM,) * 2,
        compiler_params=pltpu.CompilerParams(vmem_limit_bytes=12 * MIB),
        cost_estimate=cost,
        name="classes",
    )(classes)

    w_a, xp_a, stat_a = pl.pallas_call(
        own_kernel,
        out_shape=block_out + (jax.ShapeDtypeStruct((16, LANES), jnp.float32),),
        in_specs=[SMEM] + [VMEM] * 5,
        out_specs=(VMEM,) * 3,
        scratch_shapes=block_scratch,
        compiler_params=pltpu.CompilerParams(vmem_limit_bytes=20 * MIB),
        cost_estimate=cost,
        name="own_scores",
    )(prior_blocks, images, precision.reshape(1, OWN), rotation_offset.reshape(1, OWN), cp, norm)

    w_b, xp_b, mine = pl.pallas_call(
        other_kernel,
        out_shape=block_out + (jax.ShapeDtypeStruct((2, 16, LANES), jnp.float32),),
        in_specs=[SMEM] + [VMEM] * 6,
        out_specs=(VMEM,) * 3,
        scratch_shapes=block_scratch,
        compiler_params=pltpu.CompilerParams(vmem_limit_bytes=20 * MIB),
        cost_estimate=cost,
        name="other_scores",
    )(prior_blocks, other_images, other_precision.reshape(1, OWN), other_offset.reshape(1, OWN), cp, norm, stat_a)
    theirs = lax.ppermute(mine, "dom", swap)

    parts, evidence = pl.pallas_call(
        sums_kernel,
        out_shape=(
            jax.ShapeDtypeStruct((CHUNKS, HALF_ROWS, LANES), jnp.float32),
            jax.ShapeDtypeStruct((8, LANES), jnp.float32),
        ),
        in_specs=[VMEM] * 6,
        out_specs=(VMEM, VMEM),
        scratch_shapes=[pltpu.VMEM((ROWS, RESIDUES * COLS), jnp.float32)],
        compiler_params=pltpu.CompilerParams(vmem_limit_bytes=20 * MIB),
        name="sums",
    )(w_a, w_b, xp_a, xp_b, mine, theirs)

    got = lax.all_to_all(parts.astype(jnp.float16), "cls", 0, 0, tiled=True)
    total = jnp.sum(got.astype(jnp.float32), axis=0).astype(jnp.float16)
    repeated = jnp.broadcast_to(total[None], (CHUNKS, HALF_ROWS, LANES))
    whole = lax.all_to_all(repeated, "cls", 0, 0, tiled=True)
    new_classes = pl.pallas_call(
        finish_kernel,
        out_shape=jax.ShapeDtypeStruct((CLASSES, BLOCKS * LANES), jnp.float32),
        in_specs=[VMEM, ANY],
        out_specs=ANY,
        scratch_shapes=[
            pltpu.VMEM(classes.shape, jnp.bfloat16),
            pltpu.VMEM((CLASSES, BLOCKS * LANES), jnp.float32),
            pltpu.SemaphoreType.DMA,
            pltpu.SemaphoreType.DMA((FINISH_STEPS,)),
        ],
        compiler_params=pltpu.CompilerParams(vmem_limit_bytes=12 * MIB),
        name="finish",
    )(whole.astype(jnp.float32).reshape(2, BLOCKS, HALF_ROWS, LANES), classes)
    return new_classes, evidence[0, :OWN]


def solution(mesh):
    in_specs = (
        P(("cls", "dom"), None),
        P(("cls", "dom")),
        P(("cls", "dom")),
        P("dom", None),
        P("cls", "dom"),
    )
    out_specs = (P("dom", None), P(("cls", "dom")))
    return jax.shard_map(shards, mesh=mesh, in_specs=in_specs, out_specs=out_specs, check_vma=False)
```

time: 80.6 us -> 67.8 us (0.84)
  blocking collectives: 0 us -> 29.3 us
  waiting for transfers between devices: 34.5 us -> 17.1 us
  starting transfers between devices: 16.8 us -> 5.85 us
  other arithmetic: 5.47 us -> 0.41 us
  local copies, waits for them, and re-layouts: 7.23 us -> 3.02 us
  Pallas kernels: 15.3 us -> 11.1 us
    all_to_all x0 -> x1, blocking collectives: none -> 29.3 us  [shards(): got = lax.all_to_all(parts.astype(jnp.float16), 'cls', 0, 0, tiled=True)]
    all_to_all x1 -> x0, waiting for transfers between devices: 17.2 us -> none  [shards(): got = lax.all_to_all(parts.astype(jnp.float16), 'cls', 0, 0, tiled=True)]
    all_to_all x1 -> x0, starting transfers between devices: 11.5 us -> none  [shards(): got = lax.all_to_all(parts.astype(jnp.float16), 'cls', 0, 0, tiled=True)]
    pallas_call x1, Pallas kernels: 4.12 us -> 1.82 us  [shards(): pl.pallas_call(sums_kernel, out_shape=(jax.ShapeDtypeStruct((CHUNKS, HALF...]
    convert_element_type x4 -> x1, other arithmetic: 2.04 us -> 0.01 us  [shards(): total = jnp.sum(got.astype(jnp.float32), axis=0).astype(jnp.float16)]
    pallas_call x2 -> x4, Pallas kernels: 11.1 us -> 9.27 us  [the longest x1 3.45 us: shards(): pl.pallas_call(other_kernel, out_shape=block_out + (jax.ShapeDtypeStruct(...]
    reshape x2 -> x0, local copies, waits for them, and re-layouts: 1.73 us -> none  [the longest x1 1.41 us: shards(): classes.reshape(2, HALF_CLASSES, -1)]
    another operation x3 -> x0, other arithmetic: 1.34 us -> none  [the longest x2 1.32 us: shards(): small = jnp.stack([precision, rotation_offset.astype(jnp.bfloat16)])]
  transfers between devices with their start and end apart: 5 -> 5, of which waited for: 3 -> 2; matrix products, arithmetic and copies ran while one was open for 8% -> 1% of each run, Pallas kernels for 0% -> 6%
where the time goes in v2:
time: 67.8 us; the launch traced here: 67.5 us
  blocking collectives  29.3 us (43%)
  waiting for transfers between devices  17.1 us (25%)
  Pallas kernels  11.1 us (16%)
  starting transfers between devices  5.85 us (9%)
  local copies, waits for them, and re-layouts  3.02 us (4%)
  between operations  0.73 us (1%)
    all_to_all x1, blocking collectives, shards(): got = lax.all_to_all(parts.astype(jnp.float16), 'cls', 0, 0, tiled=True)  29.3 us
    all_to_all x1, waiting for transfers between devices, shards(): whole = lax.all_to_all(repeated, 'cls', 0, 0, tiled=True)  16.3 us
    all_to_all x1, starting transfers between devices, shards(): whole = lax.all_to_all(repeated, 'cls', 0, 0, tiled=True)  4.68 us
    pallas_call x1, Pallas kernels, shards(): pl.pallas_call(other_kernel, out_shape=block_out + (jax.ShapeDtypeStruct(...  3.45 us
    pallas_call x1, Pallas kernels, shards(): pl.pallas_call(own_kernel, out_shape=block_out + (jax.ShapeDtypeStruct((1...  3.45 us
    pallas_call x1, Pallas kernels, shards(): pl.pallas_call(sums_kernel, out_shape=(jax.ShapeDtypeStruct((CHUNKS, HALF...  1.82 us
    pallas_call x1, Pallas kernels, shards(): pl.pallas_call(finish_kernel, out_shape=jax.ShapeDtypeStruct((CLASSES, BL...  1.53 us
    unnamed x12, local copies, waits for them, and re-layouts  1.46 us
  transfers between devices with their start and end apart: 5, of which 2 were waited for; matrix products, arithmetic and copies ran while one was open for 1% of the time, Pallas kernels for 6%

profile of v2, /device:TPU:0, one launch (start us, length us, event | category | flops | bytes accessed | tf_op | source)
XLA Modules:
  0.0 67.5 jit_solution(9372716964583303045)
XLA Ops:
  0.6 0.1 collective-permute-start
  0.7 0.5 collective-permute-start.1
  1.2 0.1 collective-permute-start.2
  1.3 1.2 %copy-done = bf16[100,4096]{1,0:T(8,128)(2,1)S(1)} copy-done((bf16[100,4096]{1,0:T(8,128)(2,1)S(1)}, bf16[100,4096]{1,0:T(8,128)(2,1)}, u32[]{:S(2)}) %copy-start) | copy-done | bytes 819224
  2.5 0.8 %classes.1 = (bf16[19,208,256]{2,1,0:T(8,128)(2,1)S(1)}, f32[104,128]{1,0:T(8,128)S(1)}) custom-call(bf16[100,4096]{1,0:T(8,128)(2,1)S(1)} %copy-done), custom_call_target="tpu_custom_call" | custom-call | flops 4000000000 | bytes 8388608 | tf_op jit(solution)/shard_map/classes/pallas_call | solution.py:328
  3.3 0.3 copy-done.2
  3.6 3.5 %own_scores.1 = (f32[36,104,128]{2,1,0:T(8,128)S(1)}, bf16[128,4864]{1,0:T(8,128)(2,1)S(1)}, f32[16,128]{1,0:T(8,128)S(1)}) custom-call(s32[2,20]{1,0:T(2,128)S(1)} %copy-done.3, bf16[96,4096]{1,0:T(8,128)(2,1)S(1)} %copy-done.2, bf16[1,96]{1,0:T(2,128)(2,1)S(1)} %bitcast.8, s32[1,96]{1,0:T(1,128)S(1)} %bitcast.9, ...), custom_call_target="tpu_custom_call" | custom-call | flops 4000000000 | bytes 8388608 | tf_op jit(solution)/shard_map/own_scores/pallas_call | solution.py:338
  7.1 0.0 collective-permute-done.1
  7.1 0.0 collective-permute-done.2
  7.1 0.0 collective-permute-done.image_ref
  7.1 3.5 %other_scores.1 = (f32[36,104,128]{2,1,0:T(8,128)S(1)}, bf16[128,4864]{1,0:T(8,128)(2,1)S(1)}, f32[2,16,128]{2,1,0:T(8,128)S(1)}) custom-call(s32[2,20]{1,0:T(2,128)S(1)} %copy-done.3, bf16[96,4096]{1,0:T(8,128)(2,1)S(1)} %collective-permute-done.image_ref, bf16[1,96]{1,0:T(2,128)(2,1)S(1)} %bitcast.10, s32[1,96]{1,0:T(1,128)S(1)} %bitcast.11, ...), custom_call_target="tpu_custom_call" | custom-call | flops 4000000000 | bytes 8388608 | tf_op jit(solution)/shard_map/other_scores/pallas_call | solution.py:349
  10.6 0.5 collective-permute-start.3
  11.1 0.8 %collective-permute-done.3.theirs = f32[2,16,128]{2,1,0:T(8,128)S(1)} collective-permute-done((f32[2,16,128]{2,1,0:T(8,128)S(1)}, f32[2,16,128]{2,1,0:T(8,128)S(1)}, u32[]{:S(2)}, u32[]{:S(2)}) %collective-permute-start.3) | collective-permute-done | bytes 16416 | tf_op jit(solution)/shard_map/ppermute | solution.py:359
  11.9 1.8 %sums.1 = (f32[64,56,128]{2,1,0:T(8,128)S(1)}, f32[8,128]{1,0:T(8,128)S(1)}) custom-call(f32[36,104,128]{2,1,0:T(8,128)S(1)} %get-tuple-element.14.w_a, f32[36,104,128]{2,1,0:T(8,128)S(1)} %get-tuple-element.16.w_b, bf16[128,4864]{1,0:T(8,128)(2,1)S(1)} %get-tuple-element.17.xp_a, bf16[128,4864]{1,0:T(8,128)(2,1)S(1)} %get-tuple-element.18.xp_b, ...), custom_call_target="tpu_custom_call" | custom-call | tf_op jit(solution)/shard_map/sums/pallas_call | solution.py:361
  13.7 0.1 convert_element_type.14
  13.9 29.3 %all_to_all.10 = f16[64,56,128]{2,1,0:T(8,128)(2,1)S(1)} all-to-all(f16[64,56,128]{2,1,0:T(8,128)(2,1)S(1)} %convert_element_type.14), channel_id=1, replica_groups=mesh['dom'=2,'cls'=64] {'cls'}, dimensions={0} | all-to-all | bytes 1835008 | tf_op jit(solution)/shard_map/all_to_all | solution.py:374
  43.2 0.2 convert_reduce_fusion
  43.3 1.0 %broadcast_in_dim.2 = f16[64,56,128]{2,1,0:T(8,128)(2,1)} broadcast(f16[56,128]{1,0:T(8,128)(2,1)S(1)} %convert_element_type.16), dimensions={1,2} | broadcast | bytes 931840 | tf_op jit(solution)/shard_map/broadcast_in_dim | solution.py:376
  44.4 4.7 %all-to-all-start.1 = ((f16[64,56,128]{2,1,0:T(8,128)(2,1)}), f16[64,56,128]{2,1,0:T(8,128)(2,1)S(1)}, u32[]{:S(2)}, u32[]{:S(2)}) async-start(f16[64,56,128]{2,1,0:T(8,128)(2,1)} %broadcast_in_dim.2), calls=%async_computation.1 | async-start | bytes 1835008 | tf_op jit(solution)/shard_map/all_to_all | solution.py:377
  49.1 0.0 copy-start.1
  49.1 0.5 slice_bitcast_fusion
  49.6 16.3 %all-to-all-done.1 = f16[64,56,128]{2,1,0:T(8,128)(2,1)S(1)} async-done(((f16[64,56,128]{2,1,0:T(8,128)(2,1)}), f16[64,56,128]{2,1,0:T(8,128)(2,1)S(1)}, u32[]{:S(2)}, u32[]{:S(2)}) %all-to-all-start.1) | async-done | bytes 917536 | tf_op jit(solution)/shard_map/all_to_all | solution.py:377
  65.9 0.1 convert.1.sum_ref
  66.0 1.5 %finish.1 = f32[100,4096]{1,0:T(8,128)} custom-call(f32[2,32,56,128]{3,2,1,0:T(8,128)S(1)} %convert.1.sum_ref, bf16[100,4096]{1,0:T(8,128)(2,1)S(1)} %copy-done.1), custom_call_target="tpu_custom_call" | custom-call | tf_op jit(solution)/shard_map/finish/pallas_call | solution.py:378
  (10 shorter events, 0.0 us)
Async XLA Ops:
  0.6 6.5 %collective-permute-start = (bf16[96,4096]{1,0:T(8,128)(2,1)}, bf16[96,4096]{1,0:T(8,128)(2,1)S(1)}, u32[]{:S(2)}, u32[]{:S(2)}) collective-permute-start(bf16[96,4096]{1,0:T(8,128)(2,1)} %image_ref.1), channel_id=1, source_target_pairs={{0,64},{64,0},{1,65},{65,1},{2,66},{66,2},{3,67},{67,3},{4,68},{68... | collective-permute-start | bytes 2359304 | tf_op jit(solution)/shard_map/ppermute | solution.py:308
  0.7 6.3 %collective-permute-start.1 = (bf16[96]{0:T(256)(128)(2,1)}, bf16[96]{0:T(256)(128)(2,1)S(1)}, u32[]{:S(2)}, u32[]{:S(2)}) collective-permute-start(bf16[96]{0:T(256)(128)(2,1)} %param.6), channel_id=1, source_target_pairs={{0,64},{64,0},{1,65},{65,1},{2,66},{66,2},{3,67},{67,3},{4,68},{68... | collective-permute-start | bytes 584 | tf_op jit(solution)/shard_map/ppermute | solution.py:309
  1.2 5.9 %collective-permute-start.2 = (s32[96]{0:T(128)}, s32[96]{0:T(128)S(1)}, u32[]{:S(2)}, u32[]{:S(2)}) collective-permute-start(s32[96]{0:T(128)} %param.7), channel_id=1, source_target_pairs={{0,64},{64,0},{1,65},{65,1},{2,66},{66,2},{3,67},{67,3},{4,68},{68... | collective-permute-start | bytes 1160 | tf_op jit(solution)/shard_map/ppermute | solution.py:310
  1.3 1.2 %copy-start = (bf16[100,4096]{1,0:T(8,128)(2,1)S(1)}, bf16[100,4096]{1,0:T(8,128)(2,1)}, u32[]{:S(2)}) copy-start(bf16[100,4096]{1,0:T(8,128)(2,1)} %cls_hbm.1) | copy-start | bytes 2457604
  2.5 1.1 %copy-start.2 = (bf16[96,4096]{1,0:T(8,128)(2,1)S(1)}, bf16[96,4096]{1,0:T(8,128)(2,1)}, u32[]{:S(2)}) copy-start(bf16[96,4096]{1,0:T(8,128)(2,1)} %image_ref.1) | copy-start | bytes 2359300
  2.5 1.1 %copy-start.3 = (s32[2,20]{1,0:T(2,128)S(1)}, s32[2,20]{1,0:T(2,128)}, u32[]{:S(2)}) copy-start(s32[2,20]{1,0:T(2,128)} %blocks_ref.3) | copy-start | bytes 484
  2.5 1.1 %copy-start.4 = (bf16[96]{0:T(256)(128)(2,1)S(1)}, bf16[96]{0:T(256)(128)(2,1)}, u32[]{:S(2)}) copy-start(bf16[96]{0:T(256)(128)(2,1)} %param.6) | copy-start | bytes 580
  2.5 1.1 %copy-start.5 = (s32[96]{0:T(128)S(1)}, s32[96]{0:T(128)}, u32[]{:S(2)}) copy-start(s32[96]{0:T(128)} %param.7) | copy-start | bytes 1156
  10.6 1.3 %collective-permute-start.3 = (f32[2,16,128]{2,1,0:T(8,128)S(1)}, f32[2,16,128]{2,1,0:T(8,128)S(1)}, u32[]{:S(2)}, u32[]{:S(2)}) collective-permute-start(f32[2,16,128]{2,1,0:T(8,128)S(1)} %get-tuple-element.19.mine), channel_id=1, source_target_pairs={{0,64},{64,0},{1,65},{65,1},{2,66},{66,2},{3,67},{67,3},{4,68},{68... | collective-permute-start | bytes 49160 | tf_op jit(solution)/shard_map/ppermute | solution.py:359
  44.4 21.5 %all-to-all-start.1 = ((f16[64,56,128]{2,1,0:T(8,128)(2,1)}), f16[64,56,128]{2,1,0:T(8,128)(2,1)S(1)}, u32[]{:S(2)}, u32[]{:S(2)}) async-start(f16[64,56,128]{2,1,0:T(8,128)(2,1)} %broadcast_in_dim.2), calls=%async_computation.1 | async-start | bytes 1835008 | tf_op jit(solution)/shard_map/all_to_all | solution.py:377
  49.1 16.9 %copy-start.1 = (bf16[100,4096]{1,0:T(8,128)(2,1)S(1)}, bf16[100,4096]{1,0:T(8,128)(2,1)}, u32[]{:S(2)}) copy-start(bf16[100,4096]{1,0:T(8,128)(2,1)} %cls_hbm.1) | copy-start | bytes 2457604

commit v3 on v2

v3 whole, which is shorter than its diff:
```python
import math

import jax
import jax.numpy as jnp
import numpy as np
from jax import lax
from jax.experimental import pallas as pl
from jax.experimental.pallas import tpu as pltpu
from jax.sharding import PartitionSpec as P

FREQUENCIES = 64
CYCLES = 32
PART = FREQUENCIES * CYCLES
ROTATIONS = 36
CLASS_BLOCK = 5
EXCLUDED = -1e30
PRIOR_WIDTH = 12.0
CLASS_PRIOR = 16.0

RESIDUES = 19
GROUP = 4
LANES = 128
OWN = 96
CLASSES = 100
ROWS = 104
SPLIT = 48
HALF_ROWS = 56
TOTAL_ROW = 52
COLS = 2 * LANES
CHUNKS = 64
BLOCKS = 32
SUM_SCALE = 0.25

MEMBERS = []
for _j in range(RESIDUES):
    _same = [(m, 1) for m in range(FREQUENCIES) if m % ROTATIONS == _j]
    _back = [(m, -1) for m in range(FREQUENCIES) if m % ROTATIONS == (ROTATIONS - _j) % ROTATIONS and _j not in (0, 18)]
    MEMBERS.append(_same + _back)


def cosine(k):
    return float(np.cos(2.0 * np.pi * k / 9.0))


def sine(k):
    return float(np.sin(2.0 * np.pi * k / 9.0))


def nine_cos(x):
    c1, c2 = cosine(1), cosine(2)
    t, u = x[0] + x[3], (x[1] + x[2]) + x[4]
    base = x[0] - 0.5 * x[3]
    p, q = x[1] - x[4], x[2] - x[4]
    y1 = base + (p * c1 + q * c2)
    y2 = base + ((p - q) * c2 - q * c1)
    y4 = base - ((p - q) * c1 + p * c2)
    return [t + u, y1, y2, t - 0.5 * u, y4]


def nine_sin(x):
    s1, s3, s4 = sine(1), sine(3), sine(4)
    p, q = x[1] + x[2], x[2] + x[4]
    d = p - q
    t = x[3] * s3
    return [None, t + (p * s1 + q * s4), (d * s1 + p * s4) - t, ((x[1] - x[2]) + x[4]) * s3, t + (d * s4 - q * s1)]


def fold(j):
    j %= ROTATIONS
    return (j, 1) if j <= 18 else (ROTATIONS - j, -1)


def signed(values, j):
    at, sign = fold(j)
    return values[at] if sign > 0 else -values[at]


def rotation_of(r4, r9):
    return next(r for r in range(ROTATIONS) if r % 4 == r4 and r % 9 == r9)


def to_rotations(a, b):
    one = ([a[0]] + [a[fold(4 * k)[0]] for k in range(1, 5)], [None] + [signed(b, 4 * k) for k in range(1, 5)])
    alt = ([a[18]] + [a[fold(18 + 4 * k)[0]] for k in range(1, 5)], [None] + [signed(b, 18 + 4 * k) for k in range(1, 5)])
    cc, cs, sc, ss = [a[9]], [None], [b[9]], [None]
    for k in range(1, 5):
        a_p, b_p = a[fold(9 + 4 * k)[0]], b[fold(9 + 4 * k)[0]]
        a_m, b_m = a[fold(9 - 4 * k)[0]], b[fold(9 - 4 * k)[0]]
        assert fold(9 + 4 * k)[1] == fold(9 - 4 * k)[1]
        cc.append(a_p + a_m)
        ss.append(a_m - a_p)
        if fold(9 + 4 * k)[1] > 0:
            sc.append(b_p + b_m)
            cs.append(b_p - b_m)
        else:
            sc.append(-(b_p + b_m))
            cs.append(b_m - b_p)
    lines = []
    for even, odd in (one, alt, (cc, cs), (sc, ss)):
        e, o = nine_cos(even), nine_sin(odd)
        lines.append([e[0]] + [e[r] + o[r] for r in range(1, 5)] + [e[9 - r] - o[9 - r] for r in range(5, 9)])
    y = [None] * ROTATIONS
    for r9 in range(9):
        g1, gm, gc, gs = (line[r9] for line in lines)
        plus, minus = g1 + gm, g1 - gm
        y[rotation_of(0, r9)] = plus + gc
        y[rotation_of(2, r9)] = plus - gc
        y[rotation_of(1, r9)] = minus + gs
        y[rotation_of(3, r9)] = minus - gs
    return y


def from_rotations(e):
    lines = [[], [], [], []]
    for r9 in range(9):
        e0, e1, e2, e3 = (e[rotation_of(r4, r9)] for r4 in range(4))
        p, q = e0 + e2, e1 + e3
        for line, value in zip(lines, (p + q, p - q, e0 - e2, e1 - e3)):
            line.append(value)
    spectra = []
    for h in lines:
        even = [h[0]] + [h[k] + h[9 - k] for k in range(1, 5)]
        odd = [None] + [h[k] - h[9 - k] for k in range(1, 5)]
        spectra.append((nine_cos(even), nine_sin(odd)))
    (one_c, one_s), (alt_c, alt_s), (cc, cs), (sc, ss) = spectra
    c, s = [None] * RESIDUES, [None] * RESIDUES
    c[0], c[18], c[9], s[9] = one_c[0], alt_c[0], cc[0], sc[0]
    for k in range(1, 5):
        for first, cosines, sines in ((0, one_c, one_s), (18, alt_c, alt_s)):
            at, sign = fold(first + 4 * k)
            c[at], s[at] = cosines[k], sines[k] if sign > 0 else -sines[k]
        at_p, sign = fold(9 + 4 * k)
        at_m, _ = fold(9 - 4 * k)
        c[at_p], c[at_m] = cc[k] - ss[k], cc[k] + ss[k]
        if sign > 0:
            s[at_p], s[at_m] = sc[k] + cs[k], sc[k] - cs[k]
        else:
            s[at_p], s[at_m] = -(sc[k] + cs[k]), cs[k] - sc[k]
    return c, s


def gather_lanes(ref, part, j):
    rows = ref.shape[0]
    pieces = [ref[:, part * PART + m * CYCLES : part * PART + (m + 1) * CYCLES] for m, _ in MEMBERS[j]]
    if len(pieces) < GROUP:
        pieces.append(jnp.zeros((rows, (GROUP - len(pieces)) * CYCLES), ref.dtype))
    return jnp.concatenate(pieces, axis=1)


def sign_lanes(j, rows):
    lane = lax.broadcasted_iota(jnp.int32, (rows, LANES), 1)
    same = sum(1 for _, s in MEMBERS[j] if s > 0) * CYCLES
    return jnp.where(lane < same, 1.0, -1.0)


def particle_row(values):
    return jnp.concatenate([values, jnp.zeros((1, LANES - OWN), values.dtype)], axis=1)


def arrange_classes(cls_ref, cp_ref, norm_ref):
    zeros = jnp.zeros((ROWS - CLASSES, COLS), jnp.float32)
    norm = jnp.zeros((CLASSES, LANES), jnp.float32)
    for j in range(RESIDUES):
        c_re = gather_lanes(cls_ref, 0, j).astype(jnp.float32)
        c_im = gather_lanes(cls_ref, 1, j).astype(jnp.float32)
        norm = norm + c_re * c_re + c_im * c_im
        cosine = jnp.concatenate([jnp.concatenate([c_re, c_im], axis=1), zeros], axis=0)
        if 0 < j < 18:
            sign = sign_lanes(j, CLASSES)
            sine = jnp.concatenate([jnp.concatenate([c_im * sign, -(c_re * sign)], axis=1), zeros], axis=0)
        else:
            sine = jnp.zeros((ROWS, COLS), jnp.float32)
        cp_ref[j] = jnp.concatenate([cosine, sine], axis=0).astype(jnp.bfloat16)
    norm = jnp.broadcast_to(jnp.sum(norm, axis=1, keepdims=True), (CLASSES, LANES))
    norm_ref[...] = jnp.concatenate([norm, jnp.zeros((ROWS - CLASSES, LANES), jnp.float32)], axis=0)


def score_kernel(blocks_ref, own_ref, other_ref, prec_a, prec_b, offset_a, offset_b, cp_ref, norm_ref, e_ref, xp_ref, stat_ref, ab_ref, base_ref, prior_ref):
    row = lax.broadcasted_iota(jnp.int32, (ROWS, LANES), 0)
    dom = lax.axis_index("dom")
    precisions = [particle_row(p[...].astype(jnp.float32)) for p in (prec_a, prec_b)]
    for half in range(2):
        lanes = slice(half * LANES, (half + 1) * LANES)
        block_row = dom if half == 0 else 1 - dom
        admit = jnp.zeros((ROWS, LANES), jnp.int32)
        for block in range(CLASSES // CLASS_BLOCK):
            inside = (row >= block * CLASS_BLOCK) & (row < (block + 1) * CLASS_BLOCK)
            admit = jnp.where(inside, blocks_ref[block_row, block], admit)
        base_ref[:, lanes] = jnp.where(admit == 1, -0.5 * norm_ref[...] * precisions[half], EXCLUDED)
        offset = particle_row((offset_a, offset_b)[half][...])
        steps = lax.rem(lax.broadcasted_iota(jnp.int32, (40, LANES), 0) - offset + ROTATIONS, ROTATIONS)
        distance = jnp.minimum(steps, ROTATIONS - steps).astype(jnp.float32) * (1.0 / PRIOR_WIDTH)
        prior_ref[:, lanes] = -0.5 * distance * distance
    zeros = jnp.zeros((LANES - OWN, RESIDUES * COLS), jnp.bfloat16)
    xp_ref[OWN:LANES] = zeros
    xp_ref[LANES + OWN :] = zeros
    for j in range(RESIDUES):
        for part in range(2):
            at = j * COLS + part * LANES
            xp_ref[0:OWN, at : at + LANES] = gather_lanes(own_ref, part, j)
            xp_ref[LANES : LANES + OWN, at : at + LANES] = gather_lanes(other_ref, part, j)
        got = lax.dot_general(
            cp_ref[j], xp_ref[:, j * COLS : (j + 1) * COLS], (((1,), (1,)), ((), ())), preferred_element_type=jnp.float32
        )
        ab_ref[j] = got[:ROWS]
        if 0 < j < 18:
            ab_ref[18 + j] = got[ROWS:]

    for half in range(2):
        lanes = slice(half * LANES, (half + 1) * LANES)
        prec = jnp.broadcast_to(precisions[half], (8, LANES))

        def scores(i, peak):
            rows = pl.ds(pl.multiple_of(i * 8, 8), 8)
            a = [ab_ref[j, rows, lanes] for j in range(19)]
            b = [None] + [ab_ref[18 + j, rows, lanes] for j in range(1, 18)]
            base = base_ref[rows, lanes]
            correlation = to_rotations(a, b)
            for r in range(ROTATIONS):
                score = correlation[r] * prec + (base + prior_ref[r : r + 1, lanes])
                e_ref[r, rows, lanes] = score
                peak = jnp.maximum(peak, score)
            return peak

        peak = lax.fori_loop(0, ROWS // 8, scores, jnp.full((8, LANES), EXCLUDED, jnp.float32), unroll=True)
        peak = jnp.broadcast_to(jnp.max(peak, axis=0, keepdims=True), (8, LANES))

        def masses(i, mass):
            rows = pl.ds(pl.multiple_of(i * 8, 8), 8)
            for r in range(ROTATIONS):
                e = jnp.exp(e_ref[r, rows, lanes] - peak)
                e_ref[r, rows, lanes] = e
                mass = mass + e
            return mass

        mass = lax.fori_loop(0, ROWS // 8, masses, jnp.zeros((8, LANES), jnp.float32), unroll=True)
        stat_ref[0:8, lanes] = peak
        stat_ref[8:16, lanes] = jnp.broadcast_to(jnp.sum(mass, axis=0, keepdims=True), (8, LANES))


def spectrum_kernel(e_ref, w_ref):
    for half in range(2):
        lanes = slice(half * LANES, (half + 1) * LANES)

        def spectra(i, carry):
            rows = pl.ds(pl.multiple_of(i * 8, 8), 8)
            c, s = from_rotations([e_ref[r, rows, lanes] for r in range(ROTATIONS)])
            for j in range(19):
                w_ref[j, rows, lanes] = c[j]
            for j in range(1, 18):
                w_ref[18 + j, rows, lanes] = s[j]
            return carry

        lax.fori_loop(0, ROWS // 8, spectra, 0, unroll=True)


def class_kernel(cls_ref, cp_ref, norm_ref):
    arrange_classes(cls_ref, cp_ref, norm_ref)


def sums_kernel(w_ref, xp_ref, mine, theirs, out_ref, evidence_ref, pc_ref):
    held = lax.broadcasted_iota(jnp.int32, (1, LANES), 1) < OWN

    def settle(half):
        here = slice(half * LANES, (half + 1) * LANES)
        there = slice((1 - half) * LANES, (2 - half) * LANES)
        peak = jnp.maximum(mine[0:1, here], theirs[0:1, there])
        lift = jnp.exp(mine[0:1, here] - peak)
        mass = mine[8:9, here] * lift + theirs[8:9, there] * jnp.exp(theirs[0:1, there] - peak)
        mass = jnp.where(held, mass, 1.0)
        return jnp.where(held, lift / mass, 0.0), peak + jnp.log(mass)

    scale_a, evidence = settle(0)
    scale_b, _ = settle(1)
    scale = jnp.concatenate([scale_a, scale_b], axis=1)
    evidence_ref[...] = evidence[:, :OWN]

    def weights_of(i):
        return w_ref[i] * scale

    totals = weights_of(0)
    totals = jnp.concatenate([totals, jnp.zeros((LANES - ROWS, COLS), jnp.float32)], axis=0)
    high = totals.astype(jnp.bfloat16)
    low = (totals - high.astype(jnp.float32)).astype(jnp.bfloat16)
    ones = jnp.ones((16, COLS), jnp.bfloat16)
    dims = (((1,), (1,)), ((), ()))
    total = lax.dot_general(ones, high, dims, preferred_element_type=jnp.float32)
    total = total + lax.dot_general(ones, low, dims, preferred_element_type=jnp.float32)
    total = total[0:1]

    for j in range(RESIDUES):
        pair = 0 < j < 18
        weight = weights_of(j)
        if pair:
            weight = jnp.concatenate([weight, weights_of(18 + j)], axis=0)
        else:
            weight = jnp.concatenate([weight, jnp.zeros((8, COLS), jnp.float32)], axis=0)
        high = weight.astype(jnp.bfloat16)
        low = (weight - high.astype(jnp.float32)).astype(jnp.bfloat16)
        lanes = slice(j * COLS, (j + 1) * COLS)
        images = xp_ref[:, lanes]
        dims = (((1,), (0,)), ((), ()))
        got = lax.dot_general(high, images, dims, preferred_element_type=jnp.float32)
        got = got + lax.dot_general(low, images, dims, preferred_element_type=jnp.float32)
        re, im = got[:ROWS, :LANES], got[:ROWS, LANES:]
        if pair:
            sign = sign_lanes(j, ROWS)
            re, im = re - sign * got[ROWS:, LANES:], im + sign * got[ROWS:, :LANES]
        pc_ref[:, j * COLS : j * COLS + LANES] = re * SUM_SCALE
        pc_ref[:, j * COLS + LANES : (j + 1) * COLS] = im * SUM_SCALE

    place = {}
    for j in range(RESIDUES):
        for at, (m, _) in enumerate(MEMBERS[j]):
            place[m] = j * COLS + at * CYCLES
    row = lax.broadcasted_iota(jnp.int32, (HALF_ROWS, LANES), 0)
    for block in range(BLOCKS):
        part, first = divmod(block, BLOCKS // 2)
        starts = [place[first * GROUP + q] + part * LANES for q in range(GROUP)]
        whole = jnp.concatenate([pc_ref[:, at : at + CYCLES] for at in starts], axis=1)
        for half in range(2):
            rows = whole[half * SPLIT : half * SPLIT + HALF_ROWS]
            out_ref[half * BLOCKS + block] = jnp.where(row == TOTAL_ROW, total * SUM_SCALE, rows)


FINISH_STEPS = 4
STEP_BLOCKS = BLOCKS // FINISH_STEPS


def finish_kernel(sum_ref, cls_hbm, out_hbm, cls_ref, out_ref, cls_sem, out_sems):
    fetch = pltpu.make_async_copy(cls_hbm, cls_ref, cls_sem)
    fetch.start()
    row = lax.broadcasted_iota(jnp.int32, (HALF_ROWS, LANES), 0)
    lane = lax.broadcasted_iota(jnp.int32, (HALF_ROWS, LANES), 1)
    share = []
    for half in range(2):
        total = sum_ref[half, 0, TOTAL_ROW : TOTAL_ROW + 1, :]
        weight = jnp.sum(jnp.where(lane == row + half * SPLIT, total, 0.0), axis=1, keepdims=True)
        share.append(1.0 / (weight * (1.0 / SUM_SCALE) + CLASS_PRIOR))
    fetch.wait()
    copies = []
    for step in range(FINISH_STEPS):
        for block in range(step * STEP_BLOCKS, (step + 1) * STEP_BLOCKS):
            lanes = slice(block * LANES, (block + 1) * LANES)
            old = cls_ref[:, lanes].astype(jnp.float32)
            for half in range(2):
                count = SPLIT if half == 0 else CLASSES - SPLIT
                rows = slice(half * SPLIT, half * SPLIT + count)
                new = sum_ref[half, block, 0:count] * (1.0 / SUM_SCALE) + CLASS_PRIOR * old[rows]
                out_ref[rows, lanes] = new * share[half][:count]
        lanes = slice(step * STEP_BLOCKS * LANES, (step + 1) * STEP_BLOCKS * LANES)
        copy = pltpu.make_async_copy(out_ref.at[:, lanes], out_hbm.at[:, lanes], out_sems.at[step])
        copy.start()
        copies.append(copy)
    for copy in copies:
        copy.wait()


VMEM = pl.BlockSpec(memory_space=pltpu.VMEM)
SMEM = pl.BlockSpec(memory_space=pltpu.SMEM)


ANY = pl.BlockSpec(memory_space=pl.ANY)
MIB = 1024 * 1024


def shards(images, precision, rotation_offset, classes, prior_blocks):
    swap = [(0, 1), (1, 0)]
    other_images = lax.ppermute(images, "dom", swap)
    other_precision = lax.ppermute(precision, "dom", swap)
    other_offset = lax.ppermute(rotation_offset, "dom", swap)

    cost = pl.CostEstimate(flops=4 * 10**9, bytes_accessed=8 * MIB, transcendentals=36 * 104 * 128)
    cp, norm = pl.pallas_call(
        class_kernel,
        out_shape=(
            jax.ShapeDtypeStruct((RESIDUES, 2 * ROWS, COLS), jnp.bfloat16),
            jax.ShapeDtypeStruct((ROWS, LANES), jnp.float32),
        ),
        in_specs=[VMEM],
        out_specs=(VMEM,) * 2,
        compiler_params=pltpu.CompilerParams(vmem_limit_bytes=12 * MIB),
        cost_estimate=cost,
        name="classes",
    )(classes)

    e, by_residue, mine = pl.pallas_call(
        score_kernel,
        out_shape=(
            jax.ShapeDtypeStruct((36, ROWS, COLS), jnp.float32),
            jax.ShapeDtypeStruct((COLS, RESIDUES * COLS), jnp.bfloat16),
            jax.ShapeDtypeStruct((16, COLS), jnp.float32),
        ),
        in_specs=[SMEM] + [VMEM] * 8,
        out_specs=(VMEM,) * 3,
        scratch_shapes=[
            pltpu.VMEM((36, ROWS, COLS), jnp.float32),
            pltpu.VMEM((ROWS, COLS), jnp.float32),
            pltpu.VMEM((40, COLS), jnp.float32),
        ],
        compiler_params=pltpu.CompilerParams(vmem_limit_bytes=20 * MIB),
        cost_estimate=cost,
        name="scores",
    )(
        prior_blocks,
        images,
        other_images,
        precision.reshape(1, OWN),
        other_precision.reshape(1, OWN),
        rotation_offset.reshape(1, OWN),
        other_offset.reshape(1, OWN),
        cp,
        norm,
    )
    theirs = lax.ppermute(mine, "dom", swap)

    weights = pl.pallas_call(
        spectrum_kernel,
        out_shape=jax.ShapeDtypeStruct((36, ROWS, COLS), jnp.float32),
        in_specs=[VMEM],
        out_specs=VMEM,
        compiler_params=pltpu.CompilerParams(vmem_limit_bytes=16 * MIB),
        cost_estimate=cost,
        name="spectra",
    )(e)

    parts, evidence = pl.pallas_call(
        sums_kernel,
        out_shape=(
            jax.ShapeDtypeStruct((CHUNKS, HALF_ROWS, LANES), jnp.float32),
            jax.ShapeDtypeStruct((1, OWN), jnp.float32),
        ),
        in_specs=[VMEM] * 4,
        out_specs=(VMEM, VMEM),
        scratch_shapes=[pltpu.VMEM((ROWS, RESIDUES * COLS), jnp.float32)],
        compiler_params=pltpu.CompilerParams(vmem_limit_bytes=20 * MIB),
        name="sums",
    )(weights, by_residue, mine, theirs)

    got = lax.all_to_all(parts.astype(jnp.float16), "cls", 0, 0, tiled=True)
    total = jnp.sum(got.astype(jnp.float32), axis=0).astype(jnp.float16)
    repeated = jnp.broadcast_to(total[None], (CHUNKS, HALF_ROWS, LANES))
    whole = lax.all_to_all(repeated, "cls", 0, 0, tiled=True)
    new_classes = pl.pallas_call(
        finish_kernel,
        out_shape=jax.ShapeDtypeStruct((CLASSES, BLOCKS * LANES), jnp.float32),
        in_specs=[VMEM, ANY],
        out_specs=ANY,
        scratch_shapes=[
            pltpu.VMEM(classes.shape, jnp.bfloat16),
            pltpu.VMEM((CLASSES, BLOCKS * LANES), jnp.float32),
            pltpu.SemaphoreType.DMA,
            pltpu.SemaphoreType.DMA((FINISH_STEPS,)),
        ],
        compiler_params=pltpu.CompilerParams(vmem_limit_bytes=12 * MIB),
        name="finish",
    )(whole.astype(jnp.float32).reshape(2, BLOCKS, HALF_ROWS, LANES), classes)
    return new_classes, evidence.reshape(OWN)


def solution(mesh):
    in_specs = (
        P(("cls", "dom"), None),
        P(("cls", "dom")),
        P(("cls", "dom")),
        P("dom", None),
        P("cls", "dom"),
    )
    out_specs = (P("dom", None), P(("cls", "dom")))
    return jax.shard_map(shards, mesh=mesh, in_specs=in_specs, out_specs=out_specs, check_vma=False)
```

time: 67.8 us -> 64.7 us (0.954)
  blocking collectives: 29.3 us -> 50.4 us
  waiting for transfers between devices: 17.1 us -> 0.01 us
  starting transfers between devices: 5.85 us -> 1.17 us
  local copies, waits for them, and re-layouts: 3.02 us -> 1.55 us
  Pallas kernels: 11.1 us -> 10.2 us
    all_to_all x0 -> x1, blocking collectives: none -> 21.2 us  [shards(): whole = lax.all_to_all(repeated, 'cls', 0, 0, tiled=True)]
    all_to_all x1 -> x0, waiting for transfers between devices: 16.3 us -> none  [shards(): whole = lax.all_to_all(repeated, 'cls', 0, 0, tiled=True)]
    all_to_all x1 -> x0, starting transfers between devices: 4.68 us -> none  [shards(): whole = lax.all_to_all(repeated, 'cls', 0, 0, tiled=True)]
    pallas_call x3, Pallas kernels: 7.74 us -> 6.49 us  [the longest x1 4.68 us: shards(): pl.pallas_call(score_kernel, out_shape=(jax.ShapeDtypeStruct((36, ROWS, C...]
    broadcast_in_dim x1, local copies, waits for them, and re-layouts: 1.05 us -> 0.12 us  [shards(): repeated = jnp.broadcast_to(total[None], (CHUNKS, HALF_ROWS, LANES))]
    ppermute x1, waiting for transfers between devices: 0.84 us -> 0.01 us  [shards(): theirs = lax.ppermute(mine, 'dom', swap)]
  transfers between devices with their start and end apart: 5 -> 4, of which waited for: 2 -> 0; matrix products, arithmetic and copies ran while one was open for 1% -> 0% of each run, Pallas kernels for 6% -> 3%
where the time goes in v3:
time: 64.7 us; the launch traced here: 64.4 us
  blocking collectives  50.4 us (78%)
  Pallas kernels  10.2 us (16%)
  local copies, waits for them, and re-layouts  1.55 us (2%)
  starting transfers between devices  1.17 us (2%)
  between operations  0.72 us (1%)
    all_to_all x1, blocking collectives, shards(): got = lax.all_to_all(parts.astype(jnp.float16), 'cls', 0, 0, tiled=True)  29.2 us
    all_to_all x1, blocking collectives, shards(): whole = lax.all_to_all(repeated, 'cls', 0, 0, tiled=True)  21.2 us
    pallas_call x1, Pallas kernels, shards(): pl.pallas_call(score_kernel, out_shape=(jax.ShapeDtypeStruct((36, ROWS, C...  4.68 us
    pallas_call x1, Pallas kernels, shards(): pl.pallas_call(sums_kernel, out_shape=(jax.ShapeDtypeStruct((CHUNKS, HALF...  2.18 us
    pallas_call x1, Pallas kernels, shards(): pl.pallas_call(finish_kernel, out_shape=jax.ShapeDtypeStruct((CLASSES, BL...  1.53 us
    unnamed x12, local copies, waits for them, and re-layouts  1.43 us
  transfers between devices with their start and end apart: 4, of which 0 were waited for; matrix products, arithmetic and copies ran while one was open for 0% of the time, Pallas kernels for 3%

profile of v3, /device:TPU:0, one launch (start us, length us, event | category | flops | bytes accessed | tf_op | source)
XLA Modules:
  0.0 64.4 jit_solution(7841714089931396763)
XLA Ops:
  0.6 0.1 collective-permute-start
  0.7 0.5 collective-permute-start.1
  1.2 0.1 collective-permute-start.2
  1.3 1.2 %copy-done = bf16[100,4096]{1,0:T(8,128)(2,1)S(1)} copy-done((bf16[100,4096]{1,0:T(8,128)(2,1)S(1)}, bf16[100,4096]{1,0:T(8,128)(2,1)}, u32[]{:S(2)}) %copy-start) | copy-done | bytes 819224
  2.5 0.8 %classes.1 = (bf16[19,208,256]{2,1,0:T(8,128)(2,1)S(1)}, f32[104,128]{1,0:T(8,128)S(1)}) custom-call(bf16[100,4096]{1,0:T(8,128)(2,1)S(1)} %copy-done), custom_call_target="tpu_custom_call" | custom-call | flops 4000000000 | bytes 8388608 | tf_op jit(solution)/shard_map/classes/pallas_call | solution.py:374
  3.3 0.0 collective-permute-done.1
  3.3 0.0 collective-permute-done.2
  3.3 0.0 collective-permute-done.other_ref
  3.3 0.3 copy-done.2
  3.6 0.0 copy-done.3
  3.6 0.0 copy-done.4
  3.6 4.7 %scores.1 = (f32[36,104,256]{2,1,0:T(8,128)S(1)}, bf16[256,4864]{1,0:T(8,128)(2,1)S(1)}, f32[16,256]{1,0:T(8,128)S(1)}) custom-call(s32[2,20]{1,0:T(2,128)S(1)} %copy-done.3, bf16[96,4096]{1,0:T(8,128)(2,1)S(1)} %copy-done.2, bf16[96,4096]{1,0:T(8,128)(2,1)S(1)} %collective-permute-done.other_ref, bf16[1,96]{1,0:T(2,128)(2,1)S(1)} %bitcast.7, ...), custom_call_target="tpu_custom_call" | custom-call | flops 4000000000 | bytes 8388608 | tf_op jit(solution)/shard_map/scores/pallas_call | solution.py:387
  8.3 0.5 collective-permute-start.3
  8.8 1.0 %spectra.1.w_ref = f32[36,104,256]{2,1,0:T(8,128)S(1)} custom-call(f32[36,104,256]{2,1,0:T(8,128)S(1)} %get-tuple-element.11.e_ref), custom_call_target="tpu_custom_call" | custom-call | flops 4000000000 | bytes 8388608 | tf_op jit(solution)/shard_map/spectra/pallas_call | solution.py:417
  9.8 0.0 collective-permute-done.3.theirs
  9.8 2.2 %sums.1 = (f32[64,56,128]{2,1,0:T(8,128)S(1)}, f32[1,96]{1,0:T(1,128)}) custom-call(f32[36,104,256]{2,1,0:T(8,128)S(1)} %spectra.1.w_ref, bf16[256,4864]{1,0:T(8,128)(2,1)S(1)} %get-tuple-element.12.xp_ref, f32[16,256]{1,0:T(8,128)S(1)} %get-tuple-element.13.mine, f32[16,256]{1,0:T(8,128)S(1)} %collective-permute-done.3.theirs), custom_call_target="tpu_custom_call" | custom-call | tf_op jit(solution)/shard_map/sums/pallas_call | solution.py:427
  12.0 0.1 convert_element_type.14
  12.1 29.2 %all_to_all.10 = f16[64,56,128]{2,1,0:T(8,128)(2,1)S(1)} all-to-all(f16[64,56,128]{2,1,0:T(8,128)(2,1)S(1)} %convert_element_type.14), channel_id=1, replica_groups=mesh['dom'=2,'cls'=64] {'cls'}, dimensions={0} | all-to-all | bytes 1835008 | tf_op jit(solution)/shard_map/all_to_all | solution.py:440
  41.2 0.2 convert_reduce_fusion
  41.4 0.1 broadcast_in_dim.2
  41.5 0.0 copy-start.1
  41.6 21.2 %all_to_all.11 = f16[64,56,128]{2,1,0:T(8,128)(2,1)S(1)} all-to-all(f16[64,56,128]{2,1,0:T(8,128)(2,1)S(1)} %broadcast_in_dim.2), channel_id=1, replica_groups=mesh['dom'=2,'cls'=64] {'cls'}, dimensions={0} | all-to-all | bytes 1835008 | tf_op jit(solution)/shard_map/all_to_all | solution.py:443
  62.8 0.1 convert.1.sum_ref
  62.9 1.5 %finish.1 = f32[100,4096]{1,0:T(8,128)} custom-call(f32[2,32,56,128]{3,2,1,0:T(8,128)S(1)} %convert.1.sum_ref, bf16[100,4096]{1,0:T(8,128)(2,1)S(1)} %copy-done.1), custom_call_target="tpu_custom_call" | custom-call | tf_op jit(solution)/shard_map/finish/pallas_call | solution.py:444
  (8 shorter events, 0.0 us)
Async XLA Ops:
  0.6 2.7 %collective-permute-start = (bf16[96,4096]{1,0:T(8,128)(2,1)}, bf16[96,4096]{1,0:T(8,128)(2,1)S(1)}, u32[]{:S(2)}, u32[]{:S(2)}) collective-permute-start(bf16[96,4096]{1,0:T(8,128)(2,1)} %own_ref.1), channel_id=1, source_target_pairs={{0,64},{64,0},{1,65},{65,1},{2,66},{66,2},{3,67},{67,3},{4,68},{68... | collective-permute-start | bytes 2359304 | tf_op jit(solution)/shard_map/ppermute | solution.py:369
  0.7 2.6 %collective-permute-start.1 = (bf16[96]{0:T(256)(128)(2,1)}, bf16[96]{0:T(256)(128)(2,1)S(1)}, u32[]{:S(2)}, u32[]{:S(2)}) collective-permute-start(bf16[96]{0:T(256)(128)(2,1)} %param.6), channel_id=1, source_target_pairs={{0,64},{64,0},{1,65},{65,1},{2,66},{66,2},{3,67},{67,3},{4,68},{68... | collective-permute-start | bytes 584 | tf_op jit(solution)/shard_map/ppermute | solution.py:370
  1.2 2.1 %collective-permute-start.2 = (s32[96]{0:T(128)}, s32[96]{0:T(128)S(1)}, u32[]{:S(2)}, u32[]{:S(2)}) collective-permute-start(s32[96]{0:T(128)} %param.7), channel_id=1, source_target_pairs={{0,64},{64,0},{1,65},{65,1},{2,66},{66,2},{3,67},{67,3},{4,68},{68... | collective-permute-start | bytes 1160 | tf_op jit(solution)/shard_map/ppermute | solution.py:371
  1.3 1.2 %copy-start = (bf16[100,4096]{1,0:T(8,128)(2,1)S(1)}, bf16[100,4096]{1,0:T(8,128)(2,1)}, u32[]{:S(2)}) copy-start(bf16[100,4096]{1,0:T(8,128)(2,1)} %cls_hbm.1) | copy-start | bytes 2457604
  2.5 1.1 %copy-start.2 = (bf16[96,4096]{1,0:T(8,128)(2,1)S(1)}, bf16[96,4096]{1,0:T(8,128)(2,1)}, u32[]{:S(2)}) copy-start(bf16[96,4096]{1,0:T(8,128)(2,1)} %own_ref.1) | copy-start | bytes 2359300
  2.5 1.1 %copy-start.3 = (s32[2,20]{1,0:T(2,128)S(1)}, s32[2,20]{1,0:T(2,128)}, u32[]{:S(2)}) copy-start(s32[2,20]{1,0:T(2,128)} %blocks_ref.1) | copy-start | bytes 484
  2.5 1.1 %copy-start.4 = (bf16[96]{0:T(256)(128)(2,1)S(1)}, bf16[96]{0:T(256)(128)(2,1)}, u32[]{:S(2)}) copy-start(bf16[96]{0:T(256)(128)(2,1)} %param.6) | copy-start | bytes 580
  2.5 1.1 %copy-start.5 = (s32[96]{0:T(128)S(1)}, s32[96]{0:T(128)}, u32[]{:S(2)}) copy-start(s32[96]{0:T(128)} %param.7) | copy-start | bytes 1156
  8.3 1.5 %collective-permute-start.3 = (f32[16,256]{1,0:T(8,128)S(1)}, f32[16,256]{1,0:T(8,128)S(1)}, u32[]{:S(2)}, u32[]{:S(2)}) collective-permute-start(f32[16,256]{1,0:T(8,128)S(1)} %get-tuple-element.13.mine), channel_id=1, source_target_pairs={{0,64},{64,0},{1,65},{65,1},{2,66},{66,2},{3,67},{67,3},{4,68},{68... | collective-permute-start | bytes 49160 | tf_op jit(solution)/shard_map/ppermute | solution.py:415
  41.5 21.3 %copy-start.1 = (bf16[100,4096]{1,0:T(8,128)(2,1)S(1)}, bf16[100,4096]{1,0:T(8,128)(2,1)}, u32[]{:S(2)}) copy-start(bf16[100,4096]{1,0:T(8,128)(2,1)} %cls_hbm.1) | copy-start | bytes 2457604

commit v4 on v3

--- a/solution.py
+++ b/solution.py
@@ -23,9 +23,10 @@
 OWN = 96
 CLASSES = 100
 ROWS = 104
+ROWS_16 = 112
 SPLIT = 48
-HALF_ROWS = 56
-TOTAL_ROW = 52
+HALF_ROWS = 52
+QUADS = 13
 COLS = 2 * LANES
 CHUNKS = 64
 BLOCKS = 32
@@ -157,25 +158,7 @@
     return jnp.concatenate([values, jnp.zeros((1, LANES - OWN), values.dtype)], axis=1)
 
 
-def arrange_classes(cls_ref, cp_ref, norm_ref):
-    zeros = jnp.zeros((ROWS - CLASSES, COLS), jnp.float32)
-    norm = jnp.zeros((CLASSES, LANES), jnp.float32)
-    for j in range(RESIDUES):
-        c_re = gather_lanes(cls_ref, 0, j).astype(jnp.float32)
-        c_im = gather_lanes(cls_ref, 1, j).astype(jnp.float32)
-        norm = norm + c_re * c_re + c_im * c_im
-        cosine = jnp.concatenate([jnp.concatenate([c_re, c_im], axis=1), zeros], axis=0)
-        if 0 < j < 18:
-            sign = sign_lanes(j, CLASSES)
-            sine = jnp.concatenate([jnp.concatenate([c_im * sign, -(c_re * sign)], axis=1), zeros], axis=0)
-        else:
-            sine = jnp.zeros((ROWS, COLS), jnp.float32)
-        cp_ref[j] = jnp.concatenate([cosine, sine], axis=0).astype(jnp.bfloat16)
-    norm = jnp.broadcast_to(jnp.sum(norm, axis=1, keepdims=True), (CLASSES, LANES))
-    norm_ref[...] = jnp.concatenate([norm, jnp.zeros((ROWS - CLASSES, LANES), jnp.float32)], axis=0)
-
-
-def score_kernel(blocks_ref, own_ref, other_ref, prec_a, prec_b, offset_a, offset_b, cp_ref, norm_ref, e_ref, xp_ref, stat_ref, ab_ref, base_ref, prior_ref):
+def score_kernel(blocks_ref, own_ref, other_ref, prec_a, prec_b, offset_a, offset_b, cp_ref, norm_ref, e_ref, xp_ref, stat_ref, top_ref, ab_ref, base_ref, prior_ref):
     row = lax.broadcasted_iota(jnp.int32, (ROWS, LANES), 0)
     dom = lax.axis_index("dom")
     precisions = [particle_row(p[...].astype(jnp.float32)) for p in (prec_a, prec_b)]
@@ -199,52 +182,58 @@
             at = j * COLS + part * LANES
             xp_ref[0:OWN, at : at + LANES] = gather_lanes(own_ref, part, j)
             xp_ref[LANES : LANES + OWN, at : at + LANES] = gather_lanes(other_ref, part, j)
+        pair = 0 < j < 18
+        operand = cp_ref[j] if pair else cp_ref[j, :ROWS_16]
         got = lax.dot_general(
-            cp_ref[j], xp_ref[:, j * COLS : (j + 1) * COLS], (((1,), (1,)), ((), ())), preferred_element_type=jnp.float32
+            operand, xp_ref[:, j * COLS : (j + 1) * COLS], (((1,), (1,)), ((), ())), preferred_element_type=jnp.float32
         )
         ab_ref[j] = got[:ROWS]
-        if 0 < j < 18:
-            ab_ref[18 + j] = got[ROWS:]
+        if pair:
+            ab_ref[18 + j] = got[ROWS_16 : ROWS_16 + ROWS]
 
     for half in range(2):
         lanes = slice(half * LANES, (half + 1) * LANES)
         prec = jnp.broadcast_to(precisions[half], (8, LANES))
 
-        def scores(i, peak):
+        def scores(i, carry):
+            peak, mass = carry
             rows = pl.ds(pl.multiple_of(i * 8, 8), 8)
             a = [ab_ref[j, rows, lanes] for j in range(19)]
             b = [None] + [ab_ref[18 + j, rows, lanes] for j in range(1, 18)]
             base = base_ref[rows, lanes]
             correlation = to_rotations(a, b)
+            score = [correlation[r] * prec + (base + prior_ref[r : r + 1, lanes]) for r in range(ROTATIONS)]
+            top = score[0]
+            for r in range(1, ROTATIONS):
+                top = jnp.maximum(top, score[r])
+            total = None
             for r in range(ROTATIONS):
-                score = correlation[r] * prec + (base + prior_ref[r : r + 1, lanes])
-                e_ref[r, rows, lanes] = score
-                peak = jnp.maximum(peak, score)
-            return peak
-
-        peak = lax.fori_loop(0, ROWS // 8, scores, jnp.full((8, LANES), EXCLUDED, jnp.float32), unroll=True)
-        peak = jnp.broadcast_to(jnp.max(peak, axis=0, keepdims=True), (8, LANES))
-
-        def masses(i, mass):
-            rows = pl.ds(pl.multiple_of(i * 8, 8), 8)
-            for r in range(ROTATIONS):
-                e = jnp.exp(e_ref[r, rows, lanes] - peak)
+                e = jnp.exp(score[r] - top)
                 e_ref[r, rows, lanes] = e
-                mass = mass + e
-            return mass
-
-        mass = lax.fori_loop(0, ROWS // 8, masses, jnp.zeros((8, LANES), jnp.float32), unroll=True)
-        stat_ref[0:8, lanes] = peak
-        stat_ref[8:16, lanes] = jnp.broadcast_to(jnp.sum(mass, axis=0, keepdims=True), (8, LANES))
-
-
-def spectrum_kernel(e_ref, w_ref):
+                total = e if total is None else total + e
+            top_ref[rows, lanes] = top
+            higher = jnp.maximum(peak, top)
+            mass = mass * jnp.exp(peak - higher) + total * jnp.exp(top - higher)
+            return higher, mass
+
+        start = (jnp.full((8, LANES), EXCLUDED, jnp.float32), jnp.zeros((8, LANES), jnp.float32))
+        tops, mass = lax.fori_loop(0, ROWS // 8, scores, start, unroll=True)
+        peak = jnp.max(tops, axis=0, keepdims=True)
+        mass = jnp.sum(mass * jnp.exp(tops - peak), axis=0, keepdims=True)
+        stat_ref[0:8, lanes] = jnp.broadcast_to(peak, (8, LANES))
+        stat_ref[8:16, lanes] = jnp.broadcast_to(mass, (8, LANES))
+
+
+def spectrum_kernel(e_ref, top_ref, stat_ref, w_ref):
     for half in range(2):
         lanes = slice(half * LANES, (half + 1) * LANES)
 
+        peak = stat_ref[0:8, lanes]
+
         def spectra(i, carry):
             rows = pl.ds(pl.multiple_of(i * 8, 8), 8)
-            c, s = from_rotations([e_ref[r, rows, lanes] for r in range(ROTATIONS)])
+            lift = jnp.exp(top_ref[rows, lanes] - peak)
+            c, s = from_rotations([e_ref[r, rows, lanes] * lift for r in range(ROTATIONS)])
             for j in range(19):
                 w_ref[j, rows, lanes] = c[j]
             for j in range(1, 18):
@@ -255,7 +244,22 @@
 
 
 def class_kernel(cls_ref, cp_ref, norm_ref):
-    arrange_classes(cls_ref, cp_ref, norm_ref)
+    pad = jnp.zeros((ROWS_16 - CLASSES, LANES), jnp.bfloat16)
+    for j in range(RESIDUES):
+        c_re = jnp.concatenate([gather_lanes(cls_ref, 0, j), pad], axis=0)
+        c_im = jnp.concatenate([gather_lanes(cls_ref, 1, j), pad], axis=0)
+        cp_ref[j, :ROWS_16, :LANES] = c_re
+        cp_ref[j, :ROWS_16, LANES:] = c_im
+        if 0 < j < 18:
+            sign = sign_lanes(j, ROWS_16).astype(jnp.bfloat16)
+            cp_ref[j, ROWS_16:, :LANES] = c_im * sign
+            cp_ref[j, ROWS_16:, LANES:] = -(c_re * sign)
+    norm = jnp.zeros((CLASSES, LANES), jnp.float32)
+    for block in range(BLOCKS):
+        member = cls_ref[:, block * LANES : (block + 1) * LANES].astype(jnp.float32)
+        norm = norm + member * member
+    norm = jnp.broadcast_to(jnp.sum(norm, axis=1, keepdims=True), (CLASSES, LANES))
+    norm_ref[...] = jnp.concatenate([norm, jnp.zeros((ROWS - CLASSES, LANES), jnp.float32)], axis=0)
 
 
 def sums_kernel(w_ref, xp_ref, mine, theirs, out_ref, evidence_ref, pc_ref):
@@ -320,7 +324,9 @@
         whole = jnp.concatenate([pc_ref[:, at : at + CYCLES] for at in starts], axis=1)
         for half in range(2):
             rows = whole[half * SPLIT : half * SPLIT + HALF_ROWS]
-            out_ref[half * BLOCKS + block] = jnp.where(row == TOTAL_ROW, total * SUM_SCALE, rows)
+            if half == 0:
+                rows = jnp.where(row == SPLIT, total * SUM_SCALE, rows)
+            out_ref[half * BLOCKS + block] = rows.reshape(QUADS, 4, LANES)
 
 
 FINISH_STEPS = 4
@@ -333,8 +339,8 @@
     row = lax.broadcasted_iota(jnp.int32, (HALF_ROWS, LANES), 0)
     lane = lax.broadcasted_iota(jnp.int32, (HALF_ROWS, LANES), 1)
     share = []
+    total = sum_ref[0, 0, SPLIT // 4, 0:1, :]
     for half in range(2):
-        total = sum_ref[half, 0, TOTAL_ROW : TOTAL_ROW + 1, :]
         weight = jnp.sum(jnp.where(lane == row + half * SPLIT, total, 0.0), axis=1, keepdims=True)
         share.append(1.0 / (weight * (1.0 / SUM_SCALE) + CLASS_PRIOR))
     fetch.wait()
@@ -346,7 +352,7 @@
             for half in range(2):
                 count = SPLIT if half == 0 else CLASSES - SPLIT
                 rows = slice(half * SPLIT, half * SPLIT + count)
-                new = sum_ref[half, block, 0:count] * (1.0 / SUM_SCALE) + CLASS_PRIOR * old[rows]
+                new = sum_ref[half, block].reshape(HALF_ROWS, LANES)[:count] * (1.0 / SUM_SCALE) + CLASS_PRIOR * old[rows]
                 out_ref[rows, lanes] = new * share[half][:count]
         lanes = slice(step * STEP_BLOCKS * LANES, (step + 1) * STEP_BLOCKS * LANES)
         copy = pltpu.make_async_copy(out_ref.at[:, lanes], out_hbm.at[:, lanes], out_sems.at[step])
@@ -374,7 +380,7 @@
     cp, norm = pl.pallas_call(
         class_kernel,
         out_shape=(
-            jax.ShapeDtypeStruct((RESIDUES, 2 * ROWS, COLS), jnp.bfloat16),
+            jax.ShapeDtypeStruct((RESIDUES, 2 * ROWS_16, COLS), jnp.bfloat16),
             jax.ShapeDtypeStruct((ROWS, LANES), jnp.float32),
         ),
         in_specs=[VMEM],
@@ -384,15 +390,16 @@
         name="classes",
     )(classes)
 
-    e, by_residue, mine = pl.pallas_call(
+    e, by_residue, mine, tops = pl.pallas_call(
         score_kernel,
         out_shape=(
             jax.ShapeDtypeStruct((36, ROWS, COLS), jnp.float32),
             jax.ShapeDtypeStruct((COLS, RESIDUES * COLS), jnp.bfloat16),
             jax.ShapeDtypeStruct((16, COLS), jnp.float32),
+            jax.ShapeDtypeStruct((ROWS, COLS), jnp.float32),
         ),
         in_specs=[SMEM] + [VMEM] * 8,
-        out_specs=(VMEM,) * 3,
+        out_specs=(VMEM,) * 4,
         scratch_shapes=[
             pltpu.VMEM((36, ROWS, COLS), jnp.float32),
             pltpu.VMEM((ROWS, COLS), jnp.float32),
@@ -417,17 +424,17 @@
     weights = pl.pallas_call(
         spectrum_kernel,
         out_shape=jax.ShapeDtypeStruct((36, ROWS, COLS), jnp.float32),
-        in_specs=[VMEM],
+        in_specs=[VMEM] * 3,
         out_specs=VMEM,
         compiler_params=pltpu.CompilerParams(vmem_limit_bytes=16 * MIB),
         cost_estimate=cost,
         name="spectra",
-    )(e)
+    )(e, tops, mine)
 
     parts, evidence = pl.pallas_call(
         sums_kernel,
         out_shape=(
-            jax.ShapeDtypeStruct((CHUNKS, HALF_ROWS, LANES), jnp.float32),
+            jax.ShapeDtypeStruct((CHUNKS, QUADS, 4, LANES), jnp.float32),
             jax.ShapeDtypeStruct((1, OWN), jnp.float32),
         ),
         in_specs=[VMEM] * 4,
@@ -439,7 +446,7 @@
 
     got = lax.all_to_all(parts.astype(jnp.float16), "cls", 0, 0, tiled=True)
     total = jnp.sum(got.astype(jnp.float32), axis=0).astype(jnp.float16)
-    repeated = jnp.broadcast_to(total[None], (CHUNKS, HALF_ROWS, LANES))
+    repeated = jnp.broadcast_to(total[None], (CHUNKS, QUADS, 4, LANES))
     whole = lax.all_to_all(repeated, "cls", 0, 0, tiled=True)
     new_classes = pl.pallas_call(
         finish_kernel,
@@ -454,7 +461,7 @@
         ],
         compiler_params=pltpu.CompilerParams(vmem_limit_bytes=12 * MIB),
         name="finish",
-    )(whole.astype(jnp.float32).reshape(2, BLOCKS, HALF_ROWS, LANES), classes)
+    )(whole.astype(jnp.float32).reshape(2, BLOCKS, QUADS, 4, LANES), classes)
     return new_classes, evidence.reshape(OWN)
 
 

time: 64.7 us -> 63.5 us (0.981)
  blocking collectives: 50.4 us -> 48.7 us
    all_to_all x1, blocking collectives: 21.2 us -> 20.3 us  [shards(): whole = lax.all_to_all(repeated, 'cls', 0, 0, tiled=True)]
    all_to_all x1, blocking collectives: 29.2 us -> 28.4 us  [shards(): got = lax.all_to_all(parts.astype(jnp.float16), 'cls', 0, 0, tiled=True)]
where the time goes in v4:
time: 63.5 us; the launch traced here: 63.3 us
  blocking collectives  48.7 us (77%)
  Pallas kernels  10.1 us (16%)
  local copies, waits for them, and re-layouts  1.58 us (2%)
  starting transfers between devices  1.17 us (2%)
  other arithmetic  0.96 us (2%)
  between operations  0.72 us (1%)
    all_to_all x1, blocking collectives, shards(): got = lax.all_to_all(parts.astype(jnp.float16), 'cls', 0, 0, tiled=True)  28.4 us
    all_to_all x1, blocking collectives, shards(): whole = lax.all_to_all(repeated, 'cls', 0, 0, tiled=True)  20.3 us
    pallas_call x1, Pallas kernels, shards(): pl.pallas_call(score_kernel, out_shape=(jax.ShapeDtypeStruct((36, ROWS, C...  4.22 us
    pallas_call x1, Pallas kernels, shards(): pl.pallas_call(sums_kernel, out_shape=(jax.ShapeDtypeStruct((CHUNKS, QUAD...  2.2 us
    pallas_call x1, Pallas kernels, shards(): pl.pallas_call(finish_kernel, out_shape=jax.ShapeDtypeStruct((CLASSES, BL...  1.6 us
    unnamed x12, local copies, waits for them, and re-layouts  1.35 us
  transfers between devices with their start and end apart: 4, of which 0 were waited for; matrix products, arithmetic and copies ran while one was open for 0% of the time, Pallas kernels for 3%

profile of v4, /device:TPU:0, one launch (start us, length us, event | category | flops | bytes accessed | tf_op | source)
XLA Modules:
  0.0 63.3 jit_solution(2023979021637290862)
XLA Ops:
  0.6 0.1 collective-permute-start
  0.7 0.5 collective-permute-start.1
  1.2 0.1 collective-permute-start.2
  1.3 1.2 %copy-done = bf16[100,4096]{1,0:T(8,128)(2,1)S(1)} copy-done((bf16[100,4096]{1,0:T(8,128)(2,1)S(1)}, bf16[100,4096]{1,0:T(8,128)(2,1)}, u32[]{:S(2)}) %copy-start) | copy-done | bytes 819224
  2.5 0.9 %classes.1 = (bf16[19,224,256]{2,1,0:T(8,128)(2,1)S(1)}, f32[104,128]{1,0:T(8,128)S(1)}) custom-call(bf16[100,4096]{1,0:T(8,128)(2,1)S(1)} %copy-done), custom_call_target="tpu_custom_call" | custom-call | flops 4000000000 | bytes 8388608 | tf_op jit(solution)/shard_map/classes/pallas_call | solution.py:380
  3.4 0.0 collective-permute-done.1
  3.4 0.0 collective-permute-done.2
  3.4 0.0 collective-permute-done.other_ref
  3.4 0.2 copy-done.2
  3.6 0.0 copy-done.3
  3.6 4.2 %scores.1 = (f32[36,104,256]{2,1,0:T(8,128)S(1)}, bf16[256,4864]{1,0:T(8,128)(2,1)S(1)}, f32[16,256]{1,0:T(8,128)S(1)}, f32[104,256]{1,0:T(8,128)S(1)}) custom-call(s32[2,20]{1,0:T(2,128)S(1)} %copy-done.3, bf16[96,4096]{1,0:T(8,128)(2,1)S(1)} %copy-done.2, bf16[96,4096]{1,0:T(8,128)(2,1)S(1)} %collective-permute-done.other_ref, bf16[1,96]{1,0:T(2,128)(2,1)S(1)} %bitcast.7, ...), custom_call_target="tpu_custom_call" | custom-call | flops 4000000000 | bytes 8388608 | tf_op jit(solution)/shard_map/scores/pallas_call | solution.py:393
  7.8 0.5 collective-permute-start.3
  8.3 1.2 %spectra.1.w_ref = f32[36,104,256]{2,1,0:T(8,128)S(1)} custom-call(f32[36,104,256]{2,1,0:T(8,128)S(1)} %get-tuple-element.12.e_ref, f32[104,256]{1,0:T(8,128)S(1)} %get-tuple-element.13.top_ref, f32[16,256]{1,0:T(8,128)S(1)} %get-tuple-element.14.stat_ref.mine), custom_call_target="tpu_custom_call" | custom-call | flops 4000000000 | bytes 8388608 | tf_op jit(solution)/shard_map/spectra/pallas_call | solution.py:424
  9.5 0.0 collective-permute-done.3.theirs
  9.5 2.2 %sums.1 = (f32[64,13,4,128]{3,2,1,0:T(4,128)S(1)}, f32[1,96]{1,0:T(1,128)}) custom-call(f32[36,104,256]{2,1,0:T(8,128)S(1)} %spectra.1.w_ref, bf16[256,4864]{1,0:T(8,128)(2,1)S(1)} %get-tuple-element.15.xp_ref, f32[16,256]{1,0:T(8,128)S(1)} %get-tuple-element.14.stat_ref.mine, f32[16,256]{1,0:T(8,128)S(1)} %collective-permute-done.3.theirs), custom_call_target="tpu_custom_call" | custom-call | tf_op jit(solution)/shard_map/sums/pallas_call | solution.py:434
  11.7 0.3 convert_element_type.14
  12.0 28.4 %all_to_all.10 = f16[64,13,4,128]{3,2,1,0:T(4,128)(2,1)S(1)} all-to-all(f16[64,13,4,128]{3,2,1,0:T(4,128)(2,1)S(1)} %convert_element_type.14), channel_id=1, replica_groups=mesh['dom'=2,'cls'=64] {'cls'}, dimensions={0} | all-to-all | bytes 1703936 | tf_op jit(solution)/shard_map/all_to_all | solution.py:447
  40.4 0.4 convert_reduce_fusion
  40.8 0.2 broadcast_in_dim.2
  41.0 0.0 copy-start.1
  41.0 20.3 %all_to_all.11 = f16[64,13,4,128]{3,2,1,0:T(4,128)(2,1)S(1)} all-to-all(f16[64,13,4,128]{3,2,1,0:T(4,128)(2,1)S(1)} %broadcast_in_dim.2), channel_id=1, replica_groups=mesh['dom'=2,'cls'=64] {'cls'}, dimensions={0} | all-to-all | bytes 1703936 | tf_op jit(solution)/shard_map/all_to_all | solution.py:450
  61.4 0.3 convert.1.sum_ref
  61.6 0.0 copy-done.1
  61.7 1.6 %finish.1 = f32[100,4096]{1,0:T(8,128)} custom-call(f32[2,32,13,4,128]{4,3,2,1,0:T(4,128)S(1)} %convert.1.sum_ref, bf16[100,4096]{1,0:T(8,128)(2,1)S(1)} %copy-done.1), custom_call_target="tpu_custom_call" | custom-call | tf_op jit(solution)/shard_map/finish/pallas_call | solution.py:451
  (8 shorter events, 0.0 us)
Async XLA Ops:
  0.6 2.8 %collective-permute-start = (bf16[96,4096]{1,0:T(8,128)(2,1)}, bf16[96,4096]{1,0:T(8,128)(2,1)S(1)}, u32[]{:S(2)}, u32[]{:S(2)}) collective-permute-start(bf16[96,4096]{1,0:T(8,128)(2,1)} %own_ref.1), channel_id=1, source_target_pairs={{0,64},{64,0},{1,65},{65,1},{2,66},{66,2},{3,67},{67,3},{4,68},{68... | collective-permute-start | bytes 2359304 | tf_op jit(solution)/shard_map/ppermute | solution.py:375
  0.7 2.7 %collective-permute-start.1 = (bf16[96]{0:T(256)(128)(2,1)}, bf16[96]{0:T(256)(128)(2,1)S(1)}, u32[]{:S(2)}, u32[]{:S(2)}) collective-permute-start(bf16[96]{0:T(256)(128)(2,1)} %param.6), channel_id=1, source_target_pairs={{0,64},{64,0},{1,65},{65,1},{2,66},{66,2},{3,67},{67,3},{4,68},{68... | collective-permute-start | bytes 584 | tf_op jit(solution)/shard_map/ppermute | solution.py:376
  1.2 2.2 %collective-permute-start.2 = (s32[96]{0:T(128)}, s32[96]{0:T(128)S(1)}, u32[]{:S(2)}, u32[]{:S(2)}) collective-permute-start(s32[96]{0:T(128)} %param.7), channel_id=1, source_target_pairs={{0,64},{64,0},{1,65},{65,1},{2,66},{66,2},{3,67},{67,3},{4,68},{68... | collective-permute-start | bytes 1160 | tf_op jit(solution)/shard_map/ppermute | solution.py:377
  1.3 1.2 %copy-start = (bf16[100,4096]{1,0:T(8,128)(2,1)S(1)}, bf16[100,4096]{1,0:T(8,128)(2,1)}, u32[]{:S(2)}) copy-start(bf16[100,4096]{1,0:T(8,128)(2,1)} %cls_hbm.1) | copy-start | bytes 2457604
  2.5 1.1 %copy-start.2 = (bf16[96,4096]{1,0:T(8,128)(2,1)S(1)}, bf16[96,4096]{1,0:T(8,128)(2,1)}, u32[]{:S(2)}) copy-start(bf16[96,4096]{1,0:T(8,128)(2,1)} %own_ref.1) | copy-start | bytes 2359300
  2.5 1.1 %copy-start.3 = (s32[2,20]{1,0:T(2,128)S(1)}, s32[2,20]{1,0:T(2,128)}, u32[]{:S(2)}) copy-start(s32[2,20]{1,0:T(2,128)} %blocks_ref.1) | copy-start | bytes 484
  2.5 1.1 %copy-start.4 = (bf16[96]{0:T(256)(128)(2,1)S(1)}, bf16[96]{0:T(256)(128)(2,1)}, u32[]{:S(2)}) copy-start(bf16[96]{0:T(256)(128)(2,1)} %param.6) | copy-start | bytes 580
  2.5 1.1 %copy-start.5 = (s32[96]{0:T(128)S(1)}, s32[96]{0:T(128)}, u32[]{:S(2)}) copy-start(s32[96]{0:T(128)} %param.7) | copy-start | bytes 1156
  7.8 1.7 %collective-permute-start.3 = (f32[16,256]{1,0:T(8,128)S(1)}, f32[16,256]{1,0:T(8,128)S(1)}, u32[]{:S(2)}, u32[]{:S(2)}) collective-permute-start(f32[16,256]{1,0:T(8,128)S(1)} %get-tuple-element.14.stat_ref.mine), channel_id=1, source_target_pairs={{0,64},{64,0},{1,65},{65,1},{2,66},{66,2},{3,67},{67,3},{4,68},{68... | collective-permute-start | bytes 49160 | tf_op jit(solution)/shard_map/ppermute | solution.py:422
  41.0 20.6 %copy-start.1 = (bf16[100,4096]{1,0:T(8,128)(2,1)S(1)}, bf16[100,4096]{1,0:T(8,128)(2,1)}, u32[]{:S(2)}) copy-start(bf16[100,4096]{1,0:T(8,128)(2,1)} %cls_hbm.1) | copy-start | bytes 2457604

commit v5 on v4

--- a/solution.py
+++ b/solution.py
@@ -32,11 +32,50 @@
 BLOCKS = 32
 SUM_SCALE = 0.25
 
-MEMBERS = []
+SLOTS = [
+    (0, 3), (1, 0, 3), (2, 1, 0), (3, 2, 1), (1, 3, 0), (1, 0, 3), (3, 1, 2), (0, 3, 1), (1, 3, 0), (2, 1, 0, 3),
+    (3, 1, 0, 2), (0, 3, 2, 1), (3, 1, 2, 0), (0, 1, 2, 3), (1, 3, 2, 0), (2, 3, 0, 1), (1, 0, 3, 2), (2, 1, 0, 3), (3, 2),
+]
+PLACE = {}
 for _j in range(RESIDUES):
     _same = [(m, 1) for m in range(FREQUENCIES) if m % ROTATIONS == _j]
     _back = [(m, -1) for m in range(FREQUENCIES) if m % ROTATIONS == (ROTATIONS - _j) % ROTATIONS and _j not in (0, 18)]
-    MEMBERS.append(_same + _back)
+    for (_m, _sign), _slot in zip(_same + _back, SLOTS[_j], strict=True):
+        PLACE[_m] = (_j, _slot, _sign)
+
+
+def quarter_of(rows):
+    return lax.broadcasted_iota(jnp.int32, (rows, LANES), 1) // CYCLES
+
+
+class Rotated:
+    def __init__(self, tile):
+        self.tile, self.done = tile, {}
+
+    def __call__(self, at, quarters):
+        key = (at, quarters % GROUP)
+        if key not in self.done:
+            value = self(at, 0) if key[1] else self.tile(at)
+            self.done[key] = pltpu.roll(value, key[1] * CYCLES, 1) if key[1] else value
+        return self.done[key]
+
+
+def by_quarter(pieces, quarter):
+    whole = None
+    for at, piece in pieces.items():
+        if whole is None:
+            whole = piece if len(pieces) == GROUP else jnp.where(quarter == at, piece, jnp.zeros_like(piece))
+        else:
+            whole = jnp.where(quarter == at, piece, whole)
+    return whole
+
+
+def to_residues(tile, rows):
+    quarter = quarter_of(rows)
+    rotated = Rotated(tile)
+    for j in range(RESIDUES):
+        pieces = {q: rotated(m // GROUP, q - m) for m, (i, q, _) in PLACE.items() if i == j}
+        yield j, by_quarter(pieces, quarter)
 
 
 def cosine(k):
@@ -140,18 +179,13 @@
     return c, s
 
 
-def gather_lanes(ref, part, j):
-    rows = ref.shape[0]
-    pieces = [ref[:, part * PART + m * CYCLES : part * PART + (m + 1) * CYCLES] for m, _ in MEMBERS[j]]
-    if len(pieces) < GROUP:
-        pieces.append(jnp.zeros((rows, (GROUP - len(pieces)) * CYCLES), ref.dtype))
-    return jnp.concatenate(pieces, axis=1)
-
-
 def sign_lanes(j, rows):
-    lane = lax.broadcasted_iota(jnp.int32, (rows, LANES), 1)
-    same = sum(1 for _, s in MEMBERS[j] if s > 0) * CYCLES
-    return jnp.where(lane < same, 1.0, -1.0)
+    quarter = quarter_of(rows)
+    sign = jnp.ones((rows, LANES), jnp.float32)
+    for i, q, direction in PLACE.values():
+        if i == j and direction < 0:
+            sign = jnp.where(quarter == q, -1.0, sign)
+    return sign
 
 
 def particle_row(values):
@@ -159,17 +193,18 @@
 
 
 def score_kernel(blocks_ref, own_ref, other_ref, prec_a, prec_b, offset_a, offset_b, cp_ref, norm_ref, e_ref, xp_ref, stat_ref, top_ref, ab_ref, base_ref, prior_ref):
-    row = lax.broadcasted_iota(jnp.int32, (ROWS, LANES), 0)
-    dom = lax.axis_index("dom")
+    blocks = CLASSES // CLASS_BLOCK
+    first = lax.broadcasted_iota(jnp.int32, (ROWS, blocks), 1) * CLASS_BLOCK
+    row = lax.broadcasted_iota(jnp.int32, (ROWS, blocks), 0)
+    inside = (row >= first) & (row < first + CLASS_BLOCK)
+    swapped = lax.axis_index("dom") == 1
+    allowed = [blocks_ref[0:1], blocks_ref[1:2]]
     precisions = [particle_row(p[...].astype(jnp.float32)) for p in (prec_a, prec_b)]
     for half in range(2):
         lanes = slice(half * LANES, (half + 1) * LANES)
-        block_row = dom if half == 0 else 1 - dom
-        admit = jnp.zeros((ROWS, LANES), jnp.int32)
-        for block in range(CLASSES // CLASS_BLOCK):
-            inside = (row >= block * CLASS_BLOCK) & (row < (block + 1) * CLASS_BLOCK)
-            admit = jnp.where(inside, blocks_ref[block_row, block], admit)
-        base_ref[:, lanes] = jnp.where(admit == 1, -0.5 * norm_ref[...] * precisions[half], EXCLUDED)
+        admit = jnp.where(swapped, allowed[1 - half], allowed[half]) == 1
+        admit = jnp.sum(jnp.where(inside & admit, 1.0, 0.0), axis=1, keepdims=True)
+        base_ref[:, lanes] = jnp.where(admit > 0.0, -0.5 * norm_ref[...] * precisions[half], EXCLUDED)
         offset = particle_row((offset_a, offset_b)[half][...])
         steps = lax.rem(lax.broadcasted_iota(jnp.int32, (40, LANES), 0) - offset + ROTATIONS, ROTATIONS)
         distance = jnp.minimum(steps, ROTATIONS - steps).astype(jnp.float32) * (1.0 / PRIOR_WIDTH)
@@ -177,11 +212,14 @@
     zeros = jnp.zeros((LANES - OWN, RESIDUES * COLS), jnp.bfloat16)
     xp_ref[OWN:LANES] = zeros
     xp_ref[LANES + OWN :] = zeros
+    for first_row, ref in ((0, own_ref), (LANES, other_ref)):
+        for part in range(2):
+            for i in range(0, OWN, 16):
+                tiles = lambda t: ref[i : i + 16, part * PART + t * LANES : part * PART + (t + 1) * LANES]
+                for j, value in to_residues(tiles, 16):
+                    at = j * COLS + part * LANES
+                    xp_ref[first_row + i : first_row + i + 16, at : at + LANES] = value
     for j in range(RESIDUES):
-        for part in range(2):
-            at = j * COLS + part * LANES
-            xp_ref[0:OWN, at : at + LANES] = gather_lanes(own_ref, part, j)
-            xp_ref[LANES : LANES + OWN, at : at + LANES] = gather_lanes(other_ref, part, j)
         pair = 0 < j < 18
         operand = cp_ref[j] if pair else cp_ref[j, :ROWS_16]
         got = lax.dot_general(
@@ -245,15 +283,14 @@
 
 def class_kernel(cls_ref, cp_ref, norm_ref):
     pad = jnp.zeros((ROWS_16 - CLASSES, LANES), jnp.bfloat16)
-    for j in range(RESIDUES):
-        c_re = jnp.concatenate([gather_lanes(cls_ref, 0, j), pad], axis=0)
-        c_im = jnp.concatenate([gather_lanes(cls_ref, 1, j), pad], axis=0)
-        cp_ref[j, :ROWS_16, :LANES] = c_re
-        cp_ref[j, :ROWS_16, LANES:] = c_im
-        if 0 < j < 18:
-            sign = sign_lanes(j, ROWS_16).astype(jnp.bfloat16)
-            cp_ref[j, ROWS_16:, :LANES] = c_im * sign
-            cp_ref[j, ROWS_16:, LANES:] = -(c_re * sign)
+    for part in range(2):
+        tiles = lambda t: cls_ref[:, part * PART + t * LANES : part * PART + (t + 1) * LANES]
+        for j, value in to_residues(tiles, CLASSES):
+            value = jnp.concatenate([value, pad], axis=0)
+            cp_ref[j, :ROWS_16, part * LANES : (part + 1) * LANES] = value
+            if 0 < j < 18:
+                sign = sign_lanes(j, ROWS_16) * (1.0 if part else -1.0)
+                cp_ref[j, ROWS_16:, (1 - part) * LANES : (2 - part) * LANES] = value * sign.astype(jnp.bfloat16)
     norm = jnp.zeros((CLASSES, LANES), jnp.float32)
     for block in range(BLOCKS):
         member = cls_ref[:, block * LANES : (block + 1) * LANES].astype(jnp.float32)
@@ -262,22 +299,23 @@
     norm_ref[...] = jnp.concatenate([norm, jnp.zeros((ROWS - CLASSES, LANES), jnp.float32)], axis=0)
 
 
-def sums_kernel(w_ref, xp_ref, mine, theirs, out_ref, evidence_ref, pc_ref):
+def settle(mine, theirs, half):
+    here = slice(half * LANES, (half + 1) * LANES)
+    there = slice((1 - half) * LANES, (2 - half) * LANES)
+    peak = jnp.maximum(mine[0:1, here], theirs[0:1, there])
+    mass = mine[8:9, here] * jnp.exp(mine[0:1, here] - peak)
+    mass = mass + theirs[8:9, there] * jnp.exp(theirs[0:1, there] - peak)
     held = lax.broadcasted_iota(jnp.int32, (1, LANES), 1) < OWN
-
-    def settle(half):
-        here = slice(half * LANES, (half + 1) * LANES)
-        there = slice((1 - half) * LANES, (2 - half) * LANES)
-        peak = jnp.maximum(mine[0:1, here], theirs[0:1, there])
-        lift = jnp.exp(mine[0:1, here] - peak)
-        mass = mine[8:9, here] * lift + theirs[8:9, there] * jnp.exp(theirs[0:1, there] - peak)
-        mass = jnp.where(held, mass, 1.0)
-        return jnp.where(held, lift / mass, 0.0), peak + jnp.log(mass)
-
-    scale_a, evidence = settle(0)
-    scale_b, _ = settle(1)
-    scale = jnp.concatenate([scale_a, scale_b], axis=1)
-    evidence_ref[...] = evidence[:, :OWN]
+    return held, peak, jnp.where(held, mass, 1.0)
+
+
+def sums_kernel(w_ref, xp_ref, mine, theirs, out_ref, pc_ref):
+    scale = []
+    for half in range(2):
+        held, peak, mass = settle(mine, theirs, half)
+        lift = jnp.exp(mine[0:1, half * LANES : (half + 1) * LANES] - peak)
+        scale.append(jnp.where(held, lift * SUM_SCALE / mass, 0.0))
+    scale = jnp.concatenate(scale, axis=1)
 
     def weights_of(i):
         return w_ref[i] * scale
@@ -310,32 +348,36 @@
         if pair:
             sign = sign_lanes(j, ROWS)
             re, im = re - sign * got[ROWS:, LANES:], im + sign * got[ROWS:, :LANES]
-        pc_ref[:, j * COLS : j * COLS + LANES] = re * SUM_SCALE
-        pc_ref[:, j * COLS + LANES : (j + 1) * COLS] = im * SUM_SCALE
-
-    place = {}
-    for j in range(RESIDUES):
-        for at, (m, _) in enumerate(MEMBERS[j]):
-            place[m] = j * COLS + at * CYCLES
-    row = lax.broadcasted_iota(jnp.int32, (HALF_ROWS, LANES), 0)
-    for block in range(BLOCKS):
-        part, first = divmod(block, BLOCKS // 2)
-        starts = [place[first * GROUP + q] + part * LANES for q in range(GROUP)]
-        whole = jnp.concatenate([pc_ref[:, at : at + CYCLES] for at in starts], axis=1)
-        for half in range(2):
-            rows = whole[half * SPLIT : half * SPLIT + HALF_ROWS]
-            if half == 0:
-                rows = jnp.where(row == SPLIT, total * SUM_SCALE, rows)
-            out_ref[half * BLOCKS + block] = rows.reshape(QUADS, 4, LANES)
+        pc_ref[:, j * COLS : j * COLS + LANES] = re
+        pc_ref[:, j * COLS + LANES : (j + 1) * COLS] = im
+
+    quarter = quarter_of(8)
+    last = jnp.broadcast_to(total, (4, LANES))
+    for part in range(2):
+        for i in range(ROWS // 8):
+            rotated = Rotated(lambda j: pc_ref[i * 8 : (i + 1) * 8, j * COLS + part * LANES : j * COLS + (part + 1) * LANES])
+            for t in range(BLOCKS // 2):
+                pieces = {m % GROUP: rotated(PLACE[m][0], m - PLACE[m][1]) for m in range(t * GROUP, (t + 1) * GROUP)}
+                value = by_quarter(pieces, quarter)
+                half, at = divmod(i, SPLIT // 8) if i < ROWS // 8 - 1 else (1, i - SPLIT // 8)
+                block = half * BLOCKS + part * (BLOCKS // 2) + t
+                if i == ROWS // 8 - 1:
+                    out_ref[block, QUADS - 1] = value[:4]
+                else:
+                    out_ref[block, 2 * at : 2 * at + 2] = value.reshape(2, 4, LANES)
+                if half == 0 and at == 0:
+                    out_ref[block, QUADS - 1] = last
 
 
 FINISH_STEPS = 4
 STEP_BLOCKS = BLOCKS // FINISH_STEPS
 
 
-def finish_kernel(sum_ref, cls_hbm, out_hbm, cls_ref, out_ref, cls_sem, out_sems):
-    fetch = pltpu.make_async_copy(cls_hbm, cls_ref, cls_sem)
-    fetch.start()
+def finish_kernel(sum_ref, cls_ref, mine, theirs, out_hbm, evidence_hbm, out_ref, evidence_ref, out_sems, evidence_sem):
+    _, peak, mass = settle(mine, theirs, 0)
+    evidence_ref[...] = (peak + jnp.log(mass))[:, :OWN]
+    send = pltpu.make_async_copy(evidence_ref, evidence_hbm, evidence_sem)
+    send.start()
     row = lax.broadcasted_iota(jnp.int32, (HALF_ROWS, LANES), 0)
     lane = lax.broadcasted_iota(jnp.int32, (HALF_ROWS, LANES), 1)
     share = []
@@ -343,7 +385,6 @@
     for half in range(2):
         weight = jnp.sum(jnp.where(lane == row + half * SPLIT, total, 0.0), axis=1, keepdims=True)
         share.append(1.0 / (weight * (1.0 / SUM_SCALE) + CLASS_PRIOR))
-    fetch.wait()
     copies = []
     for step in range(FINISH_STEPS):
         for block in range(step * STEP_BLOCKS, (step + 1) * STEP_BLOCKS):
@@ -360,10 +401,10 @@
         copies.append(copy)
     for copy in copies:
         copy.wait()
+    send.wait()
 
 
 VMEM = pl.BlockSpec(memory_space=pltpu.VMEM)
-SMEM = pl.BlockSpec(memory_space=pltpu.SMEM)
 
 
 ANY = pl.BlockSpec(memory_space=pl.ANY)
@@ -398,7 +439,7 @@
             jax.ShapeDtypeStruct((16, COLS), jnp.float32),
             jax.ShapeDtypeStruct((ROWS, COLS), jnp.float32),
         ),
-        in_specs=[SMEM] + [VMEM] * 8,
+        in_specs=[VMEM] * 9,
         out_specs=(VMEM,) * 4,
         scratch_shapes=[
             pltpu.VMEM((36, ROWS, COLS), jnp.float32),
@@ -431,14 +472,11 @@
         name="spectra",
     )(e, tops, mine)
 
-    parts, evidence = pl.pallas_call(
+    parts = pl.pallas_call(
         sums_kernel,
-        out_shape=(
-            jax.ShapeDtypeStruct((CHUNKS, QUADS, 4, LANES), jnp.float32),
-            jax.ShapeDtypeStruct((1, OWN), jnp.float32),
-        ),
+        out_shape=jax.ShapeDtypeStruct((CHUNKS, QUADS, 4, LANES), jnp.float32),
         in_specs=[VMEM] * 4,
-        out_specs=(VMEM, VMEM),
+        out_specs=VMEM,
         scratch_shapes=[pltpu.VMEM((ROWS, RESIDUES * COLS), jnp.float32)],
         compiler_params=pltpu.CompilerParams(vmem_limit_bytes=20 * MIB),
         name="sums",
@@ -448,20 +486,23 @@
     total = jnp.sum(got.astype(jnp.float32), axis=0).astype(jnp.float16)
     repeated = jnp.broadcast_to(total[None], (CHUNKS, QUADS, 4, LANES))
     whole = lax.all_to_all(repeated, "cls", 0, 0, tiled=True)
-    new_classes = pl.pallas_call(
+    new_classes, evidence = pl.pallas_call(
         finish_kernel,
-        out_shape=jax.ShapeDtypeStruct((CLASSES, BLOCKS * LANES), jnp.float32),
-        in_specs=[VMEM, ANY],
-        out_specs=ANY,
+        out_shape=(
+            jax.ShapeDtypeStruct((CLASSES, BLOCKS * LANES), jnp.float32),
+            jax.ShapeDtypeStruct((1, OWN), jnp.float32),
+        ),
+        in_specs=[VMEM] * 4,
+        out_specs=(ANY, ANY),
         scratch_shapes=[
-            pltpu.VMEM(classes.shape, jnp.bfloat16),
             pltpu.VMEM((CLASSES, BLOCKS * LANES), jnp.float32),
+            pltpu.VMEM((1, OWN), jnp.float32),
+            pltpu.SemaphoreType.DMA((FINISH_STEPS,)),
             pltpu.SemaphoreType.DMA,
-            pltpu.SemaphoreType.DMA((FINISH_STEPS,)),
         ],
         compiler_params=pltpu.CompilerParams(vmem_limit_bytes=12 * MIB),
         name="finish",
-    )(whole.astype(jnp.float32).reshape(2, BLOCKS, QUADS, 4, LANES), classes)
+    )(whole.astype(jnp.float32).reshape(2, BLOCKS, QUADS, 4, LANES), classes, mine, theirs)
     return new_classes, evidence.reshape(OWN)
 
 

time: 63.5 us -> 61.7 us (0.972)
  Pallas kernels: 10.1 us -> 8.11 us
    pallas_call x2, Pallas kernels: 3.81 us -> 2.9 us  [the longest x1 1.46 us: shards(): pl.pallas_call(sums_kernel, out_shape=jax.ShapeDtypeStruct((CHUNKS, QUADS...]
    pallas_call x1, Pallas kernels: 4.22 us -> 3.32 us  [shards(): pl.pallas_call(score_kernel, out_shape=(jax.ShapeDtypeStruct((36, ROWS, C...]
where the time goes in v5:
time: 61.7 us; the launch traced here: 61.5 us
  blocking collectives  48.7 us (79%)
  Pallas kernels  8.11 us (13%)
  local copies, waits for them, and re-layouts  1.77 us (3%)
  starting transfers between devices  1.17 us (2%)
  other arithmetic  0.97 us (2%)
  between operations  0.73 us (1%)
    all_to_all x1, blocking collectives, shards(): got = lax.all_to_all(parts.astype(jnp.float16), 'cls', 0, 0, tiled=True)  28.3 us
    all_to_all x1, blocking collectives, shards(): whole = lax.all_to_all(repeated, 'cls', 0, 0, tiled=True)  20.3 us
    pallas_call x1, Pallas kernels, shards(): pl.pallas_call(score_kernel, out_shape=(jax.ShapeDtypeStruct((36, ROWS, C...  3.32 us
    unnamed x12, local copies, waits for them, and re-layouts  1.55 us
    pallas_call x1, Pallas kernels, shards(): pl.pallas_call(sums_kernel, out_shape=jax.ShapeDtypeStruct((CHUNKS, QUADS...  1.46 us
    pallas_call x1, Pallas kernels, shards(): pl.pallas_call(finish_kernel, out_shape=(jax.ShapeDtypeStruct((CLASSES, B...  1.45 us
  transfers between devices with their start and end apart: 4, of which 0 were waited for; matrix products, arithmetic and copies ran while one was open for 0% of the time, Pallas kernels for 3%

profile of v5, /device:TPU:0, one launch (start us, length us, event | category | flops | bytes accessed | tf_op | source)
XLA Modules:
  0.0 61.5 jit_solution(8406979016213878499)
XLA Ops:
  0.6 0.1 collective-permute-start
  0.7 0.5 collective-permute-start.1
  1.2 0.1 collective-permute-start.2
  1.3 1.2 %copy-done = bf16[100,4096]{1,0:T(8,128)(2,1)S(1)} copy-done((bf16[100,4096]{1,0:T(8,128)(2,1)S(1)}, bf16[100,4096]{1,0:T(8,128)(2,1)}, u32[]{:S(2)}) %copy-start) | copy-done | bytes 819224
  2.5 0.7 %classes.1 = (bf16[19,224,256]{2,1,0:T(8,128)(2,1)S(1)}, f32[104,128]{1,0:T(8,128)S(1)}) custom-call(bf16[100,4096]{1,0:T(8,128)(2,1)S(1)} %copy-done), custom_call_target="tpu_custom_call" | custom-call | flops 4000000000 | bytes 8388608 | tf_op jit(solution)/shard_map/classes/pallas_call | solution.py:421
  3.2 0.0 collective-permute-done.1
  3.2 0.0 collective-permute-done.2
  3.2 0.0 collective-permute-done.other_ref
  3.2 0.4 copy-done.2
  3.6 0.0 copy-done.3
  3.6 3.3 %scores.1 = (f32[36,104,256]{2,1,0:T(8,128)S(1)}, bf16[256,4864]{1,0:T(8,128)(2,1)S(1)}, f32[16,256]{1,0:T(8,128)S(1)}, f32[104,256]{1,0:T(8,128)S(1)}) custom-call(s32[2,20]{1,0:T(2,128)S(1)} %copy-done.3, bf16[96,4096]{1,0:T(8,128)(2,1)S(1)} %copy-done.2, bf16[96,4096]{1,0:T(8,128)(2,1)S(1)} %collective-permute-done.other_ref, bf16[1,96]{1,0:T(2,128)(2,1)S(1)} %bitcast.7, ...), custom_call_target="tpu_custom_call" | custom-call | flops 4000000000 | bytes 8388608 | tf_op jit(solution)/shard_map/scores/pallas_call | solution.py:434
  6.9 0.5 collective-permute-start.3
  7.4 1.2 %spectra.1.w_ref = f32[36,104,256]{2,1,0:T(8,128)S(1)} custom-call(f32[36,104,256]{2,1,0:T(8,128)S(1)} %get-tuple-element.12.e_ref, f32[104,256]{1,0:T(8,128)S(1)} %get-tuple-element.13.top_ref, f32[16,256]{1,0:T(8,128)S(1)} %get-tuple-element.14.stat_ref.mine), custom_call_target="tpu_custom_call" | custom-call | flops 4000000000 | bytes 8388608 | tf_op jit(solution)/shard_map/spectra/pallas_call | solution.py:465
  8.6 0.0 collective-permute-done.3.theirs
  8.6 1.5 %sums.1 = f32[64,13,4,128]{3,2,1,0:T(4,128)S(1)} custom-call(f32[36,104,256]{2,1,0:T(8,128)S(1)} %spectra.1.w_ref, bf16[256,4864]{1,0:T(8,128)(2,1)S(1)} %get-tuple-element.15.xp_ref, f32[16,256]{1,0:T(8,128)S(1)} %get-tuple-element.14.stat_ref.mine, f32[16,256]{1,0:T(8,128)S(1)} %collective-permute-done.3.theirs), custom_call_target="tpu_custom_call" | custom-call | tf_op jit(solution)/shard_map/sums/pallas_call | solution.py:475
  10.1 0.3 convert_element_type.14
  10.4 28.3 %all_to_all.10 = f16[64,13,4,128]{3,2,1,0:T(4,128)(2,1)S(1)} all-to-all(f16[64,13,4,128]{3,2,1,0:T(4,128)(2,1)S(1)} %convert_element_type.14), channel_id=1, replica_groups=mesh['dom'=2,'cls'=64] {'cls'}, dimensions={0} | all-to-all | bytes 1703936 | tf_op jit(solution)/shard_map/all_to_all | solution.py:485
  38.7 0.4 convert_reduce_fusion
  39.1 0.2 broadcast_in_dim.2
  39.3 0.0 copy-start.1
  39.4 20.3 %all_to_all.11 = f16[64,13,4,128]{3,2,1,0:T(4,128)(2,1)S(1)} all-to-all(f16[64,13,4,128]{3,2,1,0:T(4,128)(2,1)S(1)} %broadcast_in_dim.2), channel_id=1, replica_groups=mesh['dom'=2,'cls'=64] {'cls'}, dimensions={0} | all-to-all | bytes 1703936 | tf_op jit(solution)/shard_map/all_to_all | solution.py:488
  59.7 0.3 convert.1.sum_ref
  60.0 0.0 copy-done.1
  60.0 1.4 %finish.1 = (f32[100,4096]{1,0:T(8,128)}, f32[1,96]{1,0:T(1,128)}) custom-call(f32[2,32,13,4,128]{4,3,2,1,0:T(4,128)S(1)} %convert.1.sum_ref, bf16[100,4096]{1,0:T(8,128)(2,1)S(1)} %copy-done.1, f32[16,256]{1,0:T(8,128)S(1)} %get-tuple-element.14.stat_ref.mine, f32[16,256]{1,0:T(8,128)S(1)} %collective-permute-done.3.theirs), custom_call_target="tpu_custom_call" | custom-call | tf_op jit(solution)/shard_map/finish/pallas_call | solution.py:489
  (8 shorter events, 0.0 us)
Async XLA Ops:
  0.6 2.6 %collective-permute-start = (bf16[96,4096]{1,0:T(8,128)(2,1)}, bf16[96,4096]{1,0:T(8,128)(2,1)S(1)}, u32[]{:S(2)}, u32[]{:S(2)}) collective-permute-start(bf16[96,4096]{1,0:T(8,128)(2,1)} %own_ref.1), channel_id=1, source_target_pairs={{0,64},{64,0},{1,65},{65,1},{2,66},{66,2},{3,67},{67,3},{4,68},{68... | collective-permute-start | bytes 2359304 | tf_op jit(solution)/shard_map/ppermute | solution.py:416
  0.7 2.5 %collective-permute-start.1 = (bf16[96]{0:T(256)(128)(2,1)}, bf16[96]{0:T(256)(128)(2,1)S(1)}, u32[]{:S(2)}, u32[]{:S(2)}) collective-permute-start(bf16[96]{0:T(256)(128)(2,1)} %param.6), channel_id=1, source_target_pairs={{0,64},{64,0},{1,65},{65,1},{2,66},{66,2},{3,67},{67,3},{4,68},{68... | collective-permute-start | bytes 584 | tf_op jit(solution)/shard_map/ppermute | solution.py:417
  1.2 2.0 %collective-permute-start.2 = (s32[96]{0:T(128)}, s32[96]{0:T(128)S(1)}, u32[]{:S(2)}, u32[]{:S(2)}) collective-permute-start(s32[96]{0:T(128)} %param.7), channel_id=1, source_target_pairs={{0,64},{64,0},{1,65},{65,1},{2,66},{66,2},{3,67},{67,3},{4,68},{68... | collective-permute-start | bytes 1160 | tf_op jit(solution)/shard_map/ppermute | solution.py:418
  1.3 1.2 %copy-start = (bf16[100,4096]{1,0:T(8,128)(2,1)S(1)}, bf16[100,4096]{1,0:T(8,128)(2,1)}, u32[]{:S(2)}) copy-start(bf16[100,4096]{1,0:T(8,128)(2,1)} %cls_ref.3) | copy-start | bytes 2457604
  2.5 1.1 %copy-start.2 = (bf16[96,4096]{1,0:T(8,128)(2,1)S(1)}, bf16[96,4096]{1,0:T(8,128)(2,1)}, u32[]{:S(2)}) copy-start(bf16[96,4096]{1,0:T(8,128)(2,1)} %own_ref.1) | copy-start | bytes 2359300
  2.5 1.1 %copy-start.3 = (s32[2,20]{1,0:T(2,128)S(1)}, s32[2,20]{1,0:T(2,128)}, u32[]{:S(2)}) copy-start(s32[2,20]{1,0:T(2,128)} %blocks_ref.1) | copy-start | bytes 484
  2.5 1.1 %copy-start.4 = (bf16[96]{0:T(256)(128)(2,1)S(1)}, bf16[96]{0:T(256)(128)(2,1)}, u32[]{:S(2)}) copy-start(bf16[96]{0:T(256)(128)(2,1)} %param.6) | copy-start | bytes 580
  2.5 1.1 %copy-start.5 = (s32[96]{0:T(128)S(1)}, s32[96]{0:T(128)}, u32[]{:S(2)}) copy-start(s32[96]{0:T(128)} %param.7) | copy-start | bytes 1156
  6.9 1.7 %collective-permute-start.3 = (f32[16,256]{1,0:T(8,128)S(1)}, f32[16,256]{1,0:T(8,128)S(1)}, u32[]{:S(2)}, u32[]{:S(2)}) collective-permute-start(f32[16,256]{1,0:T(8,128)S(1)} %get-tuple-element.14.stat_ref.mine), channel_id=1, source_target_pairs={{0,64},{64,0},{1,65},{65,1},{2,66},{66,2},{3,67},{67,3},{4,68},{68... | collective-permute-start | bytes 49160 | tf_op jit(solution)/shard_map/ppermute | solution.py:463
  39.3 20.7 %copy-start.1 = (bf16[100,4096]{1,0:T(8,128)(2,1)S(1)}, bf16[100,4096]{1,0:T(8,128)(2,1)}, u32[]{:S(2)}) copy-start(bf16[100,4096]{1,0:T(8,128)(2,1)} %cls_ref.3) | copy-start | bytes 2457604

commit v6 on v5

--- a/solution.py
+++ b/solution.py
@@ -14,6 +14,7 @@
 ROTATIONS = 36
 CLASS_BLOCK = 5
 EXCLUDED = -1e30
+LOG2_E = math.log2(math.e)
 PRIOR_WIDTH = 12.0
 CLASS_PRIOR = 16.0
 
@@ -199,7 +200,7 @@
     inside = (row >= first) & (row < first + CLASS_BLOCK)
     swapped = lax.axis_index("dom") == 1
     allowed = [blocks_ref[0:1], blocks_ref[1:2]]
-    precisions = [particle_row(p[...].astype(jnp.float32)) for p in (prec_a, prec_b)]
+    precisions = [particle_row(p[...].astype(jnp.float32) * LOG2_E) for p in (prec_a, prec_b)]
     for half in range(2):
         lanes = slice(half * LANES, (half + 1) * LANES)
         admit = jnp.where(swapped, allowed[1 - half], allowed[half]) == 1
@@ -208,7 +209,7 @@
         offset = particle_row((offset_a, offset_b)[half][...])
         steps = lax.rem(lax.broadcasted_iota(jnp.int32, (40, LANES), 0) - offset + ROTATIONS, ROTATIONS)
         distance = jnp.minimum(steps, ROTATIONS - steps).astype(jnp.float32) * (1.0 / PRIOR_WIDTH)
-        prior_ref[:, lanes] = -0.5 * distance * distance
+        prior_ref[:, lanes] = (-0.5 * LOG2_E) * distance * distance
     zeros = jnp.zeros((LANES - OWN, RESIDUES * COLS), jnp.bfloat16)
     xp_ref[OWN:LANES] = zeros
     xp_ref[LANES + OWN :] = zeros
@@ -236,28 +237,28 @@
         def scores(i, carry):
             peak, mass = carry
             rows = pl.ds(pl.multiple_of(i * 8, 8), 8)
-            a = [ab_ref[j, rows, lanes] for j in range(19)]
-            b = [None] + [ab_ref[18 + j, rows, lanes] for j in range(1, 18)]
-            base = base_ref[rows, lanes]
-            correlation = to_rotations(a, b)
-            score = [correlation[r] * prec + (base + prior_ref[r : r + 1, lanes]) for r in range(ROTATIONS)]
+            a = [ab_ref[j, rows, lanes] * prec for j in range(19)]
+            b = [None] + [ab_ref[18 + j, rows, lanes] * prec for j in range(1, 18)]
+            a[0] = a[0] + base_ref[rows, lanes]
+            score = to_rotations(a, b)
+            score = [score[r] + prior_ref[r : r + 1, lanes] for r in range(ROTATIONS)]
             top = score[0]
             for r in range(1, ROTATIONS):
                 top = jnp.maximum(top, score[r])
             total = None
             for r in range(ROTATIONS):
-                e = jnp.exp(score[r] - top)
+                e = jnp.exp2(score[r] - top)
                 e_ref[r, rows, lanes] = e
                 total = e if total is None else total + e
             top_ref[rows, lanes] = top
             higher = jnp.maximum(peak, top)
-            mass = mass * jnp.exp(peak - higher) + total * jnp.exp(top - higher)
+            mass = mass * jnp.exp2(peak - higher) + total * jnp.exp2(top - higher)
             return higher, mass
 
         start = (jnp.full((8, LANES), EXCLUDED, jnp.float32), jnp.zeros((8, LANES), jnp.float32))
         tops, mass = lax.fori_loop(0, ROWS // 8, scores, start, unroll=True)
         peak = jnp.max(tops, axis=0, keepdims=True)
-        mass = jnp.sum(mass * jnp.exp(tops - peak), axis=0, keepdims=True)
+        mass = jnp.sum(mass * jnp.exp2(tops - peak), axis=0, keepdims=True)
         stat_ref[0:8, lanes] = jnp.broadcast_to(peak, (8, LANES))
         stat_ref[8:16, lanes] = jnp.broadcast_to(mass, (8, LANES))
 
@@ -270,7 +271,7 @@
 
         def spectra(i, carry):
             rows = pl.ds(pl.multiple_of(i * 8, 8), 8)
-            lift = jnp.exp(top_ref[rows, lanes] - peak)
+            lift = jnp.exp2(top_ref[rows, lanes] - peak)
             c, s = from_rotations([e_ref[r, rows, lanes] * lift for r in range(ROTATIONS)])
             for j in range(19):
                 w_ref[j, rows, lanes] = c[j]
@@ -303,8 +304,8 @@
     here = slice(half * LANES, (half + 1) * LANES)
     there = slice((1 - half) * LANES, (2 - half) * LANES)
     peak = jnp.maximum(mine[0:1, here], theirs[0:1, there])
-    mass = mine[8:9, here] * jnp.exp(mine[0:1, here] - peak)
-    mass = mass + theirs[8:9, there] * jnp.exp(theirs[0:1, there] - peak)
+    mass = mine[8:9, here] * jnp.exp2(mine[0:1, here] - peak)
+    mass = mass + theirs[8:9, there] * jnp.exp2(theirs[0:1, there] - peak)
     held = lax.broadcasted_iota(jnp.int32, (1, LANES), 1) < OWN
     return held, peak, jnp.where(held, mass, 1.0)
 
@@ -313,7 +314,7 @@
     scale = []
     for half in range(2):
         held, peak, mass = settle(mine, theirs, half)
-        lift = jnp.exp(mine[0:1, half * LANES : (half + 1) * LANES] - peak)
+        lift = jnp.exp2(mine[0:1, half * LANES : (half + 1) * LANES] - peak)
         scale.append(jnp.where(held, lift * SUM_SCALE / mass, 0.0))
     scale = jnp.concatenate(scale, axis=1)
 
@@ -375,7 +376,7 @@
 
 def finish_kernel(sum_ref, cls_ref, mine, theirs, out_hbm, evidence_hbm, out_ref, evidence_ref, out_sems, evidence_sem):
     _, peak, mass = settle(mine, theirs, 0)
-    evidence_ref[...] = (peak + jnp.log(mass))[:, :OWN]
+    evidence_ref[...] = (peak * (1.0 / LOG2_E) + jnp.log(mass))[:, :OWN]
     send = pltpu.make_async_copy(evidence_ref, evidence_hbm, evidence_sem)
     send.start()
     row = lax.broadcasted_iota(jnp.int32, (HALF_ROWS, LANES), 0)
@@ -384,7 +385,7 @@
     total = sum_ref[0, 0, SPLIT // 4, 0:1, :]
     for half in range(2):
         weight = jnp.sum(jnp.where(lane == row + half * SPLIT, total, 0.0), axis=1, keepdims=True)
-        share.append(1.0 / (weight * (1.0 / SUM_SCALE) + CLASS_PRIOR))
+        share.append((1.0 / SUM_SCALE) / (weight * (1.0 / SUM_SCALE) + CLASS_PRIOR))
     copies = []
     for step in range(FINISH_STEPS):
         for block in range(step * STEP_BLOCKS, (step + 1) * STEP_BLOCKS):
@@ -393,7 +394,7 @@
             for half in range(2):
                 count = SPLIT if half == 0 else CLASSES - SPLIT
                 rows = slice(half * SPLIT, half * SPLIT + count)
-                new = sum_ref[half, block].reshape(HALF_ROWS, LANES)[:count] * (1.0 / SUM_SCALE) + CLASS_PRIOR * old[rows]
+                new = sum_ref[half, block].reshape(HALF_ROWS, LANES)[:count] + (CLASS_PRIOR * SUM_SCALE) * old[rows]
                 out_ref[rows, lanes] = new * share[half][:count]
         lanes = slice(step * STEP_BLOCKS * LANES, (step + 1) * STEP_BLOCKS * LANES)
         copy = pltpu.make_async_copy(out_ref.at[:, lanes], out_hbm.at[:, lanes], out_sems.at[step])
@@ -482,7 +483,7 @@
         name="sums",
     )(weights, by_residue, mine, theirs)
 
-    got = lax.all_to_all(parts.astype(jnp.float16), "cls", 0, 0, tiled=True)
+    got = lax.all_to_all(parts.reshape(CHUNKS * HALF_ROWS, LANES).astype(jnp.float16).reshape(parts.shape), "cls", 0, 0, tiled=True)
     total = jnp.sum(got.astype(jnp.float32), axis=0).astype(jnp.float16)
     repeated = jnp.broadcast_to(total[None], (CHUNKS, QUADS, 4, LANES))
     whole = lax.all_to_all(repeated, "cls", 0, 0, tiled=True)
@@ -502,7 +503,7 @@
         ],
         compiler_params=pltpu.CompilerParams(vmem_limit_bytes=12 * MIB),
         name="finish",
-    )(whole.astype(jnp.float32).reshape(2, BLOCKS, QUADS, 4, LANES), classes, mine, theirs)
+    )(whole.reshape(CHUNKS * HALF_ROWS, LANES).astype(jnp.float32).reshape(2, BLOCKS, QUADS, 4, LANES), classes, mine, theirs)
     return new_classes, evidence.reshape(OWN)
 
 

time: 61.7 us -> 61.6 us (level)
  no operation moved by 1% of the time
where the time goes in v6:
time: 61.6 us; the launch traced here: 61.3 us
  blocking collectives  48.7 us (79%)
  Pallas kernels  7.97 us (13%)
  local copies, waits for them, and re-layouts  1.77 us (3%)
  starting transfers between devices  1.17 us (2%)
  other arithmetic  0.97 us (2%)
  between operations  0.73 us (1%)
    all_to_all x1, blocking collectives, shards(): lax.all_to_all(parts.reshape(CHUNKS * HALF_ROWS, LANES).astype(jnp.float1...  28.4 us
    all_to_all x1, blocking collectives, shards(): whole = lax.all_to_all(repeated, 'cls', 0, 0, tiled=True)  20.3 us
    pallas_call x1, Pallas kernels, shards(): pl.pallas_call(score_kernel, out_shape=(jax.ShapeDtypeStruct((36, ROWS, C...  3.24 us
    unnamed x12, local copies, waits for them, and re-layouts  1.55 us
    pallas_call x1, Pallas kernels, shards(): pl.pallas_call(sums_kernel, out_shape=jax.ShapeDtypeStruct((CHUNKS, QUADS...  1.45 us
    pallas_call x1, Pallas kernels, shards(): pl.pallas_call(finish_kernel, out_shape=(jax.ShapeDtypeStruct((CLASSES, B...  1.39 us
  transfers between devices with their start and end apart: 4, of which 0 were waited for; matrix products, arithmetic and copies ran while one was open for 0% of the time, Pallas kernels for 3%

profile of v6, /device:TPU:0, one launch (start us, length us, event | category | flops | bytes accessed | tf_op | source)
XLA Modules:
  0.0 61.3 jit_solution(4778154760720743301)
XLA Ops:
  0.6 0.1 collective-permute-start
  0.7 0.5 collective-permute-start.1
  1.2 0.1 collective-permute-start.2
  1.3 1.2 %copy-done = bf16[100,4096]{1,0:T(8,128)(2,1)S(1)} copy-done((bf16[100,4096]{1,0:T(8,128)(2,1)S(1)}, bf16[100,4096]{1,0:T(8,128)(2,1)}, u32[]{:S(2)}) %copy-start) | copy-done | bytes 819224
  2.5 0.7 %classes.1 = (bf16[19,224,256]{2,1,0:T(8,128)(2,1)S(1)}, f32[104,128]{1,0:T(8,128)S(1)}) custom-call(bf16[100,4096]{1,0:T(8,128)(2,1)S(1)} %copy-done), custom_call_target="tpu_custom_call" | custom-call | flops 4000000000 | bytes 8388608 | tf_op jit(solution)/shard_map/classes/pallas_call | solution.py:422
  3.2 0.0 collective-permute-done.1
  3.2 0.0 collective-permute-done.2
  3.2 0.0 collective-permute-done.other_ref
  3.2 0.4 copy-done.2
  3.6 0.0 copy-done.3
  3.6 3.2 %scores.1 = (f32[36,104,256]{2,1,0:T(8,128)S(1)}, bf16[256,4864]{1,0:T(8,128)(2,1)S(1)}, f32[16,256]{1,0:T(8,128)S(1)}, f32[104,256]{1,0:T(8,128)S(1)}) custom-call(s32[2,20]{1,0:T(2,128)S(1)} %copy-done.3, bf16[96,4096]{1,0:T(8,128)(2,1)S(1)} %copy-done.2, bf16[96,4096]{1,0:T(8,128)(2,1)S(1)} %collective-permute-done.other_ref, bf16[1,96]{1,0:T(2,128)(2,1)S(1)} %bitcast.7, ...), custom_call_target="tpu_custom_call" | custom-call | flops 4000000000 | bytes 8388608 | tf_op jit(solution)/shard_map/scores/pallas_call | solution.py:435
  6.9 0.5 collective-permute-start.3
  7.4 1.2 %spectra.1.w_ref = f32[36,104,256]{2,1,0:T(8,128)S(1)} custom-call(f32[36,104,256]{2,1,0:T(8,128)S(1)} %get-tuple-element.12.e_ref, f32[104,256]{1,0:T(8,128)S(1)} %get-tuple-element.13.top_ref, f32[16,256]{1,0:T(8,128)S(1)} %get-tuple-element.14.stat_ref.mine), custom_call_target="tpu_custom_call" | custom-call | flops 4000000000 | bytes 8388608 | tf_op jit(solution)/shard_map/spectra/pallas_call | solution.py:466
  8.5 0.0 collective-permute-done.3.theirs
  8.6 1.4 %sums.1 = f32[64,13,4,128]{3,2,1,0:T(4,128)S(1)} custom-call(f32[36,104,256]{2,1,0:T(8,128)S(1)} %spectra.1.w_ref, bf16[256,4864]{1,0:T(8,128)(2,1)S(1)} %get-tuple-element.15.xp_ref, f32[16,256]{1,0:T(8,128)S(1)} %get-tuple-element.14.stat_ref.mine, f32[16,256]{1,0:T(8,128)S(1)} %collective-permute-done.3.theirs), custom_call_target="tpu_custom_call" | custom-call | tf_op jit(solution)/shard_map/sums/pallas_call | solution.py:476
  10.0 0.3 convert_element_type.21
  10.3 28.4 %all_to_all.10 = f16[64,13,4,128]{3,2,1,0:T(4,128)(2,1)S(1)} all-to-all(f16[64,13,4,128]{3,2,1,0:T(4,128)(2,1)S(1)} %convert_element_type.21), channel_id=1, replica_groups=mesh['dom'=2,'cls'=64] {'cls'}, dimensions={0} | all-to-all | bytes 1703936 | tf_op jit(solution)/shard_map/all_to_all | solution.py:486
  38.7 0.4 convert_reduce_fusion
  39.1 0.2 broadcast_in_dim.2
  39.3 0.0 copy-start.1
  39.3 20.3 %all_to_all.11 = f16[64,13,4,128]{3,2,1,0:T(4,128)(2,1)S(1)} all-to-all(f16[64,13,4,128]{3,2,1,0:T(4,128)(2,1)S(1)} %broadcast_in_dim.2), channel_id=1, replica_groups=mesh['dom'=2,'cls'=64] {'cls'}, dimensions={0} | all-to-all | bytes 1703936 | tf_op jit(solution)/shard_map/all_to_all | solution.py:489
  59.6 0.3 convert.1.sum_ref
  59.9 0.0 copy-done.1
  60.0 1.4 %finish.1 = (f32[100,4096]{1,0:T(8,128)}, f32[1,96]{1,0:T(1,128)}) custom-call(f32[2,32,13,4,128]{4,3,2,1,0:T(4,128)S(1)} %convert.1.sum_ref, bf16[100,4096]{1,0:T(8,128)(2,1)S(1)} %copy-done.1, f32[16,256]{1,0:T(8,128)S(1)} %get-tuple-element.14.stat_ref.mine, f32[16,256]{1,0:T(8,128)S(1)} %collective-permute-done.3.theirs), custom_call_target="tpu_custom_call" | custom-call | tf_op jit(solution)/shard_map/finish/pallas_call | solution.py:490
  (8 shorter events, 0.0 us)
Async XLA Ops:
  0.6 2.6 %collective-permute-start = (bf16[96,4096]{1,0:T(8,128)(2,1)}, bf16[96,4096]{1,0:T(8,128)(2,1)S(1)}, u32[]{:S(2)}, u32[]{:S(2)}) collective-permute-start(bf16[96,4096]{1,0:T(8,128)(2,1)} %own_ref.1), channel_id=1, source_target_pairs={{0,64},{64,0},{1,65},{65,1},{2,66},{66,2},{3,67},{67,3},{4,68},{68... | collective-permute-start | bytes 2359304 | tf_op jit(solution)/shard_map/ppermute | solution.py:417
  0.7 2.5 %collective-permute-start.1 = (bf16[96]{0:T(256)(128)(2,1)}, bf16[96]{0:T(256)(128)(2,1)S(1)}, u32[]{:S(2)}, u32[]{:S(2)}) collective-permute-start(bf16[96]{0:T(256)(128)(2,1)} %param.6), channel_id=1, source_target_pairs={{0,64},{64,0},{1,65},{65,1},{2,66},{66,2},{3,67},{67,3},{4,68},{68... | collective-permute-start | bytes 584 | tf_op jit(solution)/shard_map/ppermute | solution.py:418
  1.2 2.0 %collective-permute-start.2 = (s32[96]{0:T(128)}, s32[96]{0:T(128)S(1)}, u32[]{:S(2)}, u32[]{:S(2)}) collective-permute-start(s32[96]{0:T(128)} %param.7), channel_id=1, source_target_pairs={{0,64},{64,0},{1,65},{65,1},{2,66},{66,2},{3,67},{67,3},{4,68},{68... | collective-permute-start | bytes 1160 | tf_op jit(solution)/shard_map/ppermute | solution.py:419
  1.3 1.2 %copy-start = (bf16[100,4096]{1,0:T(8,128)(2,1)S(1)}, bf16[100,4096]{1,0:T(8,128)(2,1)}, u32[]{:S(2)}) copy-start(bf16[100,4096]{1,0:T(8,128)(2,1)} %cls_ref.3) | copy-start | bytes 2457604
  2.5 1.1 %copy-start.2 = (bf16[96,4096]{1,0:T(8,128)(2,1)S(1)}, bf16[96,4096]{1,0:T(8,128)(2,1)}, u32[]{:S(2)}) copy-start(bf16[96,4096]{1,0:T(8,128)(2,1)} %own_ref.1) | copy-start | bytes 2359300
  2.5 1.1 %copy-start.3 = (s32[2,20]{1,0:T(2,128)S(1)}, s32[2,20]{1,0:T(2,128)}, u32[]{:S(2)}) copy-start(s32[2,20]{1,0:T(2,128)} %blocks_ref.1) | copy-start | bytes 484
  2.5 1.1 %copy-start.4 = (bf16[96]{0:T(256)(128)(2,1)S(1)}, bf16[96]{0:T(256)(128)(2,1)}, u32[]{:S(2)}) copy-start(bf16[96]{0:T(256)(128)(2,1)} %param.6) | copy-start | bytes 580
  2.5 1.1 %copy-start.5 = (s32[96]{0:T(128)S(1)}, s32[96]{0:T(128)}, u32[]{:S(2)}) copy-start(s32[96]{0:T(128)} %param.7) | copy-start | bytes 1156
  6.9 1.7 %collective-permute-start.3 = (f32[16,256]{1,0:T(8,128)S(1)}, f32[16,256]{1,0:T(8,128)S(1)}, u32[]{:S(2)}, u32[]{:S(2)}) collective-permute-start(f32[16,256]{1,0:T(8,128)S(1)} %get-tuple-element.14.stat_ref.mine), channel_id=1, source_target_pairs={{0,64},{64,0},{1,65},{65,1},{2,66},{66,2},{3,67},{67,3},{4,68},{68... | collective-permute-start | bytes 49160 | tf_op jit(solution)/shard_map/ppermute | solution.py:464
  39.3 20.7 %copy-start.1 = (bf16[100,4096]{1,0:T(8,128)(2,1)S(1)}, bf16[100,4096]{1,0:T(8,128)(2,1)}, u32[]{:S(2)}) copy-start(bf16[100,4096]{1,0:T(8,128)(2,1)} %cls_ref.3) | copy-start | bytes 2457604

commit v7 on v6

--- a/solution.py
+++ b/solution.py
@@ -193,7 +193,26 @@
     return jnp.concatenate([values, jnp.zeros((1, LANES - OWN), values.dtype)], axis=1)
 
 
-def score_kernel(blocks_ref, own_ref, other_ref, prec_a, prec_b, offset_a, offset_b, cp_ref, norm_ref, e_ref, xp_ref, stat_ref, top_ref, ab_ref, base_ref, prior_ref):
+def correlate(image_ref, cp_ref, xp_ref, ab_ref):
+    xp_ref[OWN:] = jnp.zeros((LANES - OWN, RESIDUES * COLS), jnp.bfloat16)
+    for part in range(2):
+        for i in range(0, OWN, 16):
+            tiles = lambda t: image_ref[i : i + 16, part * PART + t * LANES : part * PART + (t + 1) * LANES]
+            for j, value in to_residues(tiles, 16):
+                at = j * COLS + part * LANES
+                xp_ref[i : i + 16, at : at + LANES] = value
+    for j in range(RESIDUES):
+        pair = 0 < j < 18
+        operand = cp_ref[j] if pair else cp_ref[j, :ROWS_16]
+        got = lax.dot_general(
+            operand, xp_ref[:, j * COLS : (j + 1) * COLS], (((1,), (1,)), ((), ())), preferred_element_type=jnp.float32
+        )
+        ab_ref[j] = got[:ROWS]
+        if pair:
+            ab_ref[18 + j] = got[ROWS_16 : ROWS_16 + ROWS]
+
+
+def score_kernel(blocks_ref, other_ref, prec_a, prec_b, offset_a, offset_b, cp_ref, norm_ref, ab_own, e_ref, xp_ref, stat_ref, top_ref, ab_other, base_ref, prior_ref):
     blocks = CLASSES // CLASS_BLOCK
     first = lax.broadcasted_iota(jnp.int32, (ROWS, blocks), 1) * CLASS_BLOCK
     row = lax.broadcasted_iota(jnp.int32, (ROWS, blocks), 0)
@@ -210,35 +229,18 @@
         steps = lax.rem(lax.broadcasted_iota(jnp.int32, (40, LANES), 0) - offset + ROTATIONS, ROTATIONS)
         distance = jnp.minimum(steps, ROTATIONS - steps).astype(jnp.float32) * (1.0 / PRIOR_WIDTH)
         prior_ref[:, lanes] = (-0.5 * LOG2_E) * distance * distance
-    zeros = jnp.zeros((LANES - OWN, RESIDUES * COLS), jnp.bfloat16)
-    xp_ref[OWN:LANES] = zeros
-    xp_ref[LANES + OWN :] = zeros
-    for first_row, ref in ((0, own_ref), (LANES, other_ref)):
-        for part in range(2):
-            for i in range(0, OWN, 16):
-                tiles = lambda t: ref[i : i + 16, part * PART + t * LANES : part * PART + (t + 1) * LANES]
-                for j, value in to_residues(tiles, 16):
-                    at = j * COLS + part * LANES
-                    xp_ref[first_row + i : first_row + i + 16, at : at + LANES] = value
-    for j in range(RESIDUES):
-        pair = 0 < j < 18
-        operand = cp_ref[j] if pair else cp_ref[j, :ROWS_16]
-        got = lax.dot_general(
-            operand, xp_ref[:, j * COLS : (j + 1) * COLS], (((1,), (1,)), ((), ())), preferred_element_type=jnp.float32
-        )
-        ab_ref[j] = got[:ROWS]
-        if pair:
-            ab_ref[18 + j] = got[ROWS_16 : ROWS_16 + ROWS]
+    correlate(other_ref, cp_ref, xp_ref, ab_other)
 
     for half in range(2):
         lanes = slice(half * LANES, (half + 1) * LANES)
         prec = jnp.broadcast_to(precisions[half], (8, LANES))
+        ab_ref = (ab_own, ab_other)[half]
 
         def scores(i, carry):
             peak, mass = carry
             rows = pl.ds(pl.multiple_of(i * 8, 8), 8)
-            a = [ab_ref[j, rows, lanes] * prec for j in range(19)]
-            b = [None] + [ab_ref[18 + j, rows, lanes] * prec for j in range(1, 18)]
+            a = [ab_ref[j, rows] * prec for j in range(19)]
+            b = [None] + [ab_ref[18 + j, rows] * prec for j in range(1, 18)]
             a[0] = a[0] + base_ref[rows, lanes]
             score = to_rotations(a, b)
             score = [score[r] + prior_ref[r : r + 1, lanes] for r in range(ROTATIONS)]
@@ -282,7 +284,12 @@
         lax.fori_loop(0, ROWS // 8, spectra, 0, unroll=True)
 
 
-def class_kernel(cls_ref, cp_ref, norm_ref):
+def sign_kernel(sign_ref):
+    for j in range(RESIDUES):
+        sign_ref[j : j + 1] = sign_lanes(j, 1)
+
+
+def own_kernel(cls_ref, sign_ref, own_ref, cp_ref, norm_ref, xp_ref, ab_ref):
     pad = jnp.zeros((ROWS_16 - CLASSES, LANES), jnp.bfloat16)
     for part in range(2):
         tiles = lambda t: cls_ref[:, part * PART + t * LANES : part * PART + (t + 1) * LANES]
@@ -290,7 +297,7 @@
             value = jnp.concatenate([value, pad], axis=0)
             cp_ref[j, :ROWS_16, part * LANES : (part + 1) * LANES] = value
             if 0 < j < 18:
-                sign = sign_lanes(j, ROWS_16) * (1.0 if part else -1.0)
+                sign = jnp.broadcast_to(sign_ref[j : j + 1], (ROWS_16, LANES)) * (1.0 if part else -1.0)
                 cp_ref[j, ROWS_16:, (1 - part) * LANES : (2 - part) * LANES] = value * sign.astype(jnp.bfloat16)
     norm = jnp.zeros((CLASSES, LANES), jnp.float32)
     for block in range(BLOCKS):
@@ -298,6 +305,7 @@
         norm = norm + member * member
     norm = jnp.broadcast_to(jnp.sum(norm, axis=1, keepdims=True), (CLASSES, LANES))
     norm_ref[...] = jnp.concatenate([norm, jnp.zeros((ROWS - CLASSES, LANES), jnp.float32)], axis=0)
+    correlate(own_ref, cp_ref, xp_ref, ab_ref)
 
 
 def settle(mine, theirs, half):
@@ -310,7 +318,7 @@
     return held, peak, jnp.where(held, mass, 1.0)
 
 
-def sums_kernel(w_ref, xp_ref, mine, theirs, out_ref, pc_ref):
+def sums_kernel(w_ref, xp_own, xp_other, mine, theirs, out_ref, pc_ref):
     scale = []
     for half in range(2):
         held, peak, mass = settle(mine, theirs, half)
@@ -341,7 +349,7 @@
         high = weight.astype(jnp.bfloat16)
         low = (weight - high.astype(jnp.float32)).astype(jnp.bfloat16)
         lanes = slice(j * COLS, (j + 1) * COLS)
-        images = xp_ref[:, lanes]
+        images = jnp.concatenate([xp_own[:, lanes], xp_other[:, lanes]], axis=0)
         dims = (((1,), (0,)), ((), ()))
         got = lax.dot_general(high, images, dims, preferred_element_type=jnp.float32)
         got = got + lax.dot_general(low, images, dims, preferred_element_type=jnp.float32)
@@ -419,31 +427,41 @@
     other_offset = lax.ppermute(rotation_offset, "dom", swap)
 
     cost = pl.CostEstimate(flops=4 * 10**9, bytes_accessed=8 * MIB, transcendentals=36 * 104 * 128)
-    cp, norm = pl.pallas_call(
-        class_kernel,
+    signs = pl.pallas_call(
+        sign_kernel,
+        out_shape=jax.ShapeDtypeStruct((RESIDUES, LANES), jnp.float32),
+        out_specs=VMEM,
+        compiler_params=pltpu.CompilerParams(vmem_limit_bytes=4 * MIB),
+        cost_estimate=cost,
+        name="signs",
+    )()
+    cp, norm, xp_own, ab_own = pl.pallas_call(
+        own_kernel,
         out_shape=(
             jax.ShapeDtypeStruct((RESIDUES, 2 * ROWS_16, COLS), jnp.bfloat16),
             jax.ShapeDtypeStruct((ROWS, LANES), jnp.float32),
+            jax.ShapeDtypeStruct((LANES, RESIDUES * COLS), jnp.bfloat16),
+            jax.ShapeDtypeStruct((36, ROWS, LANES), jnp.float32),
         ),
-        in_specs=[VMEM],
-        out_specs=(VMEM,) * 2,
-        compiler_params=pltpu.CompilerParams(vmem_limit_bytes=12 * MIB),
+        in_specs=[VMEM] * 3,
+        out_specs=(VMEM,) * 4,
+        compiler_params=pltpu.CompilerParams(vmem_limit_bytes=16 * MIB),
         cost_estimate=cost,
-        name="classes",
-    )(classes)
-
-    e, by_residue, mine, tops = pl.pallas_call(
+        name="own",
+    )(classes, signs, images)
+
+    e, xp_other, mine, tops = pl.pallas_call(
         score_kernel,
         out_shape=(
             jax.ShapeDtypeStruct((36, ROWS, COLS), jnp.float32),
-            jax.ShapeDtypeStruct((COLS, RESIDUES * COLS), jnp.bfloat16),
+            jax.ShapeDtypeStruct((LANES, RESIDUES * COLS), jnp.bfloat16),
             jax.ShapeDtypeStruct((16, COLS), jnp.float32),
             jax.ShapeDtypeStruct((ROWS, COLS), jnp.float32),
         ),
         in_specs=[VMEM] * 9,
         out_specs=(VMEM,) * 4,
         scratch_shapes=[
-            pltpu.VMEM((36, ROWS, COLS), jnp.float32),
+            pltpu.VMEM((36, ROWS, LANES), jnp.float32),
             pltpu.VMEM((ROWS, COLS), jnp.float32),
             pltpu.VMEM((40, COLS), jnp.float32),
         ],
@@ -452,7 +470,6 @@
         name="scores",
     )(
         prior_blocks,
-        images,
         other_images,
         precision.reshape(1, OWN),
         other_precision.reshape(1, OWN),
@@ -460,6 +477,7 @@
         other_offset.reshape(1, OWN),
         cp,
         norm,
+        ab_own,
     )
     theirs = lax.ppermute(mine, "dom", swap)
 
@@ -476,14 +494,16 @@
     parts = pl.pallas_call(
         sums_kernel,
         out_shape=jax.ShapeDtypeStruct((CHUNKS, QUADS, 4, LANES), jnp.float32),
-        in_specs=[VMEM] * 4,
+        in_specs=[VMEM] * 5,
         out_specs=VMEM,
         scratch_shapes=[pltpu.VMEM((ROWS, RESIDUES * COLS), jnp.float32)],
         compiler_params=pltpu.CompilerParams(vmem_limit_bytes=20 * MIB),
         name="sums",
-    )(weights, by_residue, mine, theirs)
-
-    got = lax.all_to_all(parts.reshape(CHUNKS * HALF_ROWS, LANES).astype(jnp.float16).reshape(parts.shape), "cls", 0, 0, tiled=True)
+    )(weights, xp_own, xp_other, mine, theirs)
+
+    flat = lax.optimization_barrier(parts.reshape(CHUNKS * HALF_ROWS, LANES))
+    flat = lax.optimization_barrier(flat.astype(jnp.float16))
+    got = lax.all_to_all(flat.reshape(parts.shape), "cls", 0, 0, tiled=True)
     total = jnp.sum(got.astype(jnp.float32), axis=0).astype(jnp.float16)
     repeated = jnp.broadcast_to(total[None], (CHUNKS, QUADS, 4, LANES))
     whole = lax.all_to_all(repeated, "cls", 0, 0, tiled=True)
@@ -503,7 +523,7 @@
         ],
         compiler_params=pltpu.CompilerParams(vmem_limit_bytes=12 * MIB),
         name="finish",
-    )(whole.reshape(CHUNKS * HALF_ROWS, LANES).astype(jnp.float32).reshape(2, BLOCKS, QUADS, 4, LANES), classes, mine, theirs)
+    )(lax.optimization_barrier(lax.optimization_barrier(whole.reshape(CHUNKS * HALF_ROWS, LANES)).astype(jnp.float32)).reshape(2, BLOCKS, QUADS, 4, LANES), classes, mine, theirs)
     return new_classes, evidence.reshape(OWN)
 
 

time: 61.6 us -> 60.8 us (0.987)
  local copies, waits for them, and re-layouts: 1.77 us -> 0.92 us
  blocking collectives: 48.7 us -> 49.4 us
    unnamed x12 -> x10, local copies, waits for them, and re-layouts: 1.55 us -> 0.69 us
    pallas_call x1 -> x2, Pallas kernels: 0.71 us -> 1.28 us  [the longest x1 1.27 us: shards(): pl.pallas_call(own_kernel, out_shape=(jax.ShapeDtypeStruct((RESIDUES, 2 *...]
  transfers between devices with their start and end apart: 4 -> 4, of which waited for: 0 -> 0; matrix products, arithmetic and copies ran while one was open for 0% -> 0% of each run, Pallas kernels for 3% -> 4%
where the time goes in v7:
time: 60.8 us; the launch traced here: 60.6 us
  blocking collectives  49.4 us (81%)
  Pallas kernels  8.15 us (13%)
  local copies, waits for them, and re-layouts  0.92 us (2%)
  starting transfers between devices  0.8 us (1%)
  between operations  0.73 us (1%)
    all_to_all x1, blocking collectives, shards(): got = lax.all_to_all(flat.reshape(parts.shape), 'cls', 0, 0, tiled=True)  28.7 us
    all_to_all x1, blocking collectives, shards(): whole = lax.all_to_all(repeated, 'cls', 0, 0, tiled=True)  20.6 us
    pallas_call x1, Pallas kernels, shards(): pl.pallas_call(score_kernel, out_shape=(jax.ShapeDtypeStruct((36, ROWS, C...  2.73 us
    pallas_call x1, Pallas kernels, shards(): pl.pallas_call(sums_kernel, out_shape=jax.ShapeDtypeStruct((CHUNKS, QUADS...  1.56 us
    pallas_call x1, Pallas kernels, shards(): pl.pallas_call(finish_kernel, out_shape=(jax.ShapeDtypeStruct((CLASSES, B...  1.38 us
    pallas_call x1, Pallas kernels, shards(): pl.pallas_call(own_kernel, out_shape=(jax.ShapeDtypeStruct((RESIDUES, 2 *...  1.27 us
  transfers between devices with their start and end apart: 4, of which 0 were waited for; matrix products, arithmetic and copies ran while one was open for 0% of the time, Pallas kernels for 4%

profile of v7, /device:TPU:0, one launch (start us, length us, event | category | flops | bytes accessed | tf_op | source)
XLA Modules:
  0.0 60.6 jit_solution(1409082369691588059)
XLA Ops:
  0.6 0.0 copy-start.1
  0.6 0.0 copy-start
  0.6 0.1 collective-permute-start
  0.7 0.5 collective-permute-start.1
  1.2 0.1 collective-permute-start.2
  1.3 0.4 copy-done.1
  1.8 0.3 copy-done
  2.0 1.3 %own.1 = (bf16[19,224,256]{2,1,0:T(8,128)(2,1)S(1)}, f32[104,128]{1,0:T(8,128)S(1)}, bf16[128,4864]{1,0:T(8,128)(2,1)S(1)}, f32[36,104,128]{2,1,0:T(8,128)S(1)}) custom-call(bf16[100,4096]{1,0:T(8,128)(2,1)S(1)} %copy-done, f32[19,128]{1,0:T(8,128)S(1)} %signs.1.sign_ref, bf16[96,4096]{1,0:T(8,128)(2,1)S(1)} %copy-done.1), custom_call_target="tpu_custom_call" | custom-call | flops 4000000000 | bytes 8388608 | tf_op jit(solution)/shard_map/own/pallas_call | solution.py:438
  3.3 0.0 collective-permute-done.1
  3.3 0.0 collective-permute-done.2
  3.3 0.0 collective-permute-done.other_ref
  3.3 0.0 copy-done.2
  3.4 2.7 %scores.1 = (f32[36,104,256]{2,1,0:T(8,128)S(1)}, bf16[128,4864]{1,0:T(8,128)(2,1)S(1)}, f32[16,256]{1,0:T(8,128)S(1)}, f32[104,256]{1,0:T(8,128)S(1)}) custom-call(s32[2,20]{1,0:T(2,128)S(1)} %copy-done.2, bf16[96,4096]{1,0:T(8,128)(2,1)S(1)} %collective-permute-done.other_ref, bf16[1,96]{1,0:T(2,128)(2,1)S(1)} %bitcast.11, bf16[1,96]{1,0:T(2,128)(2,1)S(1)} %bitcast.13, ...), custom_call_target="tpu_custom_call" | custom-call | flops 4000000000 | bytes 8388608 | tf_op jit(solution)/shard_map/scores/pallas_call | solution.py:453
  6.1 0.1 collective-permute-start.3
  6.2 1.2 %spectra.1.w_ref = f32[36,104,256]{2,1,0:T(8,128)S(1)} custom-call(f32[36,104,256]{2,1,0:T(8,128)S(1)} %get-tuple-element.15.e_ref, f32[104,256]{1,0:T(8,128)S(1)} %get-tuple-element.16.top_ref, f32[16,256]{1,0:T(8,128)S(1)} %get-tuple-element.17.stat_ref.mine), custom_call_target="tpu_custom_call" | custom-call | flops 4000000000 | bytes 8388608 | tf_op jit(solution)/shard_map/spectra/pallas_call | solution.py:484
  7.4 0.0 collective-permute-done.3.theirs
  7.4 1.6 %sums.1 = f32[64,13,4,128]{3,2,1,0:T(4,128)S(1)} custom-call(f32[36,104,256]{2,1,0:T(8,128)S(1)} %spectra.1.w_ref, bf16[128,4864]{1,0:T(8,128)(2,1)S(1)} %get-tuple-element.18.xp_own, bf16[128,4864]{1,0:T(8,128)(2,1)S(1)} %get-tuple-element.19.xp_other, f32[16,256]{1,0:T(8,128)S(1)} %get-tuple-element.17.stat_ref.mine, ...), custom_call_target="tpu_custom_call" | custom-call | tf_op jit(solution)/shard_map/sums/pallas_call | solution.py:494
  9.0 0.1 convert_element_type.16
  9.1 28.7 %all_to_all.10 = f16[64,13,4,128]{3,2,1,0:T(4,128)(2,1)S(1)} all-to-all(f16[64,13,4,128]{3,2,1,0:T(4,128)(2,1)S(1)} %bitcast.15), channel_id=1, replica_groups=mesh['dom'=2,'cls'=64] {'cls'}, dimensions={0} | all-to-all | bytes 1703936 | tf_op jit(solution)/shard_map/all_to_all | solution.py:506
  37.9 0.4 convert_reduce_fusion
  38.2 0.2 broadcast_in_dim.2
  38.5 20.6 %all_to_all.11 = f16[64,13,4,128]{3,2,1,0:T(4,128)(2,1)S(1)} all-to-all(f16[64,13,4,128]{3,2,1,0:T(4,128)(2,1)S(1)} %broadcast_in_dim.2), channel_id=1, replica_groups=mesh['dom'=2,'cls'=64] {'cls'}, dimensions={0} | all-to-all | bytes 1703936 | tf_op jit(solution)/shard_map/all_to_all | solution.py:509
  59.1 0.1 convert_element_type.19
  59.2 1.4 %finish.1 = (f32[100,4096]{1,0:T(8,128)}, f32[1,96]{1,0:T(1,128)}) custom-call(f32[2,32,13,4,128]{4,3,2,1,0:T(4,128)S(1)} %bitcast.9, bf16[100,4096]{1,0:T(8,128)(2,1)S(1)} %copy-done, f32[16,256]{1,0:T(8,128)S(1)} %get-tuple-element.17.stat_ref.mine, f32[16,256]{1,0:T(8,128)S(1)} %collective-permute-done.3.theirs), custom_call_target="tpu_custom_call" | custom-call | tf_op jit(solution)/shard_map/finish/pallas_call | solution.py:510
  (7 shorter events, 0.0 us)
Async XLA Ops:
  0.6 1.1 %copy-start.1 = (bf16[96,4096]{1,0:T(8,128)(2,1)S(1)}, bf16[96,4096]{1,0:T(8,128)(2,1)}, u32[]{:S(2)}) copy-start(bf16[96,4096]{1,0:T(8,128)(2,1)} %own_ref.1) | copy-start | bytes 2359300
  0.6 1.4 %copy-start = (bf16[100,4096]{1,0:T(8,128)(2,1)S(1)}, bf16[100,4096]{1,0:T(8,128)(2,1)}, u32[]{:S(2)}) copy-start(bf16[100,4096]{1,0:T(8,128)(2,1)} %cls_ref.3) | copy-start | bytes 2457604
  0.6 2.7 %collective-permute-start = (bf16[96,4096]{1,0:T(8,128)(2,1)}, bf16[96,4096]{1,0:T(8,128)(2,1)S(1)}, u32[]{:S(2)}, u32[]{:S(2)}) collective-permute-start(bf16[96,4096]{1,0:T(8,128)(2,1)} %own_ref.1), channel_id=1, source_target_pairs={{0,64},{64,0},{1,65},{65,1},{2,66},{66,2},{3,67},{67,3},{4,68},{68... | collective-permute-start | bytes 2359304 | tf_op jit(solution)/shard_map/ppermute | solution.py:425
  0.7 2.6 %collective-permute-start.1 = (bf16[96]{0:T(256)(128)(2,1)}, bf16[96]{0:T(256)(128)(2,1)S(1)}, u32[]{:S(2)}, u32[]{:S(2)}) collective-permute-start(bf16[96]{0:T(256)(128)(2,1)} %param.6), channel_id=1, source_target_pairs={{0,64},{64,0},{1,65},{65,1},{2,66},{66,2},{3,67},{67,3},{4,68},{68... | collective-permute-start | bytes 584 | tf_op jit(solution)/shard_map/ppermute | solution.py:426
  1.2 2.1 %collective-permute-start.2 = (s32[96]{0:T(128)}, s32[96]{0:T(128)S(1)}, u32[]{:S(2)}, u32[]{:S(2)}) collective-permute-start(s32[96]{0:T(128)} %param.7), channel_id=1, source_target_pairs={{0,64},{64,0},{1,65},{65,1},{2,66},{66,2},{3,67},{67,3},{4,68},{68... | collective-permute-start | bytes 1160 | tf_op jit(solution)/shard_map/ppermute | solution.py:427
  2.0 1.3 %copy-start.2 = (s32[2,20]{1,0:T(2,128)S(1)}, s32[2,20]{1,0:T(2,128)}, u32[]{:S(2)}) copy-start(s32[2,20]{1,0:T(2,128)} %blocks_ref.1) | copy-start | bytes 484
  2.0 1.3 %copy-start.3 = (bf16[96]{0:T(256)(128)(2,1)S(1)}, bf16[96]{0:T(256)(128)(2,1)}, u32[]{:S(2)}) copy-start(bf16[96]{0:T(256)(128)(2,1)} %param.6) | copy-start | bytes 580
  2.0 1.3 %copy-start.4 = (s32[96]{0:T(128)S(1)}, s32[96]{0:T(128)}, u32[]{:S(2)}) copy-start(s32[96]{0:T(128)} %param.7) | copy-start | bytes 1156
  6.1 1.3 %collective-permute-start.3 = (f32[16,256]{1,0:T(8,128)S(1)}, f32[16,256]{1,0:T(8,128)S(1)}, u32[]{:S(2)}, u32[]{:S(2)}) collective-permute-start(f32[16,256]{1,0:T(8,128)S(1)} %get-tuple-element.17.stat_ref.mine), channel_id=1, source_target_pairs={{0,64},{64,0},{1,65},{65,1},{2,66},{66,2},{3,67},{67,3},{4,68},{68... | collective-permute-start | bytes 49160 | tf_op jit(solution)/shard_map/ppermute | solution.py:482

commit v8 on v7

--- a/solution.py
+++ b/solution.py
@@ -504,8 +504,10 @@
     flat = lax.optimization_barrier(parts.reshape(CHUNKS * HALF_ROWS, LANES))
     flat = lax.optimization_barrier(flat.astype(jnp.float16))
     got = lax.all_to_all(flat.reshape(parts.shape), "cls", 0, 0, tiled=True)
-    total = jnp.sum(got.astype(jnp.float32), axis=0).astype(jnp.float16)
-    repeated = jnp.broadcast_to(total[None], (CHUNKS, QUADS, 4, LANES))
+    pairs = lax.optimization_barrier(got.reshape(CHUNKS // 2, 2 * HALF_ROWS, LANES)).astype(jnp.float32).sum(axis=0)
+    total = (pairs + jnp.roll(pairs, HALF_ROWS, axis=0)).astype(jnp.float16)
+    repeated = lax.optimization_barrier(jnp.broadcast_to(total[None], (CHUNKS // 2, 2 * HALF_ROWS, LANES)))
+    repeated = repeated.reshape(CHUNKS, QUADS, 4, LANES)
     whole = lax.all_to_all(repeated, "cls", 0, 0, tiled=True)
     new_classes, evidence = pl.pallas_call(
         finish_kernel,

time: 60.8 us -> 60.5 us (level)
  no operation moved by 1% of the time
where the time goes in v8:
time: 60.5 us; the launch traced here: 60.3 us
  blocking collectives  49.4 us (82%)
  Pallas kernels  8.15 us (13%)
  local copies, waits for them, and re-layouts  0.82 us (1%)
  starting transfers between devices  0.8 us (1%)
  between operations  0.75 us (1%)
    all_to_all x1, blocking collectives, shards(): got = lax.all_to_all(flat.reshape(parts.shape), 'cls', 0, 0, tiled=True)  28.7 us
    all_to_all x1, blocking collectives, shards(): whole = lax.all_to_all(repeated, 'cls', 0, 0, tiled=True)  20.6 us
    pallas_call x1, Pallas kernels, shards(): pl.pallas_call(score_kernel, out_shape=(jax.ShapeDtypeStruct((36, ROWS, C...  2.73 us
    pallas_call x1, Pallas kernels, shards(): pl.pallas_call(sums_kernel, out_shape=jax.ShapeDtypeStruct((CHUNKS, QUADS...  1.56 us
    pallas_call x1, Pallas kernels, shards(): pl.pallas_call(finish_kernel, out_shape=(jax.ShapeDtypeStruct((CLASSES, B...  1.38 us
    pallas_call x1, Pallas kernels, shards(): pl.pallas_call(own_kernel, out_shape=(jax.ShapeDtypeStruct((RESIDUES, 2 *...  1.27 us
  transfers between devices with their start and end apart: 4, of which 0 were waited for; matrix products, arithmetic and copies ran while one was open for 0% of the time, Pallas kernels for 4%

profile of v8, /device:TPU:0, one launch (start us, length us, event | category | flops | bytes accessed | tf_op | source)
XLA Modules:
  0.0 60.3 jit_solution(12218384668390992794)
XLA Ops:
  0.6 0.0 copy-start.1
  0.6 0.0 copy-start
  0.6 0.1 collective-permute-start
  0.7 0.5 collective-permute-start.1
  1.2 0.1 collective-permute-start.2
  1.3 0.4 copy-done.1
  1.8 0.3 copy-done
  2.0 1.3 %own.1 = (bf16[19,224,256]{2,1,0:T(8,128)(2,1)S(1)}, f32[104,128]{1,0:T(8,128)S(1)}, bf16[128,4864]{1,0:T(8,128)(2,1)S(1)}, f32[36,104,128]{2,1,0:T(8,128)S(1)}) custom-call(bf16[100,4096]{1,0:T(8,128)(2,1)S(1)} %copy-done, f32[19,128]{1,0:T(8,128)S(1)} %signs.1.sign_ref, bf16[96,4096]{1,0:T(8,128)(2,1)S(1)} %copy-done.1), custom_call_target="tpu_custom_call" | custom-call | flops 4000000000 | bytes 8388608 | tf_op jit(solution)/shard_map/own/pallas_call | solution.py:438
  3.3 0.0 collective-permute-done.1
  3.3 0.0 collective-permute-done.2
  3.3 0.0 collective-permute-done.other_ref
  3.3 0.0 copy-done.2
  3.4 2.7 %scores.1 = (f32[36,104,256]{2,1,0:T(8,128)S(1)}, bf16[128,4864]{1,0:T(8,128)(2,1)S(1)}, f32[16,256]{1,0:T(8,128)S(1)}, f32[104,256]{1,0:T(8,128)S(1)}) custom-call(s32[2,20]{1,0:T(2,128)S(1)} %copy-done.2, bf16[96,4096]{1,0:T(8,128)(2,1)S(1)} %collective-permute-done.other_ref, bf16[1,96]{1,0:T(2,128)(2,1)S(1)} %bitcast.13, bf16[1,96]{1,0:T(2,128)(2,1)S(1)} %bitcast.15, ...), custom_call_target="tpu_custom_call" | custom-call | flops 4000000000 | bytes 8388608 | tf_op jit(solution)/shard_map/scores/pallas_call | solution.py:453
  6.1 0.1 collective-permute-start.3
  6.2 1.2 %spectra.1.w_ref = f32[36,104,256]{2,1,0:T(8,128)S(1)} custom-call(f32[36,104,256]{2,1,0:T(8,128)S(1)} %get-tuple-element.15.e_ref, f32[104,256]{1,0:T(8,128)S(1)} %get-tuple-element.16.top_ref, f32[16,256]{1,0:T(8,128)S(1)} %get-tuple-element.17.stat_ref.mine), custom_call_target="tpu_custom_call" | custom-call | flops 4000000000 | bytes 8388608 | tf_op jit(solution)/shard_map/spectra/pallas_call | solution.py:484
  7.4 0.0 collective-permute-done.3.theirs
  7.4 1.6 %sums.1 = f32[64,13,4,128]{3,2,1,0:T(4,128)S(1)} custom-call(f32[36,104,256]{2,1,0:T(8,128)S(1)} %spectra.1.w_ref, bf16[128,4864]{1,0:T(8,128)(2,1)S(1)} %get-tuple-element.18.xp_own, bf16[128,4864]{1,0:T(8,128)(2,1)S(1)} %get-tuple-element.19.xp_other, f32[16,256]{1,0:T(8,128)S(1)} %get-tuple-element.17.stat_ref.mine, ...), custom_call_target="tpu_custom_call" | custom-call | tf_op jit(solution)/shard_map/sums/pallas_call | solution.py:494
  9.0 0.1 convert_element_type.16
  9.1 28.7 %all_to_all.10 = f16[64,13,4,128]{3,2,1,0:T(4,128)(2,1)S(1)} all-to-all(f16[64,13,4,128]{3,2,1,0:T(4,128)(2,1)S(1)} %bitcast.17), channel_id=1, replica_groups=mesh['dom'=2,'cls'=64] {'cls'}, dimensions={0} | all-to-all | bytes 1703936 | tf_op jit(solution)/shard_map/all_to_all | solution.py:506
  37.9 0.1 convert_reduce_fusion
  38.0 0.1 broadcast_in_dim.2
  38.1 20.6 %all_to_all.11 = f16[64,13,4,128]{3,2,1,0:T(4,128)(2,1)S(1)} all-to-all(f16[64,13,4,128]{3,2,1,0:T(4,128)(2,1)S(1)} %bitcast.20), channel_id=1, replica_groups=mesh['dom'=2,'cls'=64] {'cls'}, dimensions={0} | all-to-all | bytes 1703936 | tf_op jit(solution)/shard_map/all_to_all | solution.py:511
  58.8 0.1 convert_element_type.19
  58.9 1.4 %finish.1 = (f32[100,4096]{1,0:T(8,128)}, f32[1,96]{1,0:T(1,128)}) custom-call(f32[2,32,13,4,128]{4,3,2,1,0:T(4,128)S(1)} %bitcast.11, bf16[100,4096]{1,0:T(8,128)(2,1)S(1)} %copy-done, f32[16,256]{1,0:T(8,128)S(1)} %get-tuple-element.17.stat_ref.mine, f32[16,256]{1,0:T(8,128)S(1)} %collective-permute-done.3.theirs), custom_call_target="tpu_custom_call" | custom-call | tf_op jit(solution)/shard_map/finish/pallas_call | solution.py:512
  (8 shorter events, 0.0 us)
Async XLA Ops:
  0.6 1.1 %copy-start.1 = (bf16[96,4096]{1,0:T(8,128)(2,1)S(1)}, bf16[96,4096]{1,0:T(8,128)(2,1)}, u32[]{:S(2)}) copy-start(bf16[96,4096]{1,0:T(8,128)(2,1)} %own_ref.1) | copy-start | bytes 2359300
  0.6 1.4 %copy-start = (bf16[100,4096]{1,0:T(8,128)(2,1)S(1)}, bf16[100,4096]{1,0:T(8,128)(2,1)}, u32[]{:S(2)}) copy-start(bf16[100,4096]{1,0:T(8,128)(2,1)} %cls_ref.3) | copy-start | bytes 2457604
  0.6 2.7 %collective-permute-start = (bf16[96,4096]{1,0:T(8,128)(2,1)}, bf16[96,4096]{1,0:T(8,128)(2,1)S(1)}, u32[]{:S(2)}, u32[]{:S(2)}) collective-permute-start(bf16[96,4096]{1,0:T(8,128)(2,1)} %own_ref.1), channel_id=1, source_target_pairs={{0,64},{64,0},{1,65},{65,1},{2,66},{66,2},{3,67},{67,3},{4,68},{68... | collective-permute-start | bytes 2359304 | tf_op jit(solution)/shard_map/ppermute | solution.py:425
  0.7 2.6 %collective-permute-start.1 = (bf16[96]{0:T(256)(128)(2,1)}, bf16[96]{0:T(256)(128)(2,1)S(1)}, u32[]{:S(2)}, u32[]{:S(2)}) collective-permute-start(bf16[96]{0:T(256)(128)(2,1)} %param.6), channel_id=1, source_target_pairs={{0,64},{64,0},{1,65},{65,1},{2,66},{66,2},{3,67},{67,3},{4,68},{68... | collective-permute-start | bytes 584 | tf_op jit(solution)/shard_map/ppermute | solution.py:426
  1.2 2.1 %collective-permute-start.2 = (s32[96]{0:T(128)}, s32[96]{0:T(128)S(1)}, u32[]{:S(2)}, u32[]{:S(2)}) collective-permute-start(s32[96]{0:T(128)} %param.7), channel_id=1, source_target_pairs={{0,64},{64,0},{1,65},{65,1},{2,66},{66,2},{3,67},{67,3},{4,68},{68... | collective-permute-start | bytes 1160 | tf_op jit(solution)/shard_map/ppermute | solution.py:427
  2.0 1.3 %copy-start.2 = (s32[2,20]{1,0:T(2,128)S(1)}, s32[2,20]{1,0:T(2,128)}, u32[]{:S(2)}) copy-start(s32[2,20]{1,0:T(2,128)} %blocks_ref.1) | copy-start | bytes 484
  2.0 1.3 %copy-start.3 = (bf16[96]{0:T(256)(128)(2,1)S(1)}, bf16[96]{0:T(256)(128)(2,1)}, u32[]{:S(2)}) copy-start(bf16[96]{0:T(256)(128)(2,1)} %param.6) | copy-start | bytes 580
  2.0 1.3 %copy-start.4 = (s32[96]{0:T(128)S(1)}, s32[96]{0:T(128)}, u32[]{:S(2)}) copy-start(s32[96]{0:T(128)} %param.7) | copy-start | bytes 1156
  6.1 1.3 %collective-permute-start.3 = (f32[16,256]{1,0:T(8,128)S(1)}, f32[16,256]{1,0:T(8,128)S(1)}, u32[]{:S(2)}, u32[]{:S(2)}) collective-permute-start(f32[16,256]{1,0:T(8,128)S(1)} %get-tuple-element.17.stat_ref.mine), channel_id=1, source_target_pairs={{0,64},{64,0},{1,65},{65,1},{2,66},{66,2},{3,67},{67,3},{4,68},{68... | collective-permute-start | bytes 49160 | tf_op jit(solution)/shard_map/ppermute | solution.py:482
